TPU v7x, 32 devices: a whole 2x2x4 slice. The times are simulated.
32 devices in a mesh: chan: 8 (over z, y), win: 4 (over x, core).
Axes of the slice: x: 2, y: 2, z: 4, core: 2. Of those that a mesh axis runs over, the one named last changes fastest.
Arguments:
- strain: float32 [8, 64, 4096], P('win', 'chan'), may hold values from -6 to 6
- offset_limit: int32 [64], P('chan'), may hold values from 32 to 256
- alive: int32 [64], P('chan'), may hold values 0 or 1
Outputs:
- stacked: float32 [256, 64, 400], P('win', 'chan')
All inputs are finite; a program needn't handle non-finite values. No bound on the sum of `alive` on one device may be relied on, other than what follows from the above.
Results may differ from a plain program's by a relative error of at most 0.0003.
Values sent between devices are 32-bit elements; how exact they have to be, the bound alone decides.
No kernel may reach another device: no remote copies, remote signals or barrier semaphores. Data moves between devices by JAX's collectives and lax.ppermute only.
A program may use at most 64 MiB of HBM per device.

v0:
```python
import math

import jax
import jax.numpy as jnp
from jax import lax
from jax.sharding import PartitionSpec as P

NF = 256
MAXOFF = 256
MAXLAG = 200


EPS = 1e-06
WHITEN_BINS = 64
SAMPLE_BLOCK = 256


def shifted(value, axis, steps):
    count = lax.axis_size(axis)
    initial, last = (max(0, -steps), min(count, count - steps))
    return lax.ppermute(value, axis, [(source, source + steps) for source in range(initial, last)])


def forward_table(first, count, length, nbins):
    sample_ids = first + jnp.arange(count, dtype=jnp.int32)
    freq_ids = jnp.arange(1, nbins + 1, dtype=jnp.int32)
    phases = sample_ids[:, None] * freq_ids[None, :] % length
    angles = phases.astype(jnp.float32) * (2.0 * math.pi / length)
    return jnp.concatenate([jnp.cos(angles), -jnp.sin(angles)], axis=1)


def inverse_table(nbins, half_lags, length):
    freq_ids = jnp.arange(1, nbins + 1, dtype=jnp.int32)
    lag_ids = jnp.arange(-half_lags, half_lags, dtype=jnp.int32)
    phases = freq_ids[:, None] * lag_ids[None, :] % length
    angles = phases.astype(jnp.float32) * (2.0 * math.pi / length)
    return jnp.concatenate([jnp.cos(angles), -jnp.sin(angles)], axis=0)


def whiten(spectrum):
    nbins = spectrum.shape[-1] // 2
    real_part = spectrum[..., :nbins]
    imag_part = spectrum[..., nbins:]
    magnitude = jnp.sqrt(real_part * real_part + imag_part * imag_part)
    blocked = magnitude.reshape(magnitude.shape[:-1] + (nbins // WHITEN_BINS, WHITEN_BINS))
    levels = jnp.mean(blocked, axis=-1, keepdims=True) + EPS
    levels = jnp.broadcast_to(levels, blocked.shape).reshape(magnitude.shape)
    return spectrum / jnp.concatenate([levels, levels], axis=-1)


def cross_pair(own_rows, partner):
    nbins = own_rows.shape[-1] // 2
    own_re = own_rows[..., None, :nbins]
    own_im = own_rows[..., None, nbins:]
    part_re = partner[..., :nbins]
    part_im = partner[..., nbins:]
    real_sum = jnp.sum(own_re * part_re + own_im * part_im, axis=0)
    imag_sum = jnp.sum(own_im * part_re - own_re * part_im, axis=0)
    return jnp.concatenate([real_sum, imag_sum], axis=-1)


def local(strain, offset_limit, alive):
    win_dev, ch_dev, samples = strain.shape
    win_count = lax.axis_size("win")
    windows = win_dev * win_count
    flat_rows = strain.reshape(win_dev * ch_dev, samples)
    sample_block = min(SAMPLE_BLOCK, samples)

    def add_block(block_id, total):
        first = block_id * sample_block
        piece = lax.dynamic_slice_in_dim(flat_rows, first, sample_block, 1)
        return total + jnp.dot(
            piece,
            forward_table(first, sample_block, samples, NF),
            precision=lax.Precision.HIGHEST,
            preferred_element_type=jnp.float32,
        )

    spectrum = lax.fori_loop(
        0, samples // sample_block, add_block, jnp.zeros((win_dev * ch_dev, 2 * NF), jnp.float32)
    )
    white = whiten(spectrum.reshape(win_dev, ch_dev, 2 * NF))
    white = white * alive.astype(jnp.float32)[None, :, None]
    inverse = inverse_table(NF, MAXLAG, samples)
    scale = 1.0 / math.sqrt(NF * windows)
    share_rows = MAXOFF // win_count
    reach = MAXOFF // ch_dev

    def next_turn(turn, carry):
        block, stored = carry
        block = shifted(block, "chan", -1)
        stored = lax.dynamic_update_slice_in_dim(stored, block[:, None], turn, 1)
        return (block, stored)

    stored = jnp.zeros((win_dev, reach, ch_dev, 2 * NF), jnp.float32)
    last_block, stored = lax.fori_loop(0, reach, next_turn, (white, stored))
    extended = jnp.concatenate([white, stored.reshape(win_dev, reach * ch_dev, 2 * NF)], axis=1)
    offset_ids = jnp.arange(1, MAXOFF + 1, dtype=jnp.int32)
    columns = []
    for channel in range(ch_dev):
        partner = extended[:, channel + 1 : channel + 1 + MAXOFF]
        columns.append(cross_pair(white[:, channel], partner))
    cross = jnp.stack(columns, axis=1)
    keep = (offset_ids[:, None] <= offset_limit[None, :]).astype(jnp.float32)
    cross = cross * keep[:, :, None]
    lagged = jnp.dot(
        cross.reshape(share_rows * lax.axis_size("win") * ch_dev, 2 * NF),
        inverse,
        precision=lax.Precision.HIGHEST,
        preferred_element_type=jnp.float32,
    )
    return lax.psum_scatter(
        (lagged * scale).reshape(share_rows * lax.axis_size("win"), ch_dev, 2 * MAXLAG),
        "win",
        scatter_dimension=0,
        tiled=True,
    )


def solution(mesh):
    in_specs = (P("win", "chan", None), P("chan"), P("chan"))
    out_specs = P("win", "chan", None)
    return jax.shard_map(local, mesh=mesh, in_specs=in_specs, out_specs=out_specs, check_vma=False)
```

profile of v0, /device:TPU:0, one launch (start us, length us, event | category | flops | bytes accessed | tf_op | source)
XLA Modules:
  0.0 346.2 jit_solution(9730015154332883698)
XLA Ops:
  6.5 35.5 %while.32 = (s32[]{:T(128)}, f32[16,512]{1,0:T(8,128)S(1)}, f32[16,4096]{1,0:T(8,128)}, s32[]{:T(128)}, s32[]{:T(128)}, /*index=5*/s32[]{:T(128)}, s32[]{:T(128)}) while((s32[]{:T(128)}, f32[16,512]{1,0:T(8,128)S(1)}, f32[16,4096]{1,0:T(8,128)}, s32[]{:T(128)}, s32[]{:T(128)}, /*index=5*/s32[]{:T(128)}, s32[]{:T(128)}) %tuple.117), condition=%wide.region_1.2_spmd.clone, body=%wide.region_0.1_spmd.clone.sunk | while | flops 26296840 | bytes 1134733 | solution.py:79
  42.6 216.8 %while.31 = (s32[]{:T(128)}, f32[2,8,512]{2,1,0:T(8,128)S(1)}, f32[2,32,8,512]{3,2,1,0:T(8,128)S(1)}, s32[]{:T(128)}) while((s32[]{:T(128)}, f32[2,8,512]{2,1,0:T(8,128)S(1)}, f32[2,32,8,512]{3,2,1,0:T(8,128)S(1)}, s32[]{:T(128)}) %tuple.112), condition=%wide.region_4.5_spmd, body=%wide.region_3.4_spmd.sunk | while | flops 2 | bytes 262249 | solution.py:96
  43.9 5.5 %collective-permute-done = f32[2,8,512]{2,1,0:T(8,128)S(1)} collective-permute-done((f32[2,8,512]{2,1,0:T(8,128)S(1)}, f32[2,8,512]{2,1,0:T(8,128)S(1)}, u32[]{:S(2)}, u32[]{:S(2)}) %collective-permute-start) | collective-permute-done | bytes 32800 | tf_op jit(solution)/shard_map/while/body/eval_jaxpr/ppermute | solution.py:21
  50.7 5.4 %collective-permute-done = f32[2,8,512]{2,1,0:T(8,128)S(1)} collective-permute-done((f32[2,8,512]{2,1,0:T(8,128)S(1)}, f32[2,8,512]{2,1,0:T(8,128)S(1)}, u32[]{:S(2)}, u32[]{:S(2)}) %collective-permute-start) | collective-permute-done | bytes 32800 | tf_op jit(solution)/shard_map/while/body/eval_jaxpr/ppermute | solution.py:21
  57.5 5.4 %collective-permute-done = f32[2,8,512]{2,1,0:T(8,128)S(1)} collective-permute-done((f32[2,8,512]{2,1,0:T(8,128)S(1)}, f32[2,8,512]{2,1,0:T(8,128)S(1)}, u32[]{:S(2)}, u32[]{:S(2)}) %collective-permute-start) | collective-permute-done | bytes 32800 | tf_op jit(solution)/shard_map/while/body/eval_jaxpr/ppermute | solution.py:21
  64.2 5.4 %collective-permute-done = f32[2,8,512]{2,1,0:T(8,128)S(1)} collective-permute-done((f32[2,8,512]{2,1,0:T(8,128)S(1)}, f32[2,8,512]{2,1,0:T(8,128)S(1)}, u32[]{:S(2)}, u32[]{:S(2)}) %collective-permute-start) | collective-permute-done | bytes 32800 | tf_op jit(solution)/shard_map/while/body/eval_jaxpr/ppermute | solution.py:21
  70.9 5.6 %collective-permute-done = f32[2,8,512]{2,1,0:T(8,128)S(1)} collective-permute-done((f32[2,8,512]{2,1,0:T(8,128)S(1)}, f32[2,8,512]{2,1,0:T(8,128)S(1)}, u32[]{:S(2)}, u32[]{:S(2)}) %collective-permute-start) | collective-permute-done | bytes 32800 | tf_op jit(solution)/shard_map/while/body/eval_jaxpr/ppermute | solution.py:21
  84.6 5.4 %collective-permute-done = f32[2,8,512]{2,1,0:T(8,128)S(1)} collective-permute-done((f32[2,8,512]{2,1,0:T(8,128)S(1)}, f32[2,8,512]{2,1,0:T(8,128)S(1)}, u32[]{:S(2)}, u32[]{:S(2)}) %collective-permute-start) | collective-permute-done | bytes 32800 | tf_op jit(solution)/shard_map/while/body/eval_jaxpr/ppermute | solution.py:21
  91.3 5.4 %collective-permute-done = f32[2,8,512]{2,1,0:T(8,128)S(1)} collective-permute-done((f32[2,8,512]{2,1,0:T(8,128)S(1)}, f32[2,8,512]{2,1,0:T(8,128)S(1)}, u32[]{:S(2)}, u32[]{:S(2)}) %collective-permute-start) | collective-permute-done | bytes 32800 | tf_op jit(solution)/shard_map/while/body/eval_jaxpr/ppermute | solution.py:21
  98.1 5.4 %collective-permute-done = f32[2,8,512]{2,1,0:T(8,128)S(1)} collective-permute-done((f32[2,8,512]{2,1,0:T(8,128)S(1)}, f32[2,8,512]{2,1,0:T(8,128)S(1)}, u32[]{:S(2)}, u32[]{:S(2)}) %collective-permute-start) | collective-permute-done | bytes 32800 | tf_op jit(solution)/shard_map/while/body/eval_jaxpr/ppermute | solution.py:21
  104.8 5.5 %collective-permute-done = f32[2,8,512]{2,1,0:T(8,128)S(1)} collective-permute-done((f32[2,8,512]{2,1,0:T(8,128)S(1)}, f32[2,8,512]{2,1,0:T(8,128)S(1)}, u32[]{:S(2)}, u32[]{:S(2)}) %collective-permute-start) | collective-permute-done | bytes 32800 | tf_op jit(solution)/shard_map/while/body/eval_jaxpr/ppermute | solution.py:21
  111.6 5.7 %collective-permute-done = f32[2,8,512]{2,1,0:T(8,128)S(1)} collective-permute-done((f32[2,8,512]{2,1,0:T(8,128)S(1)}, f32[2,8,512]{2,1,0:T(8,128)S(1)}, u32[]{:S(2)}, u32[]{:S(2)}) %collective-permute-start) | collective-permute-done | bytes 32800 | tf_op jit(solution)/shard_map/while/body/eval_jaxpr/ppermute | solution.py:21
  118.6 5.4 %collective-permute-done = f32[2,8,512]{2,1,0:T(8,128)S(1)} collective-permute-done((f32[2,8,512]{2,1,0:T(8,128)S(1)}, f32[2,8,512]{2,1,0:T(8,128)S(1)}, u32[]{:S(2)}, u32[]{:S(2)}) %collective-permute-start) | collective-permute-done | bytes 32800 | tf_op jit(solution)/shard_map/while/body/eval_jaxpr/ppermute | solution.py:21
  125.4 5.4 %collective-permute-done = f32[2,8,512]{2,1,0:T(8,128)S(1)} collective-permute-done((f32[2,8,512]{2,1,0:T(8,128)S(1)}, f32[2,8,512]{2,1,0:T(8,128)S(1)}, u32[]{:S(2)}, u32[]{:S(2)}) %collective-permute-start) | collective-permute-done | bytes 32800 | tf_op jit(solution)/shard_map/while/body/eval_jaxpr/ppermute | solution.py:21
  132.1 5.4 %collective-permute-done = f32[2,8,512]{2,1,0:T(8,128)S(1)} collective-permute-done((f32[2,8,512]{2,1,0:T(8,128)S(1)}, f32[2,8,512]{2,1,0:T(8,128)S(1)}, u32[]{:S(2)}, u32[]{:S(2)}) %collective-permute-start) | collective-permute-done | bytes 32800 | tf_op jit(solution)/shard_map/while/body/eval_jaxpr/ppermute | solution.py:21
  138.8 5.4 %collective-permute-done = f32[2,8,512]{2,1,0:T(8,128)S(1)} collective-permute-done((f32[2,8,512]{2,1,0:T(8,128)S(1)}, f32[2,8,512]{2,1,0:T(8,128)S(1)}, u32[]{:S(2)}, u32[]{:S(2)}) %collective-permute-start) | collective-permute-done | bytes 32800 | tf_op jit(solution)/shard_map/while/body/eval_jaxpr/ppermute | solution.py:21
  145.6 5.6 %collective-permute-done = f32[2,8,512]{2,1,0:T(8,128)S(1)} collective-permute-done((f32[2,8,512]{2,1,0:T(8,128)S(1)}, f32[2,8,512]{2,1,0:T(8,128)S(1)}, u32[]{:S(2)}, u32[]{:S(2)}) %collective-permute-start) | collective-permute-done | bytes 32800 | tf_op jit(solution)/shard_map/while/body/eval_jaxpr/ppermute | solution.py:21
  152.5 5.4 %collective-permute-done = f32[2,8,512]{2,1,0:T(8,128)S(1)} collective-permute-done((f32[2,8,512]{2,1,0:T(8,128)S(1)}, f32[2,8,512]{2,1,0:T(8,128)S(1)}, u32[]{:S(2)}, u32[]{:S(2)}) %collective-permute-start) | collective-permute-done | bytes 32800 | tf_op jit(solution)/shard_map/while/body/eval_jaxpr/ppermute | solution.py:21
  159.3 5.4 %collective-permute-done = f32[2,8,512]{2,1,0:T(8,128)S(1)} collective-permute-done((f32[2,8,512]{2,1,0:T(8,128)S(1)}, f32[2,8,512]{2,1,0:T(8,128)S(1)}, u32[]{:S(2)}, u32[]{:S(2)}) %collective-permute-start) | collective-permute-done | bytes 32800 | tf_op jit(solution)/shard_map/while/body/eval_jaxpr/ppermute | solution.py:21
  166.0 5.4 %collective-permute-done = f32[2,8,512]{2,1,0:T(8,128)S(1)} collective-permute-done((f32[2,8,512]{2,1,0:T(8,128)S(1)}, f32[2,8,512]{2,1,0:T(8,128)S(1)}, u32[]{:S(2)}, u32[]{:S(2)}) %collective-permute-start) | collective-permute-done | bytes 32800 | tf_op jit(solution)/shard_map/while/body/eval_jaxpr/ppermute | solution.py:21
  172.7 5.4 %collective-permute-done = f32[2,8,512]{2,1,0:T(8,128)S(1)} collective-permute-done((f32[2,8,512]{2,1,0:T(8,128)S(1)}, f32[2,8,512]{2,1,0:T(8,128)S(1)}, u32[]{:S(2)}, u32[]{:S(2)}) %collective-permute-start) | collective-permute-done | bytes 32800 | tf_op jit(solution)/shard_map/while/body/eval_jaxpr/ppermute | solution.py:21
  179.5 5.6 %collective-permute-done = f32[2,8,512]{2,1,0:T(8,128)S(1)} collective-permute-done((f32[2,8,512]{2,1,0:T(8,128)S(1)}, f32[2,8,512]{2,1,0:T(8,128)S(1)}, u32[]{:S(2)}, u32[]{:S(2)}) %collective-permute-start) | collective-permute-done | bytes 32800 | tf_op jit(solution)/shard_map/while/body/eval_jaxpr/ppermute | solution.py:21
  186.4 5.4 %collective-permute-done = f32[2,8,512]{2,1,0:T(8,128)S(1)} collective-permute-done((f32[2,8,512]{2,1,0:T(8,128)S(1)}, f32[2,8,512]{2,1,0:T(8,128)S(1)}, u32[]{:S(2)}, u32[]{:S(2)}) %collective-permute-start) | collective-permute-done | bytes 32800 | tf_op jit(solution)/shard_map/while/body/eval_jaxpr/ppermute | solution.py:21
  193.1 5.4 %collective-permute-done = f32[2,8,512]{2,1,0:T(8,128)S(1)} collective-permute-done((f32[2,8,512]{2,1,0:T(8,128)S(1)}, f32[2,8,512]{2,1,0:T(8,128)S(1)}, u32[]{:S(2)}, u32[]{:S(2)}) %collective-permute-start) | collective-permute-done | bytes 32800 | tf_op jit(solution)/shard_map/while/body/eval_jaxpr/ppermute | solution.py:21
  199.9 5.4 %collective-permute-done = f32[2,8,512]{2,1,0:T(8,128)S(1)} collective-permute-done((f32[2,8,512]{2,1,0:T(8,128)S(1)}, f32[2,8,512]{2,1,0:T(8,128)S(1)}, u32[]{:S(2)}, u32[]{:S(2)}) %collective-permute-start) | collective-permute-done | bytes 32800 | tf_op jit(solution)/shard_map/while/body/eval_jaxpr/ppermute | solution.py:21
  206.6 5.4 %collective-permute-done = f32[2,8,512]{2,1,0:T(8,128)S(1)} collective-permute-done((f32[2,8,512]{2,1,0:T(8,128)S(1)}, f32[2,8,512]{2,1,0:T(8,128)S(1)}, u32[]{:S(2)}, u32[]{:S(2)}) %collective-permute-start) | collective-permute-done | bytes 32800 | tf_op jit(solution)/shard_map/while/body/eval_jaxpr/ppermute | solution.py:21
  213.4 5.6 %collective-permute-done = f32[2,8,512]{2,1,0:T(8,128)S(1)} collective-permute-done((f32[2,8,512]{2,1,0:T(8,128)S(1)}, f32[2,8,512]{2,1,0:T(8,128)S(1)}, u32[]{:S(2)}, u32[]{:S(2)}) %collective-permute-start) | collective-permute-done | bytes 32800 | tf_op jit(solution)/shard_map/while/body/eval_jaxpr/ppermute | solution.py:21
  220.3 5.4 %collective-permute-done = f32[2,8,512]{2,1,0:T(8,128)S(1)} collective-permute-done((f32[2,8,512]{2,1,0:T(8,128)S(1)}, f32[2,8,512]{2,1,0:T(8,128)S(1)}, u32[]{:S(2)}, u32[]{:S(2)}) %collective-permute-start) | collective-permute-done | bytes 32800 | tf_op jit(solution)/shard_map/while/body/eval_jaxpr/ppermute | solution.py:21
  254.0 5.4 %collective-permute-done = f32[2,8,512]{2,1,0:T(8,128)S(1)} collective-permute-done((f32[2,8,512]{2,1,0:T(8,128)S(1)}, f32[2,8,512]{2,1,0:T(8,128)S(1)}, u32[]{:S(2)}, u32[]{:S(2)}) %collective-permute-start) | collective-permute-done | bytes 32800 | tf_op jit(solution)/shard_map/while/body/eval_jaxpr/ppermute | solution.py:21
  270.7 11.1 %stack.37 = f32[256,8,512]{2,1,0:T(8,128)} concatenate(f32[256,1,512]{2,1,0:T(1,128)} %stack.29, f32[256,1,512]{2,1,0:T(1,128)} %stack.30, f32[256,1,512]{2,1,0:T(1,128)S(1)} %copy-done, f32[256,1,512]{2,1,0:T(1,128)S(1)} %stack.32, f32[256,1,512]{2,1,0:T(1,128)S(1)} %stack.33, f32[256,1,512]{2,1,0:T(1,128)S(1)} %stack.34, f32[256,1,512]{2,1,0:T(1,128)S(1)} %stack.35, ...), dimensions={1} | concatenate | bytes 8388608 | tf_op jit(solution)/shard_map/stack | solution.py:103
  281.8 8.0 %fusion.11 = f32[2048,400]{0,1:T(8,128)S(1)} fusion(f32[256,8,512]{2,1,0:T(8,128)} %stack.37, f32[2048]{0:T(1024)S(1)} %compare_convert_fusion, f32[256,400]{1,0:T(8,128)} %get-tuple-element.241, f32[256,400]{1,0:T(8,128)} %get-tuple-element.240), kind=kOutput, calls=%fused_computation.35 | convolution fusion | flops 5035237376 | bytes 8298496 | tf_op jit(solution)/shard_map/dot_general | solution.py:106
  293.1 46.3 %reduce-scatter.2.cloned.1.call-done = f32[64,8,400]{2,1,0:T(8,128)} async-done(((f32[256,8,400]{2,1,0:T(8,128)}), f32[64,8,400]{2,1,0:T(8,128)}) %reduce-scatter.2.cloned.1.call-update) | async-done | bytes 819216 | tf_op jit(solution)/shard_map/reduce_scatter | solution.py:112
  (209 shorter events, 118.8 us)
Async XLA Ops:
  6.5 332.8 %reduce-scatter.2.cloned.1.call-start = ((), (), s32[]{:S(2)}) async-start(), calls=%async_computation.1 | async-start | bytes 5242880 | tf_op jit(solution)/shard_map/reduce_scatter | solution.py:112
  42.6 6.8 %collective-permute-start = (f32[2,8,512]{2,1,0:T(8,128)S(1)}, f32[2,8,512]{2,1,0:T(8,128)S(1)}, u32[]{:S(2)}, u32[]{:S(2)}) collective-permute-start(f32[2,8,512]{2,1,0:T(8,128)S(1)} %get-tuple-element.322), channel_id=1, source_target_pairs={{4,0},{8,4},{12,8},{16,12},{20,16},{24,20},{28,24},{5,1},{9,5},{13... | collective-permute-start | bytes 98312 | tf_op jit(solution)/shard_map/while/body/eval_jaxpr/ppermute | solution.py:21
  49.4 6.7 %collective-permute-start = (f32[2,8,512]{2,1,0:T(8,128)S(1)}, f32[2,8,512]{2,1,0:T(8,128)S(1)}, u32[]{:S(2)}, u32[]{:S(2)}) collective-permute-start(f32[2,8,512]{2,1,0:T(8,128)S(1)} %get-tuple-element.322), channel_id=1, source_target_pairs={{4,0},{8,4},{12,8},{16,12},{20,16},{24,20},{28,24},{5,1},{9,5},{13... | collective-permute-start | bytes 98312 | tf_op jit(solution)/shard_map/while/body/eval_jaxpr/ppermute | solution.py:21
  56.2 6.7 %collective-permute-start = (f32[2,8,512]{2,1,0:T(8,128)S(1)}, f32[2,8,512]{2,1,0:T(8,128)S(1)}, u32[]{:S(2)}, u32[]{:S(2)}) collective-permute-start(f32[2,8,512]{2,1,0:T(8,128)S(1)} %get-tuple-element.322), channel_id=1, source_target_pairs={{4,0},{8,4},{12,8},{16,12},{20,16},{24,20},{28,24},{5,1},{9,5},{13... | collective-permute-start | bytes 98312 | tf_op jit(solution)/shard_map/while/body/eval_jaxpr/ppermute | solution.py:21
  62.9 6.7 %collective-permute-start = (f32[2,8,512]{2,1,0:T(8,128)S(1)}, f32[2,8,512]{2,1,0:T(8,128)S(1)}, u32[]{:S(2)}, u32[]{:S(2)}) collective-permute-start(f32[2,8,512]{2,1,0:T(8,128)S(1)} %get-tuple-element.322), channel_id=1, source_target_pairs={{4,0},{8,4},{12,8},{16,12},{20,16},{24,20},{28,24},{5,1},{9,5},{13... | collective-permute-start | bytes 98312 | tf_op jit(solution)/shard_map/while/body/eval_jaxpr/ppermute | solution.py:21
  69.6 6.9 %collective-permute-start = (f32[2,8,512]{2,1,0:T(8,128)S(1)}, f32[2,8,512]{2,1,0:T(8,128)S(1)}, u32[]{:S(2)}, u32[]{:S(2)}) collective-permute-start(f32[2,8,512]{2,1,0:T(8,128)S(1)} %get-tuple-element.322), channel_id=1, source_target_pairs={{4,0},{8,4},{12,8},{16,12},{20,16},{24,20},{28,24},{5,1},{9,5},{13... | collective-permute-start | bytes 98312 | tf_op jit(solution)/shard_map/while/body/eval_jaxpr/ppermute | solution.py:21
  83.3 6.7 %collective-permute-start = (f32[2,8,512]{2,1,0:T(8,128)S(1)}, f32[2,8,512]{2,1,0:T(8,128)S(1)}, u32[]{:S(2)}, u32[]{:S(2)}) collective-permute-start(f32[2,8,512]{2,1,0:T(8,128)S(1)} %get-tuple-element.322), channel_id=1, source_target_pairs={{4,0},{8,4},{12,8},{16,12},{20,16},{24,20},{28,24},{5,1},{9,5},{13... | collective-permute-start | bytes 98312 | tf_op jit(solution)/shard_map/while/body/eval_jaxpr/ppermute | solution.py:21
  90.0 6.7 %collective-permute-start = (f32[2,8,512]{2,1,0:T(8,128)S(1)}, f32[2,8,512]{2,1,0:T(8,128)S(1)}, u32[]{:S(2)}, u32[]{:S(2)}) collective-permute-start(f32[2,8,512]{2,1,0:T(8,128)S(1)} %get-tuple-element.322), channel_id=1, source_target_pairs={{4,0},{8,4},{12,8},{16,12},{20,16},{24,20},{28,24},{5,1},{9,5},{13... | collective-permute-start | bytes 98312 | tf_op jit(solution)/shard_map/while/body/eval_jaxpr/ppermute | solution.py:21
  96.8 6.7 %collective-permute-start = (f32[2,8,512]{2,1,0:T(8,128)S(1)}, f32[2,8,512]{2,1,0:T(8,128)S(1)}, u32[]{:S(2)}, u32[]{:S(2)}) collective-permute-start(f32[2,8,512]{2,1,0:T(8,128)S(1)} %get-tuple-element.322), channel_id=1, source_target_pairs={{4,0},{8,4},{12,8},{16,12},{20,16},{24,20},{28,24},{5,1},{9,5},{13... | collective-permute-start | bytes 98312 | tf_op jit(solution)/shard_map/while/body/eval_jaxpr/ppermute | solution.py:21
  103.5 6.8 %collective-permute-start = (f32[2,8,512]{2,1,0:T(8,128)S(1)}, f32[2,8,512]{2,1,0:T(8,128)S(1)}, u32[]{:S(2)}, u32[]{:S(2)}) collective-permute-start(f32[2,8,512]{2,1,0:T(8,128)S(1)} %get-tuple-element.322), channel_id=1, source_target_pairs={{4,0},{8,4},{12,8},{16,12},{20,16},{24,20},{28,24},{5,1},{9,5},{13... | collective-permute-start | bytes 98312 | tf_op jit(solution)/shard_map/while/body/eval_jaxpr/ppermute | solution.py:21
  110.3 7.0 %collective-permute-start = (f32[2,8,512]{2,1,0:T(8,128)S(1)}, f32[2,8,512]{2,1,0:T(8,128)S(1)}, u32[]{:S(2)}, u32[]{:S(2)}) collective-permute-start(f32[2,8,512]{2,1,0:T(8,128)S(1)} %get-tuple-element.322), channel_id=1, source_target_pairs={{4,0},{8,4},{12,8},{16,12},{20,16},{24,20},{28,24},{5,1},{9,5},{13... | collective-permute-start | bytes 98312 | tf_op jit(solution)/shard_map/while/body/eval_jaxpr/ppermute | solution.py:21
  117.3 6.7 %collective-permute-start = (f32[2,8,512]{2,1,0:T(8,128)S(1)}, f32[2,8,512]{2,1,0:T(8,128)S(1)}, u32[]{:S(2)}, u32[]{:S(2)}) collective-permute-start(f32[2,8,512]{2,1,0:T(8,128)S(1)} %get-tuple-element.322), channel_id=1, source_target_pairs={{4,0},{8,4},{12,8},{16,12},{20,16},{24,20},{28,24},{5,1},{9,5},{13... | collective-permute-start | bytes 98312 | tf_op jit(solution)/shard_map/while/body/eval_jaxpr/ppermute | solution.py:21
  124.1 6.7 %collective-permute-start = (f32[2,8,512]{2,1,0:T(8,128)S(1)}, f32[2,8,512]{2,1,0:T(8,128)S(1)}, u32[]{:S(2)}, u32[]{:S(2)}) collective-permute-start(f32[2,8,512]{2,1,0:T(8,128)S(1)} %get-tuple-element.322), channel_id=1, source_target_pairs={{4,0},{8,4},{12,8},{16,12},{20,16},{24,20},{28,24},{5,1},{9,5},{13... | collective-permute-start | bytes 98312 | tf_op jit(solution)/shard_map/while/body/eval_jaxpr/ppermute | solution.py:21
  130.8 6.7 %collective-permute-start = (f32[2,8,512]{2,1,0:T(8,128)S(1)}, f32[2,8,512]{2,1,0:T(8,128)S(1)}, u32[]{:S(2)}, u32[]{:S(2)}) collective-permute-start(f32[2,8,512]{2,1,0:T(8,128)S(1)} %get-tuple-element.322), channel_id=1, source_target_pairs={{4,0},{8,4},{12,8},{16,12},{20,16},{24,20},{28,24},{5,1},{9,5},{13... | collective-permute-start | bytes 98312 | tf_op jit(solution)/shard_map/while/body/eval_jaxpr/ppermute | solution.py:21
  137.5 6.7 %collective-permute-start = (f32[2,8,512]{2,1,0:T(8,128)S(1)}, f32[2,8,512]{2,1,0:T(8,128)S(1)}, u32[]{:S(2)}, u32[]{:S(2)}) collective-permute-start(f32[2,8,512]{2,1,0:T(8,128)S(1)} %get-tuple-element.322), channel_id=1, source_target_pairs={{4,0},{8,4},{12,8},{16,12},{20,16},{24,20},{28,24},{5,1},{9,5},{13... | collective-permute-start | bytes 98312 | tf_op jit(solution)/shard_map/while/body/eval_jaxpr/ppermute | solution.py:21
  144.3 6.9 %collective-permute-start = (f32[2,8,512]{2,1,0:T(8,128)S(1)}, f32[2,8,512]{2,1,0:T(8,128)S(1)}, u32[]{:S(2)}, u32[]{:S(2)}) collective-permute-start(f32[2,8,512]{2,1,0:T(8,128)S(1)} %get-tuple-element.322), channel_id=1, source_target_pairs={{4,0},{8,4},{12,8},{16,12},{20,16},{24,20},{28,24},{5,1},{9,5},{13... | collective-permute-start | bytes 98312 | tf_op jit(solution)/shard_map/while/body/eval_jaxpr/ppermute | solution.py:21
  151.2 6.7 %collective-permute-start = (f32[2,8,512]{2,1,0:T(8,128)S(1)}, f32[2,8,512]{2,1,0:T(8,128)S(1)}, u32[]{:S(2)}, u32[]{:S(2)}) collective-permute-start(f32[2,8,512]{2,1,0:T(8,128)S(1)} %get-tuple-element.322), channel_id=1, source_target_pairs={{4,0},{8,4},{12,8},{16,12},{20,16},{24,20},{28,24},{5,1},{9,5},{13... | collective-permute-start | bytes 98312 | tf_op jit(solution)/shard_map/while/body/eval_jaxpr/ppermute | solution.py:21
  158.0 6.7 %collective-permute-start = (f32[2,8,512]{2,1,0:T(8,128)S(1)}, f32[2,8,512]{2,1,0:T(8,128)S(1)}, u32[]{:S(2)}, u32[]{:S(2)}) collective-permute-start(f32[2,8,512]{2,1,0:T(8,128)S(1)} %get-tuple-element.322), channel_id=1, source_target_pairs={{4,0},{8,4},{12,8},{16,12},{20,16},{24,20},{28,24},{5,1},{9,5},{13... | collective-permute-start | bytes 98312 | tf_op jit(solution)/shard_map/while/body/eval_jaxpr/ppermute | solution.py:21
  164.7 6.7 %collective-permute-start = (f32[2,8,512]{2,1,0:T(8,128)S(1)}, f32[2,8,512]{2,1,0:T(8,128)S(1)}, u32[]{:S(2)}, u32[]{:S(2)}) collective-permute-start(f32[2,8,512]{2,1,0:T(8,128)S(1)} %get-tuple-element.322), channel_id=1, source_target_pairs={{4,0},{8,4},{12,8},{16,12},{20,16},{24,20},{28,24},{5,1},{9,5},{13... | collective-permute-start | bytes 98312 | tf_op jit(solution)/shard_map/while/body/eval_jaxpr/ppermute | solution.py:21
  171.4 6.7 %collective-permute-start = (f32[2,8,512]{2,1,0:T(8,128)S(1)}, f32[2,8,512]{2,1,0:T(8,128)S(1)}, u32[]{:S(2)}, u32[]{:S(2)}) collective-permute-start(f32[2,8,512]{2,1,0:T(8,128)S(1)} %get-tuple-element.322), channel_id=1, source_target_pairs={{4,0},{8,4},{12,8},{16,12},{20,16},{24,20},{28,24},{5,1},{9,5},{13... | collective-permute-start | bytes 98312 | tf_op jit(solution)/shard_map/while/body/eval_jaxpr/ppermute | solution.py:21
  178.2 6.9 %collective-permute-start = (f32[2,8,512]{2,1,0:T(8,128)S(1)}, f32[2,8,512]{2,1,0:T(8,128)S(1)}, u32[]{:S(2)}, u32[]{:S(2)}) collective-permute-start(f32[2,8,512]{2,1,0:T(8,128)S(1)} %get-tuple-element.322), channel_id=1, source_target_pairs={{4,0},{8,4},{12,8},{16,12},{20,16},{24,20},{28,24},{5,1},{9,5},{13... | collective-permute-start | bytes 98312 | tf_op jit(solution)/shard_map/while/body/eval_jaxpr/ppermute | solution.py:21
  185.1 6.7 %collective-permute-start = (f32[2,8,512]{2,1,0:T(8,128)S(1)}, f32[2,8,512]{2,1,0:T(8,128)S(1)}, u32[]{:S(2)}, u32[]{:S(2)}) collective-permute-start(f32[2,8,512]{2,1,0:T(8,128)S(1)} %get-tuple-element.322), channel_id=1, source_target_pairs={{4,0},{8,4},{12,8},{16,12},{20,16},{24,20},{28,24},{5,1},{9,5},{13... | collective-permute-start | bytes 98312 | tf_op jit(solution)/shard_map/while/body/eval_jaxpr/ppermute | solution.py:21
  191.8 6.7 %collective-permute-start = (f32[2,8,512]{2,1,0:T(8,128)S(1)}, f32[2,8,512]{2,1,0:T(8,128)S(1)}, u32[]{:S(2)}, u32[]{:S(2)}) collective-permute-start(f32[2,8,512]{2,1,0:T(8,128)S(1)} %get-tuple-element.322), channel_id=1, source_target_pairs={{4,0},{8,4},{12,8},{16,12},{20,16},{24,20},{28,24},{5,1},{9,5},{13... | collective-permute-start | bytes 98312 | tf_op jit(solution)/shard_map/while/body/eval_jaxpr/ppermute | solution.py:21
  198.6 6.7 %collective-permute-start = (f32[2,8,512]{2,1,0:T(8,128)S(1)}, f32[2,8,512]{2,1,0:T(8,128)S(1)}, u32[]{:S(2)}, u32[]{:S(2)}) collective-permute-start(f32[2,8,512]{2,1,0:T(8,128)S(1)} %get-tuple-element.322), channel_id=1, source_target_pairs={{4,0},{8,4},{12,8},{16,12},{20,16},{24,20},{28,24},{5,1},{9,5},{13... | collective-permute-start | bytes 98312 | tf_op jit(solution)/shard_map/while/body/eval_jaxpr/ppermute | solution.py:21
  205.3 6.7 %collective-permute-start = (f32[2,8,512]{2,1,0:T(8,128)S(1)}, f32[2,8,512]{2,1,0:T(8,128)S(1)}, u32[]{:S(2)}, u32[]{:S(2)}) collective-permute-start(f32[2,8,512]{2,1,0:T(8,128)S(1)} %get-tuple-element.322), channel_id=1, source_target_pairs={{4,0},{8,4},{12,8},{16,12},{20,16},{24,20},{28,24},{5,1},{9,5},{13... | collective-permute-start | bytes 98312 | tf_op jit(solution)/shard_map/while/body/eval_jaxpr/ppermute | solution.py:21
  212.1 6.9 %collective-permute-start = (f32[2,8,512]{2,1,0:T(8,128)S(1)}, f32[2,8,512]{2,1,0:T(8,128)S(1)}, u32[]{:S(2)}, u32[]{:S(2)}) collective-permute-start(f32[2,8,512]{2,1,0:T(8,128)S(1)} %get-tuple-element.322), channel_id=1, source_target_pairs={{4,0},{8,4},{12,8},{16,12},{20,16},{24,20},{28,24},{5,1},{9,5},{13... | collective-permute-start | bytes 98312 | tf_op jit(solution)/shard_map/while/body/eval_jaxpr/ppermute | solution.py:21
  219.0 6.7 %collective-permute-start = (f32[2,8,512]{2,1,0:T(8,128)S(1)}, f32[2,8,512]{2,1,0:T(8,128)S(1)}, u32[]{:S(2)}, u32[]{:S(2)}) collective-permute-start(f32[2,8,512]{2,1,0:T(8,128)S(1)} %get-tuple-element.322), channel_id=1, source_target_pairs={{4,0},{8,4},{12,8},{16,12},{20,16},{24,20},{28,24},{5,1},{9,5},{13... | collective-permute-start | bytes 98312 | tf_op jit(solution)/shard_map/while/body/eval_jaxpr/ppermute | solution.py:21
  225.7 6.7 %collective-permute-start = (f32[2,8,512]{2,1,0:T(8,128)S(1)}, f32[2,8,512]{2,1,0:T(8,128)S(1)}, u32[]{:S(2)}, u32[]{:S(2)}) collective-permute-start(f32[2,8,512]{2,1,0:T(8,128)S(1)} %get-tuple-element.322), channel_id=1, source_target_pairs={{4,0},{8,4},{12,8},{16,12},{20,16},{24,20},{28,24},{5,1},{9,5},{13... | collective-permute-start | bytes 98312 | tf_op jit(solution)/shard_map/while/body/eval_jaxpr/ppermute | solution.py:21
  232.5 6.7 %collective-permute-start = (f32[2,8,512]{2,1,0:T(8,128)S(1)}, f32[2,8,512]{2,1,0:T(8,128)S(1)}, u32[]{:S(2)}, u32[]{:S(2)}) collective-permute-start(f32[2,8,512]{2,1,0:T(8,128)S(1)} %get-tuple-element.322), channel_id=1, source_target_pairs={{4,0},{8,4},{12,8},{16,12},{20,16},{24,20},{28,24},{5,1},{9,5},{13... | collective-permute-start | bytes 98312 | tf_op jit(solution)/shard_map/while/body/eval_jaxpr/ppermute | solution.py:21
  239.2 6.7 %collective-permute-start = (f32[2,8,512]{2,1,0:T(8,128)S(1)}, f32[2,8,512]{2,1,0:T(8,128)S(1)}, u32[]{:S(2)}, u32[]{:S(2)}) collective-permute-start(f32[2,8,512]{2,1,0:T(8,128)S(1)} %get-tuple-element.322), channel_id=1, source_target_pairs={{4,0},{8,4},{12,8},{16,12},{20,16},{24,20},{28,24},{5,1},{9,5},{13... | collective-permute-start | bytes 98312 | tf_op jit(solution)/shard_map/while/body/eval_jaxpr/ppermute | solution.py:21
  245.9 6.7 %collective-permute-start = (f32[2,8,512]{2,1,0:T(8,128)S(1)}, f32[2,8,512]{2,1,0:T(8,128)S(1)}, u32[]{:S(2)}, u32[]{:S(2)}) collective-permute-start(f32[2,8,512]{2,1,0:T(8,128)S(1)} %get-tuple-element.322), channel_id=1, source_target_pairs={{4,0},{8,4},{12,8},{16,12},{20,16},{24,20},{28,24},{5,1},{9,5},{13... | collective-permute-start | bytes 98312 | tf_op jit(solution)/shard_map/while/body/eval_jaxpr/ppermute | solution.py:21
  252.7 6.7 %collective-permute-start = (f32[2,8,512]{2,1,0:T(8,128)S(1)}, f32[2,8,512]{2,1,0:T(8,128)S(1)}, u32[]{:S(2)}, u32[]{:S(2)}) collective-permute-start(f32[2,8,512]{2,1,0:T(8,128)S(1)} %get-tuple-element.322), channel_id=1, source_target_pairs={{4,0},{8,4},{12,8},{16,12},{20,16},{24,20},{28,24},{5,1},{9,5},{13... | collective-permute-start | bytes 98312 | tf_op jit(solution)/shard_map/while/body/eval_jaxpr/ppermute | solution.py:21
  (4 other events, 52.0 us)
Sparse Core Ops, SparseCore 0:
  293.2 46.1 reduce-scatter.1
where the time goes:
time: 349 us; the launch traced here: 346 us
  waiting for transfers between devices  221 us (63%)
  starting transfers between devices  41.3 us (12%)
  matrix products  25.5 us (7%)
  other arithmetic  23.4 us (7%)
  local copies, waits for them, and re-layouts  20.6 us (6%)
  between operations  13.7 us (4%)
    ppermute x32, waiting for transfers between devices, shifted(): lax.ppermute(value, axis, [(source, source + steps) for source in range(i...  174 us
    reduce_scatter x1, waiting for transfers between devices, local(): lax.psum_scatter((lagged * scale).reshape(share_rows * lax.axis_size('win...  46.3 us
    ppermute x32, starting transfers between devices, shifted(): lax.ppermute(value, axis, [(source, source + steps) for source in range(i...  41.3 us
    cos x16, other arithmetic, forward_table(): return jnp.concatenate([jnp.cos(angles), -jnp.sin(angles)], axis=1)  17.7 us
    dot_general x16, matrix products, add_block(): jnp.dot(piece, forward_table(first, sample_block, samples, NF), precision...  17.5 us
    another operation x9, local copies, waits for them, and re-layouts, local(): cross = jnp.stack(columns, axis=1)  16.4 us
    dot_general x1, matrix products, local(): jnp.dot(cross.reshape(share_rows * lax.axis_size('win') * ch_dev, 2 * NF)...  7.96 us
  transfers between devices with their start and end apart: 33, of which 33 were waited for; matrix products, arithmetic and copies ran while one was open for 0% of the time, Pallas kernels for 0%

commit v1 on v0

v1 whole, which is shorter than its diff:
```python
import functools
import math

import jax
import jax.numpy as jnp
import ml_dtypes
import numpy as np
from jax import lax
from jax.experimental import pallas as pl
from jax.experimental.pallas import tpu as pltpu
from jax.sharding import PartitionSpec as P

NF = 256
MAXOFF = 256
MAXLAG = 200
EPS = 1e-06
WHITEN_BINS = 64
LANES = 128
SUB = 8
TILES = 2 * NF // LANES
BF16 = jnp.bfloat16
F32 = jnp.float32
MIB = 1 << 20


def split(table):
    high = table.astype(ml_dtypes.bfloat16)
    low = (table - high.astype(np.float64)).astype(ml_dtypes.bfloat16)
    return high, low


def phase(product, length):
    return (product % length) * (2.0 * math.pi / length)


def forward_tables(samples, chunk):
    freq = np.arange(1, NF + 1, dtype=np.int64)
    inner = phase(np.arange(chunk, dtype=np.int64)[:, None] * freq[None, :], samples)
    outer = phase(np.arange(samples // chunk, dtype=np.int64)[:, None] * chunk * freq[None, :], samples)
    twiddle = np.concatenate([np.cos(outer), np.sin(outer)], axis=1).astype(np.float32)
    return split(np.concatenate([np.cos(inner), -np.sin(inner)], axis=1)) + (twiddle,)


def inverse_tables(samples, scale):
    freq = np.arange(1, NF + 1, dtype=np.int64)
    lags = np.arange(-MAXLAG, MAXLAG, dtype=np.int64)
    angles = phase(freq[:, None] * lags[None, :], samples)
    return split(scale * np.concatenate([np.cos(angles), -np.sin(angles)], axis=0))


def halves(value):
    high = value.astype(BF16)
    return high, (value - high.astype(F32)).astype(BF16)


def mm(a, b):
    return jnp.dot(a, b, preferred_element_type=F32)


def column(ref, count):
    rows = lax.broadcasted_iota(jnp.int32, (count, LANES), 0)
    value = jnp.zeros((count, LANES), jnp.int32)
    for index in range(count):
        value = jnp.where(rows == index, ref[index], value)
    return value


def whiten_kernel(alive_ref, strain_ref, high_ref, low_ref, twiddle_ref, white_ref):
    wins, chans, samples = strain_ref.shape
    rows = wins * chans
    chunk = high_ref.shape[0]
    strain = strain_ref[...].reshape(rows, samples)
    pieces = samples // chunk
    stacked = jnp.concatenate([strain[:, a * chunk : (a + 1) * chunk] for a in range(pieces)], axis=0)
    x_high, x_low = halves(stacked)
    part = mm(x_high, high_ref[...]) + mm(x_high, low_ref[...]) + mm(x_low, high_ref[...])
    real = jnp.zeros((rows, NF), F32)
    imag = jnp.zeros((rows, NF), F32)
    for a in range(pieces):
        p_re = part[a * rows : (a + 1) * rows, :NF]
        p_im = part[a * rows : (a + 1) * rows, NF:]
        cos = twiddle_ref[a : a + 1, :NF]
        sin = twiddle_ref[a : a + 1, NF:]
        real = real + p_re * cos + p_im * sin
        imag = imag + p_im * cos - p_re * sin
    magnitude = jnp.sqrt(real * real + imag * imag)
    block_r = lax.broadcasted_iota(jnp.int32, (NF, NF), 0) // WHITEN_BINS
    block_c = lax.broadcasted_iota(jnp.int32, (NF, NF), 1) // WHITEN_BINS
    mean = jnp.where(block_r == block_c, 1.0 / WHITEN_BINS, 0.0).astype(BF16)
    m_high, m_low = halves(magnitude)
    level = mm(m_high, mean) + mm(m_low, mean) + EPS
    live = column(alive_ref, chans).astype(F32)
    for w in range(wins):
        keep = slice(w * chans, (w + 1) * chans)
        for tile in range(TILES):
            source = real if tile < TILES // 2 else imag
            lanes = slice(tile % (TILES // 2) * LANES, (tile % (TILES // 2) + 1) * LANES)
            white_ref[(tile * wins + w) * chans : (tile * wins + w + 1) * chans, :] = (
                source[keep, lanes] / level[keep, lanes] * live
            )


def whiten(strain, alive):
    wins, chans, samples = strain.shape
    chunk = min(256, samples)
    high, low, twiddle = forward_tables(samples, chunk)
    rows = wins * chans
    return pl.pallas_call(
        whiten_kernel,
        out_shape=jax.ShapeDtypeStruct((TILES * rows, LANES), F32),
        in_specs=[pl.BlockSpec(memory_space=pltpu.SMEM)] + [pl.BlockSpec(memory_space=pltpu.VMEM)] * 4,
        out_specs=pl.BlockSpec(memory_space=pltpu.VMEM),
        compiler_params=pltpu.CompilerParams(vmem_limit_bytes=32 * MIB),
        cost_estimate=pl.CostEstimate(flops=6 * rows * samples * 2 * NF, bytes_accessed=4 * rows * samples, transcendentals=0),
        name="whiten",
    )(alive, strain, high, low, twiddle)


def correlate_kernel(orders, wins, chans, share, lead_only, limit_ref, *refs):
    count = len(orders)
    blocks = refs[:count]
    high_ref, low_ref, out_ref = refs[count : count + 3]
    own, partner, x_high, x_low, lagged, in_sem, out_sem = refs[count + 3 :]
    groups = own.shape[0]
    octets = share // SUB
    place = lax.axis_index("win")

    def load(index):
        copies = []
        for position in range(groups):
            group = orders[index][position]
            target = own.at[group] if index == 0 else partner.at[group, :, :, pl.ds((index - 1) * chans, chans), :]
            copies.append(pltpu.make_async_copy(blocks[index].at[position], target, in_sem.at[index, position]))
        return copies

    def store(first, rows, source):
        return pltpu.make_async_copy(source, out_ref.at[pl.ds(first, rows)], out_sem.at[first // SUB])

    def work():
        copies = [copy for index in range(count) for copy in load(index)]
        for copy in copies:
            copy.start()
        limit = column(limit_ref, chans)
        have = (count - 1) * chans
        total = partner.shape[3]
        if have < total:
            partner[:, :, :, have:, :] = jnp.zeros(partner.shape[:3] + (total - have, LANES), F32)
        for copy in copies:
            copy.wait()
        row_ids = lax.broadcasted_iota(jnp.int32, (chans, LANES), 0)
        half = TILES // 2

        def octet(g, carry):
            first = pl.multiple_of(g * SUB, SUB)
            sums = [[jnp.zeros((chans, LANES), F32) for _ in range(TILES)] for _ in range(SUB)]
            for group in range(groups):
                for w in range(wins):
                    mine = [own[group, t, w] for t in range(TILES)]
                    now = [partner[group, t, w, pl.ds(first, SUB), :] for t in range(TILES)]
                    later = [partner[group, t, w, pl.ds(first + SUB, SUB), :] for t in range(TILES)]
                    for j in range(SUB):
                        if j + 1 < SUB:
                            theirs = [
                                pltpu.roll(jnp.where(row_ids > j, now[t], later[t]), SUB - 1 - j, 0)
                                for t in range(TILES)
                            ]
                        else:
                            theirs = later
                        for t in range(half):
                            a_re, a_im, b_re, b_im = mine[t], mine[t + half], theirs[t], theirs[t + half]
                            sums[j][t] = sums[j][t] + (a_re * b_re + a_im * b_im)
                            sums[j][t + half] = sums[j][t + half] + (a_im * b_re - a_re * b_im)
            offset = place * share + first
            for j in range(0, SUB, 2):
                pair = []
                for k in (j, j + 1):
                    keep = limit > offset + k
                    pair.append(jnp.concatenate([jnp.where(keep, value, 0.0) for value in sums[k]], axis=1))
                high, low = halves(jnp.concatenate(pair, axis=0))
                rows = pl.ds(pl.multiple_of((first + j) * chans, 2 * chans), 2 * chans)
                x_high[rows, :] = high
                x_low[rows, :] = low
            return carry

        step = octets // 2
        stores = []
        for part in range(2):
            lax.fori_loop(part * step, (part + 1) * step, octet, 0)
            rows = slice(part * step * SUB * chans, (part + 1) * step * SUB * chans)
            result = (
                mm(x_high[rows, :], high_ref[...]) + mm(x_high[rows, :], low_ref[...]) + mm(x_low[rows, :], high_ref[...])
            )
            lagged[part * step * SUB : (part + 1) * step * SUB] = result.reshape(step * SUB, chans, result.shape[1])
            copy = store(part * step * SUB, step * SUB, lagged.at[pl.ds(part * step * SUB, step * SUB)])
            copy.start()
            stores.append(copy)
        for copy in stores:
            copy.wait()

    def blank():
        step = octets // 2 * SUB
        lagged[:step] = jnp.zeros((step,) + lagged.shape[1:], F32)
        stores = [store(part * step, step, lagged.at[pl.ds(0, step)]) for part in range(2)]
        for copy in stores:
            copy.start()
        for copy in stores:
            copy.wait()

    if lead_only:
        pl.when(place == 0)(work)
        pl.when(place != 0)(blank)
    else:
        work()


def correlate(blocks, orders, offset_limit, wins, chans, share, samples, scale, lead_only):
    high, low = inverse_tables(samples, scale)
    groups = len(orders[0])
    shape = (groups, TILES, wins, chans, LANES)
    octets = share // SUB
    rows = share * chans
    lags = 2 * MAXLAG
    body = functools.partial(correlate_kernel, orders, wins, chans, share, lead_only)
    return pl.pallas_call(
        body,
        out_shape=jax.ShapeDtypeStruct((share, chans, lags), F32),
        in_specs=[pl.BlockSpec(memory_space=pltpu.SMEM)]
        + [pl.BlockSpec(memory_space=pl.ANY)] * len(blocks)
        + [pl.BlockSpec(memory_space=pltpu.VMEM)] * 2,
        out_specs=pl.BlockSpec(memory_space=pl.ANY),
        scratch_shapes=[
            pltpu.VMEM(shape, F32),
            pltpu.VMEM((groups, TILES, wins, share + SUB, LANES), F32),
            pltpu.VMEM((rows, 2 * NF), BF16),
            pltpu.VMEM((rows, 2 * NF), BF16),
            pltpu.VMEM((share, chans, lags), F32),
            pltpu.SemaphoreType.DMA((len(blocks), groups)),
            pltpu.SemaphoreType.DMA((octets,)),
        ],
        compiler_params=pltpu.CompilerParams(vmem_limit_bytes=32 * MIB),
        cost_estimate=pl.CostEstimate(flops=6 * rows * 2 * NF * lags, bytes_accessed=4 * rows * lags, transcendentals=0),
        name="correlate",
    )(offset_limit, *[block.reshape(shape) for block in blocks], high, low)


def local(strain, offset_limit, alive):
    win_dev, ch_dev, samples = strain.shape
    win_count = lax.axis_size("win")
    chan_count = lax.axis_size("chan")
    scale = 1.0 / math.sqrt(NF * win_dev * win_count)
    share = MAXOFF // win_count
    reach = share // ch_dev
    axes = ("chan", "win")
    finish = functools.partial(
        correlate,
        offset_limit=offset_limit,
        wins=win_dev,
        chans=ch_dev,
        share=share,
        samples=samples,
        scale=scale,
    )
    white = whiten(strain, alive)

    def device(chan, win):
        return chan * win_count + win

    def exchange(value, mask):
        pairs = [(device(c, w), device(c, w ^ mask)) for c in range(chan_count) for w in range(win_count)]
        return lax.ppermute(value, axes, pairs)

    def ahead(steps, source, target):
        return [(device(c + steps, source), device(c, target)) for c in range(chan_count - steps)]

    if win_count == 4 and chan_count * ch_dev <= share:
        block = white
        for mask in (2, 1):
            block = jnp.concatenate([block, exchange(block, mask)], axis=0)
        relative = (0, 2, 1, 3)
        near = (chan_count + 1) // 2
        blocks = [block, block]
        orders = [relative, relative]
        far, far_orders = [], []
        for k in range(chan_count - near):
            pairs = ahead(near + k, 3, 1)
            if k + 1 < near:
                pairs = pairs + ahead(k + 1, 0, 0)
            got = lax.ppermute(block, axes, pairs)
            if k + 1 < near:
                blocks.append(got)
                orders.append(relative)
            far.append(exchange(got, 1))
            far_orders.append(tuple(3 ^ r for r in relative))
        return finish(blocks + far, orders + far_orders, lead_only=True)

    gathered = lax.all_gather(white, "win", tiled=True)
    order = tuple(range(win_count))
    blocks = [gathered]
    for steps in range(reach + 1):
        pairs = [
            (device(c + reach * w + steps, w), device(c, w))
            for w in range(win_count)
            for c in range(chan_count)
            if c + reach * w + steps < chan_count
        ]
        blocks.append(lax.ppermute(gathered, axes, pairs) if pairs else jnp.zeros_like(gathered))
    return finish(blocks, [order] * len(blocks), lead_only=False)


def solution(mesh):
    in_specs = (P("win", "chan", None), P("chan"), P("chan"))
    out_specs = P("win", "chan", None)
    return jax.shard_map(local, mesh=mesh, in_specs=in_specs, out_specs=out_specs, check_vma=False)
```

time: 349 us -> 34.3 us (0.10)
  waiting for transfers between devices: 221 us -> 4.56 us
  matrix products: 25.5 us -> 0 us
  other arithmetic: 23.4 us -> 0.01 us
  starting transfers between devices: 41.3 us -> 18 us
  local copies, waits for them, and re-layouts: 20.6 us -> 5.01 us
  between operations: 13.7 us -> 0.08 us
  Pallas kernels: 0 us -> 6.33 us
    ppermute x32 -> x10, waiting for transfers between devices: 174 us -> 4.56 us  [the longest x6 4.47 us: exchange(): return lax.ppermute(value, axes, pairs)]
    reduce_scatter x1 -> x0, waiting for transfers between devices: 46.3 us -> none  [local(): lax.psum_scatter((lagged * scale).reshape(share_rows * lax.axis_size('win...]
    dot_general x17 -> x0, matrix products: 25.5 us -> none  [the longest x16 17.5 us: add_block(): jnp.dot(piece, forward_table(first, sample_block, samples, NF), precision...]
    ppermute x32 -> x10, starting transfers between devices: 41.3 us -> 18 us  [the longest x6 13.5 us: exchange(): return lax.ppermute(value, axes, pairs)]
    cos x17 -> x0, other arithmetic: 20.9 us -> none  [the longest x16 17.7 us: forward_table(): return jnp.concatenate([jnp.cos(angles), -jnp.sin(angles)], axis=1)]
    another operation x9 -> x0, local copies, waits for them, and re-layouts: 16.4 us -> none  [local(): cross = jnp.stack(columns, axis=1)]
    pallas_call x0 -> x2, Pallas kernels: none -> 6.33 us  [the longest x1 5.28 us: correlate(): pl.pallas_call(body, out_shape=jax.ShapeDtypeStruct((share, chans, lags),...]
    unnamed x11 -> x16, local copies, waits for them, and re-layouts: 0.04 us -> 5.01 us
  transfers between devices with their start and end apart: 33 -> 10, of which waited for: 33 -> 5; matrix products, arithmetic and copies ran while one was open for 0% -> 0% of each run, Pallas kernels for 0% -> 0%
where the time goes in v1:
time: 34.3 us; the launch traced here: 34 us
  starting transfers between devices  18 us (52%)
  Pallas kernels  6.33 us (18%)
  local copies, waits for them, and re-layouts  5.01 us (15%)
  waiting for transfers between devices  4.56 us (13%)
    ppermute x6, starting transfers between devices, exchange(): return lax.ppermute(value, axes, pairs)  13.5 us
    pallas_call x1, Pallas kernels, correlate(): pl.pallas_call(body, out_shape=jax.ShapeDtypeStruct((share, chans, lags),...  5.28 us
    unnamed x16, local copies, waits for them, and re-layouts  5.01 us
    ppermute x4, starting transfers between devices, local(): got = lax.ppermute(block, axes, pairs)  4.55 us
    ppermute x6, waiting for transfers between devices, exchange(): return lax.ppermute(value, axes, pairs)  4.47 us
    pallas_call x1, Pallas kernels, whiten(): pl.pallas_call(whiten_kernel, out_shape=jax.ShapeDtypeStruct((TILES * row...  1.05 us
  transfers between devices with their start and end apart: 10, of which 5 were waited for; matrix products, arithmetic and copies ran while one was open for 0% of the time, Pallas kernels for 0%

profile of v1, /device:TPU:0, one launch (start us, length us, event | category | flops | bytes accessed | tf_op | source)
XLA Modules:
  0.0 34.0 jit_solution(6435068141368982967)
XLA Ops:
  0.0 0.0 copy-start.1
  0.0 0.0 copy-start.2
  0.0 1.0 %copy-done.2 = f32[2,8,4096]{2,1,0:T(8,128)S(1)} copy-done((f32[2,8,4096]{2,1,0:T(8,128)S(1)}, f32[2,8,4096]{2,1,0:T(8,128)}, u32[]{:S(2)}) %copy-start.2) | copy-done | bytes 262168
  1.0 0.9 %copy-done.3 = bf16[256,512]{1,0:T(8,128)(2,1)S(1)} copy-done((bf16[256,512]{1,0:T(8,128)(2,1)S(1)}, bf16[256,512]{1,0:T(8,128)(2,1)}, u32[]{:S(2)}) %copy-start.3) | copy-done | bytes 262168
  2.0 0.9 %copy-done.4 = bf16[256,512]{1,0:T(8,128)(2,1)S(1)} copy-done((bf16[256,512]{1,0:T(8,128)(2,1)S(1)}, bf16[256,512]{1,0:T(8,128)(2,1)}, u32[]{:S(2)}) %copy-start.4) | copy-done | bytes 262168
  2.9 0.8 %copy-done.5 = f32[16,512]{1,0:T(8,128)S(1)} copy-done((f32[16,512]{1,0:T(8,128)S(1)}, f32[16,512]{1,0:T(8,128)}, u32[]{:S(2)}) %copy-start.5) | copy-done | bytes 32792
  3.7 0.7 %copy-done.6 = s32[8]{0:T(128)S(1)} copy-done((s32[8]{0:T(128)S(1)}, s32[8]{0:T(128)}, u32[]{:S(2)}) %copy-start.6) | copy-done | bytes 56
  4.4 1.0 %whiten.1 = f32[64,128]{1,0:T(8,128)S(1)} custom-call(s32[8]{0:T(128)S(1)} %copy-done.6, f32[2,8,4096]{2,1,0:T(8,128)S(1)} %copy-done.2, bf16[256,512]{1,0:T(8,128)(2,1)S(1)} %copy-done.4, bf16[256,512]{1,0:T(8,128)(2,1)S(1)} %copy-done.3, f32[16,512]{1,0:T(8,128)S(1)} %copy-done.5), custom_call_target="tpu_custom_call" | custom-call | flops 201326592 | bytes 262144 | tf_op jit(solution)/shard_map/whiten/pallas_call | solution.py:108
  5.4 3.0 %collective-permute-start = (f32[64,128]{1,0:T(8,128)S(1)}, f32[64,128]{1,0:T(8,128)S(1)}, u32[]{:S(2)}, u32[]{:S(2)}) collective-permute-start(f32[64,128]{1,0:T(8,128)S(1)} %whiten.1), channel_id=1, source_target_pairs={{0,2},{1,3},{2,0},{3,1},{4,6},{5,7},{6,4},{7,5},{8,10},{9,11},{10,... | collective-permute-start | bytes 98312 | tf_op jit(solution)/shard_map/ppermute | solution.py:270
  8.4 1.9 %collective-permute-done = f32[64,128]{1,0:T(8,128)S(1)} collective-permute-done((f32[64,128]{1,0:T(8,128)S(1)}, f32[64,128]{1,0:T(8,128)S(1)}, u32[]{:S(2)}, u32[]{:S(2)}) %collective-permute-start) | collective-permute-done | bytes 32800 | tf_op jit(solution)/shard_map/ppermute | solution.py:270
  10.3 0.0 collective-permute-start.1
  10.3 1.2 %collective-permute-done.1 = f32[128,128]{1,0:T(8,128)S(1)} collective-permute-done((f32[128,128]{1,0:T(8,128)S(1)}, f32[128,128]{1,0:T(8,128)S(1)}, u32[]{:S(2)}, u32[]{:S(2)}) %collective-permute-start.1) | collective-permute-done | bytes 65568 | tf_op jit(solution)/shard_map/ppermute | solution.py:270
  11.6 0.7 %collective-permute-start.8 = (f32[256,128]{1,0:T(8,128)S(1)}, f32[256,128]{1,0:T(8,128)S(1)}, u32[]{:S(2)}, u32[]{:S(2)}) collective-permute-start(f32[256,128]{1,0:T(8,128)S(1)} %pad_maximum_fusion), channel_id=1, source_target_pairs={{31,1}} | collective-permute-start | bytes 393224 | tf_op jit(solution)/shard_map/ppermute | solution.py:288
  12.3 1.3 %collective-permute-start.4 = (f32[256,128]{1,0:T(8,128)S(1)}, f32[256,128]{1,0:T(8,128)S(1)}, u32[]{:S(2)}, u32[]{:S(2)}) collective-permute-start(f32[256,128]{1,0:T(8,128)S(1)} %pad_maximum_fusion), channel_id=1, source_target_pairs={{27,1},{31,5},{12,0},{16,4},{20,8},{24,12},{28,16}} | collective-permute-start | bytes 393224 | tf_op jit(solution)/shard_map/ppermute | solution.py:288
  13.6 1.3 %collective-permute-start.3 = (f32[256,128]{1,0:T(8,128)S(1)}, f32[256,128]{1,0:T(8,128)S(1)}, u32[]{:S(2)}, u32[]{:S(2)}) collective-permute-start(f32[256,128]{1,0:T(8,128)S(1)} %pad_maximum_fusion), channel_id=1, source_target_pairs={{23,1},{27,5},{31,9},{8,0},{12,4},{16,8},{20,12},{24,16},{28,20}} | collective-permute-start | bytes 393224 | tf_op jit(solution)/shard_map/ppermute | solution.py:288
  14.9 1.3 %collective-permute-start.2 = (f32[256,128]{1,0:T(8,128)S(1)}, f32[256,128]{1,0:T(8,128)S(1)}, u32[]{:S(2)}, u32[]{:S(2)}) collective-permute-start(f32[256,128]{1,0:T(8,128)S(1)} %pad_maximum_fusion), channel_id=1, source_target_pairs={{19,1},{23,5},{27,9},{31,13},{4,0},{8,4},{12,8},{16,12},{20,16},{2... | collective-permute-start | bytes 393224 | tf_op jit(solution)/shard_map/ppermute | solution.py:288
  16.2 0.0 collective-permute-done.8
  16.2 5.3 %collective-permute-start.9 = (f32[256,128]{1,0:T(8,128)S(1)}, f32[256,128]{1,0:T(8,128)S(1)}, u32[]{:S(2)}, u32[]{:S(2)}) collective-permute-start(f32[256,128]{1,0:T(8,128)S(1)} %collective-permute-done.8), channel_id=1, source_target_pairs={{0,1},{1,0},{2,3},{3,2},{4,5},{5,4},{6,7},{7,6},{8,9},{9,8},{10,11... | collective-permute-start | bytes 393224 | tf_op jit(solution)/shard_map/ppermute | solution.py:270
  21.5 0.0 collective-permute-done.4
  21.5 0.0 collective-permute-start.7
  21.5 0.1 collective-permute-done.3
  21.6 5.1 %collective-permute-start.6 = (f32[256,128]{1,0:T(8,128)S(1)}, f32[256,128]{1,0:T(8,128)S(1)}, u32[]{:S(2)}, u32[]{:S(2)}) collective-permute-start(f32[256,128]{1,0:T(8,128)S(1)} %collective-permute-done.3), channel_id=1, source_target_pairs={{0,1},{1,0},{2,3},{3,2},{4,5},{5,4},{6,7},{7,6},{8,9},{9,8},{10,11... | collective-permute-start | bytes 393224 | tf_op jit(solution)/shard_map/ppermute | solution.py:270
  26.7 0.0 collective-permute-done.2
  26.7 0.0 collective-permute-start.5
  26.7 0.0 collective-permute-done.9
  26.7 0.0 collective-permute-done.7
  26.8 1.0 %collective-permute-done.6 = f32[256,128]{1,0:T(8,128)S(1)} collective-permute-done((f32[256,128]{1,0:T(8,128)S(1)}, f32[256,128]{1,0:T(8,128)S(1)}, u32[]{:S(2)}, u32[]{:S(2)}) %collective-permute-start.6) | collective-permute-done | bytes 131104 | tf_op jit(solution)/shard_map/ppermute | solution.py:270
  27.7 0.4 %collective-permute-done.5 = f32[256,128]{1,0:T(8,128)S(1)} collective-permute-done((f32[256,128]{1,0:T(8,128)S(1)}, f32[256,128]{1,0:T(8,128)S(1)}, u32[]{:S(2)}, u32[]{:S(2)}) %collective-permute-start.5) | collective-permute-done | bytes 131104 | tf_op jit(solution)/shard_map/ppermute | solution.py:270
  28.1 0.0 copy-done
  28.1 0.0 copy-done.1
  28.1 0.6 %copy-done.7 = s32[8]{0:T(128)S(1)} copy-done((s32[8]{0:T(128)S(1)}, s32[8]{0:T(128)}, u32[]{:S(2)}) %copy-start.7) | copy-done | bytes 56
  28.7 5.3 %correlate.1 = f32[64,8,400]{2,1,0:T(8,128)} custom-call(s32[8]{0:T(128)S(1)} %copy-done.7, f32[4,4,2,8,128]{4,3,2,1,0:T(8,128)S(1)} %bitcast.8, f32[4,4,2,8,128]{4,3,2,1,0:T(8,128)S(1)} %bitcast.9, f32[4,4,2,8,128]{4,3,2,1,0:T(8,128)S(1)} %bitcast.12, f32[4,4,2,8,128]{4,3,2,1,0:T(8,128)S(1)} %bitcast.11, f32[4,4,2,8,128]{4,3,2,1,0:T(8,128)S(1)} %bitcast.10, ...), custom_call_target="tpu_custom_call" | custom-call | flops 629145600 | bytes 819200 | tf_op jit(solution)/shard_map/correlate/pallas_call | solution.py:224
  (8 shorter events, 0.0 us)
Async XLA Ops:
  0.0 28.1 %copy-start = (bf16[512,400]{1,0:T(8,128)(2,1)S(1)}, bf16[512,400]{1,0:T(8,128)(2,1)}, u32[]{:S(2)}) copy-start(bf16[512,400]{1,0:T(8,128)(2,1)} %constant.14.clone.refs_10_) | copy-start | bytes 1228804
  0.0 28.1 %copy-start.1 = (bf16[512,400]{1,0:T(8,128)(2,1)S(1)}, bf16[512,400]{1,0:T(8,128)(2,1)}, u32[]{:S(2)}) copy-start(bf16[512,400]{1,0:T(8,128)(2,1)} %constant.13.clone.refs_9_) | copy-start | bytes 1228804
  0.0 1.0 %copy-start.2 = (f32[2,8,4096]{2,1,0:T(8,128)S(1)}, f32[2,8,4096]{2,1,0:T(8,128)}, u32[]{:S(2)}) copy-start(f32[2,8,4096]{2,1,0:T(8,128)} %strain_ref.1) | copy-start | bytes 786436
  1.0 0.9 %copy-start.3 = (bf16[256,512]{1,0:T(8,128)(2,1)S(1)}, bf16[256,512]{1,0:T(8,128)(2,1)}, u32[]{:S(2)}) copy-start(bf16[256,512]{1,0:T(8,128)(2,1)} %constant.11.clone.low_ref) | copy-start | bytes 786436
  2.0 0.9 %copy-start.4 = (bf16[256,512]{1,0:T(8,128)(2,1)S(1)}, bf16[256,512]{1,0:T(8,128)(2,1)}, u32[]{:S(2)}) copy-start(bf16[256,512]{1,0:T(8,128)(2,1)} %constant.10.clone.high_ref) | copy-start | bytes 786436
  2.9 0.8 %copy-start.5 = (f32[16,512]{1,0:T(8,128)S(1)}, f32[16,512]{1,0:T(8,128)}, u32[]{:S(2)}) copy-start(f32[16,512]{1,0:T(8,128)} %constant.12.clone.twiddle_ref) | copy-start | bytes 98308
  3.7 0.7 %copy-start.6 = (s32[8]{0:T(128)S(1)}, s32[8]{0:T(128)}, u32[]{:S(2)}) copy-start(s32[8]{0:T(128)} %alive_ref.1) | copy-start | bytes 100
  5.4 4.9 %collective-permute-start = (f32[64,128]{1,0:T(8,128)S(1)}, f32[64,128]{1,0:T(8,128)S(1)}, u32[]{:S(2)}, u32[]{:S(2)}) collective-permute-start(f32[64,128]{1,0:T(8,128)S(1)} %whiten.1), channel_id=1, source_target_pairs={{0,2},{1,3},{2,0},{3,1},{4,6},{5,7},{6,4},{7,5},{8,10},{9,11},{10,... | collective-permute-start | bytes 98312 | tf_op jit(solution)/shard_map/ppermute | solution.py:270
  10.3 1.3 %collective-permute-start.1 = (f32[128,128]{1,0:T(8,128)S(1)}, f32[128,128]{1,0:T(8,128)S(1)}, u32[]{:S(2)}, u32[]{:S(2)}) collective-permute-start(f32[128,128]{1,0:T(8,128)S(1)} %pad_maximum_fusion.1), channel_id=1, source_target_pairs={{0,1},{1,0},{2,3},{3,2},{4,5},{5,4},{6,7},{7,6},{8,9},{9,8},{10,11... | collective-permute-start | bytes 196616 | tf_op jit(solution)/shard_map/ppermute | solution.py:270
  11.6 4.6 %collective-permute-start.8 = (f32[256,128]{1,0:T(8,128)S(1)}, f32[256,128]{1,0:T(8,128)S(1)}, u32[]{:S(2)}, u32[]{:S(2)}) collective-permute-start(f32[256,128]{1,0:T(8,128)S(1)} %pad_maximum_fusion), channel_id=1, source_target_pairs={{31,1}} | collective-permute-start | bytes 393224 | tf_op jit(solution)/shard_map/ppermute | solution.py:288
  12.3 9.2 %collective-permute-start.4 = (f32[256,128]{1,0:T(8,128)S(1)}, f32[256,128]{1,0:T(8,128)S(1)}, u32[]{:S(2)}, u32[]{:S(2)}) collective-permute-start(f32[256,128]{1,0:T(8,128)S(1)} %pad_maximum_fusion), channel_id=1, source_target_pairs={{27,1},{31,5},{12,0},{16,4},{20,8},{24,12},{28,16}} | collective-permute-start | bytes 393224 | tf_op jit(solution)/shard_map/ppermute | solution.py:288
  13.6 8.0 %collective-permute-start.3 = (f32[256,128]{1,0:T(8,128)S(1)}, f32[256,128]{1,0:T(8,128)S(1)}, u32[]{:S(2)}, u32[]{:S(2)}) collective-permute-start(f32[256,128]{1,0:T(8,128)S(1)} %pad_maximum_fusion), channel_id=1, source_target_pairs={{23,1},{27,5},{31,9},{8,0},{12,4},{16,8},{20,12},{24,16},{28,20}} | collective-permute-start | bytes 393224 | tf_op jit(solution)/shard_map/ppermute | solution.py:288
  14.9 11.9 %collective-permute-start.2 = (f32[256,128]{1,0:T(8,128)S(1)}, f32[256,128]{1,0:T(8,128)S(1)}, u32[]{:S(2)}, u32[]{:S(2)}) collective-permute-start(f32[256,128]{1,0:T(8,128)S(1)} %pad_maximum_fusion), channel_id=1, source_target_pairs={{19,1},{23,5},{27,9},{31,13},{4,0},{8,4},{12,8},{16,12},{20,16},{2... | collective-permute-start | bytes 393224 | tf_op jit(solution)/shard_map/ppermute | solution.py:288
  16.2 10.6 %collective-permute-start.9 = (f32[256,128]{1,0:T(8,128)S(1)}, f32[256,128]{1,0:T(8,128)S(1)}, u32[]{:S(2)}, u32[]{:S(2)}) collective-permute-start(f32[256,128]{1,0:T(8,128)S(1)} %collective-permute-done.8), channel_id=1, source_target_pairs={{0,1},{1,0},{2,3},{3,2},{4,5},{5,4},{6,7},{7,6},{8,9},{9,8},{10,11... | collective-permute-start | bytes 393224 | tf_op jit(solution)/shard_map/ppermute | solution.py:270
  21.5 5.2 %collective-permute-start.7 = (f32[256,128]{1,0:T(8,128)S(1)}, f32[256,128]{1,0:T(8,128)S(1)}, u32[]{:S(2)}, u32[]{:S(2)}) collective-permute-start(f32[256,128]{1,0:T(8,128)S(1)} %collective-permute-done.4), channel_id=1, source_target_pairs={{0,1},{1,0},{2,3},{3,2},{4,5},{5,4},{6,7},{7,6},{8,9},{9,8},{10,11... | collective-permute-start | bytes 393224 | tf_op jit(solution)/shard_map/ppermute | solution.py:270
  21.6 6.1 %collective-permute-start.6 = (f32[256,128]{1,0:T(8,128)S(1)}, f32[256,128]{1,0:T(8,128)S(1)}, u32[]{:S(2)}, u32[]{:S(2)}) collective-permute-start(f32[256,128]{1,0:T(8,128)S(1)} %collective-permute-done.3), channel_id=1, source_target_pairs={{0,1},{1,0},{2,3},{3,2},{4,5},{5,4},{6,7},{7,6},{8,9},{9,8},{10,11... | collective-permute-start | bytes 393224 | tf_op jit(solution)/shard_map/ppermute | solution.py:270
  26.7 1.3 %collective-permute-start.5 = (f32[256,128]{1,0:T(8,128)S(1)}, f32[256,128]{1,0:T(8,128)S(1)}, u32[]{:S(2)}, u32[]{:S(2)}) collective-permute-start(f32[256,128]{1,0:T(8,128)S(1)} %collective-permute-done.2), channel_id=1, source_target_pairs={{0,1},{1,0},{2,3},{3,2},{4,5},{5,4},{6,7},{7,6},{8,9},{9,8},{10,11... | collective-permute-start | bytes 393224 | tf_op jit(solution)/shard_map/ppermute | solution.py:270
  28.1 0.7 %copy-start.7 = (s32[8]{0:T(128)S(1)}, s32[8]{0:T(128)}, u32[]{:S(2)}) copy-start(s32[8]{0:T(128)} %limit_ref.1) | copy-start | bytes 100

commit v2 on v1

--- a/solution.py
+++ b/solution.py
@@ -65,15 +65,33 @@
     return value
 
 
-def whiten_kernel(alive_ref, strain_ref, high_ref, low_ref, twiddle_ref, white_ref):
+def whiten_kernel(alive_hbm, limit_hbm, strain_hbm, table_hbm, twiddle_hbm, white_ref, limit_out, *scratch):
+    alive_ref, limit_ref, strain_ref, table_ref, twiddle_ref, sems = scratch
     wins, chans, samples = strain_ref.shape
+    chunk = table_ref.shape[0] // 2
+    copies = [
+        pltpu.make_async_copy(source, target, sems.at[index])
+        for index, (source, target) in enumerate(
+            [
+                (strain_hbm, strain_ref),
+                (table_hbm, table_ref),
+                (twiddle_hbm, twiddle_ref),
+                (alive_hbm, alive_ref),
+                (limit_hbm, limit_ref),
+            ]
+        )
+    ]
+    for copy in copies:
+        copy.start()
+    for copy in copies:
+        copy.wait()
     rows = wins * chans
-    chunk = high_ref.shape[0]
     strain = strain_ref[...].reshape(rows, samples)
     pieces = samples // chunk
     stacked = jnp.concatenate([strain[:, a * chunk : (a + 1) * chunk] for a in range(pieces)], axis=0)
     x_high, x_low = halves(stacked)
-    part = mm(x_high, high_ref[...]) + mm(x_high, low_ref[...]) + mm(x_low, high_ref[...])
+    high = table_ref[:chunk, :]
+    part = mm(x_high, high) + mm(x_high, table_ref[chunk:, :]) + mm(x_low, high)
     real = jnp.zeros((rows, NF), F32)
     imag = jnp.zeros((rows, NF), F32)
     for a in range(pieces):
@@ -90,6 +108,7 @@
     m_high, m_low = halves(magnitude)
     level = mm(m_high, mean) + mm(m_low, mean) + EPS
     live = column(alive_ref, chans).astype(F32)
+    limit_out[...] = column(limit_ref, chans)
     for w in range(wins):
         keep = slice(w * chans, (w + 1) * chans)
         for tile in range(TILES):
@@ -100,20 +119,32 @@
             )
 
 
-def whiten(strain, alive):
+def whiten(strain, alive, offset_limit):
     wins, chans, samples = strain.shape
     chunk = min(256, samples)
     high, low, twiddle = forward_tables(samples, chunk)
+    table = np.concatenate([high, low], axis=0)
     rows = wins * chans
     return pl.pallas_call(
         whiten_kernel,
-        out_shape=jax.ShapeDtypeStruct((TILES * rows, LANES), F32),
-        in_specs=[pl.BlockSpec(memory_space=pltpu.SMEM)] + [pl.BlockSpec(memory_space=pltpu.VMEM)] * 4,
-        out_specs=pl.BlockSpec(memory_space=pltpu.VMEM),
+        out_shape=(
+            jax.ShapeDtypeStruct((TILES * rows, LANES), F32),
+            jax.ShapeDtypeStruct((chans, LANES), jnp.int32),
+        ),
+        in_specs=[pl.BlockSpec(memory_space=pltpu.HBM)] * 5,
+        out_specs=(pl.BlockSpec(memory_space=pltpu.VMEM),) * 2,
+        scratch_shapes=[
+            pltpu.SMEM((chans,), jnp.int32),
+            pltpu.SMEM((chans,), jnp.int32),
+            pltpu.VMEM(strain.shape, F32),
+            pltpu.VMEM(table.shape, BF16),
+            pltpu.VMEM(twiddle.shape, F32),
+            pltpu.SemaphoreType.DMA((5,)),
+        ],
         compiler_params=pltpu.CompilerParams(vmem_limit_bytes=32 * MIB),
         cost_estimate=pl.CostEstimate(flops=6 * rows * samples * 2 * NF, bytes_accessed=4 * rows * samples, transcendentals=0),
         name="whiten",
-    )(alive, strain, high, low, twiddle)
+    )(*[pltpu.with_memory_space_constraint(jnp.asarray(x), pltpu.HBM) for x in (alive, offset_limit, strain, table, twiddle)])
 
 
 def correlate_kernel(orders, wins, chans, share, lead_only, limit_ref, *refs):
@@ -140,14 +171,13 @@
         copies = [copy for index in range(count) for copy in load(index)]
         for copy in copies:
             copy.start()
-        limit = column(limit_ref, chans)
+        limit = limit_ref[...]
         have = (count - 1) * chans
         total = partner.shape[3]
         if have < total:
             partner[:, :, :, have:, :] = jnp.zeros(partner.shape[:3] + (total - have, LANES), F32)
         for copy in copies:
             copy.wait()
-        row_ids = lax.broadcasted_iota(jnp.int32, (chans, LANES), 0)
         half = TILES // 2
 
         def octet(g, carry):
@@ -156,16 +186,8 @@
             for group in range(groups):
                 for w in range(wins):
                     mine = [own[group, t, w] for t in range(TILES)]
-                    now = [partner[group, t, w, pl.ds(first, SUB), :] for t in range(TILES)]
-                    later = [partner[group, t, w, pl.ds(first + SUB, SUB), :] for t in range(TILES)]
                     for j in range(SUB):
-                        if j + 1 < SUB:
-                            theirs = [
-                                pltpu.roll(jnp.where(row_ids > j, now[t], later[t]), SUB - 1 - j, 0)
-                                for t in range(TILES)
-                            ]
-                        else:
-                            theirs = later
+                        theirs = [partner[group, t, w, pl.ds(first + j + 1, SUB), :] for t in range(TILES)]
                         for t in range(half):
                             a_re, a_im, b_re, b_im = mine[t], mine[t + half], theirs[t], theirs[t + half]
                             sums[j][t] = sums[j][t] + (a_re * b_re + a_im * b_im)
@@ -213,7 +235,7 @@
         work()
 
 
-def correlate(blocks, orders, offset_limit, wins, chans, share, samples, scale, lead_only):
+def correlate(blocks, orders, limit, wins, chans, share, samples, scale, lead_only):
     high, low = inverse_tables(samples, scale)
     groups = len(orders[0])
     shape = (groups, TILES, wins, chans, LANES)
@@ -224,7 +246,7 @@
     return pl.pallas_call(
         body,
         out_shape=jax.ShapeDtypeStruct((share, chans, lags), F32),
-        in_specs=[pl.BlockSpec(memory_space=pltpu.SMEM)]
+        in_specs=[pl.BlockSpec(memory_space=pltpu.VMEM)]
         + [pl.BlockSpec(memory_space=pl.ANY)] * len(blocks)
         + [pl.BlockSpec(memory_space=pltpu.VMEM)] * 2,
         out_specs=pl.BlockSpec(memory_space=pl.ANY),
@@ -240,7 +262,7 @@
         compiler_params=pltpu.CompilerParams(vmem_limit_bytes=32 * MIB),
         cost_estimate=pl.CostEstimate(flops=6 * rows * 2 * NF * lags, bytes_accessed=4 * rows * lags, transcendentals=0),
         name="correlate",
-    )(offset_limit, *[block.reshape(shape) for block in blocks], high, low)
+    )(limit, *[block.reshape(shape) for block in blocks], high, low)
 
 
 def local(strain, offset_limit, alive):
@@ -251,16 +273,16 @@
     share = MAXOFF // win_count
     reach = share // ch_dev
     axes = ("chan", "win")
+    white, limit = whiten(strain, alive, offset_limit)
     finish = functools.partial(
         correlate,
-        offset_limit=offset_limit,
+        limit=limit,
         wins=win_dev,
         chans=ch_dev,
         share=share,
         samples=samples,
         scale=scale,
     )
-    white = whiten(strain, alive)
 
     def device(chan, win):
         return chan * win_count + win
@@ -277,21 +299,16 @@
         for mask in (2, 1):
             block = jnp.concatenate([block, exchange(block, mask)], axis=0)
         relative = (0, 2, 1, 3)
-        near = (chan_count + 1) // 2
-        blocks = [block, block]
-        orders = [relative, relative]
-        far, far_orders = [], []
-        for k in range(chan_count - near):
-            pairs = ahead(near + k, 3, 1)
-            if k + 1 < near:
-                pairs = pairs + ahead(k + 1, 0, 0)
-            got = lax.ppermute(block, axes, pairs)
-            if k + 1 < near:
-                blocks.append(got)
-                orders.append(relative)
-            far.append(exchange(got, 1))
-            far_orders.append(tuple(3 ^ r for r in relative))
-        return finish(blocks + far, orders + far_orders, lead_only=True)
+        crossed = tuple(3 ^ r for r in relative)
+        blocks, orders = {0: block}, {0: relative}
+        blocks[1], orders[1] = lax.ppermute(block, axes, ahead(1, 0, 0)), relative
+        for even in range(2, chan_count, 2):
+            pairs = ahead(even, 3, 0) + ahead(even + 1, 0, 1)
+            blocks[even], orders[even] = lax.ppermute(block, axes, pairs), crossed
+            if even + 1 < chan_count:
+                blocks[even + 1], orders[even + 1] = exchange(blocks[even], 1), relative
+        near = range(chan_count)
+        return finish([block] + [blocks[d] for d in near], [relative] + [orders[d] for d in near], lead_only=True)
 
     gathered = lax.all_gather(white, "win", tiled=True)
     order = tuple(range(win_count))

time: 34.3 us -> 26.1 us (0.76)
  starting transfers between devices: 18 us -> 8.84 us
  waiting for transfers between devices: 4.56 us -> 10.8 us
  local copies, waits for them, and re-layouts: 5.01 us -> 0.02 us
    ppermute x6 -> x5, starting transfers between devices: 13.5 us -> 3.68 us  [exchange(): return lax.ppermute(value, axes, pairs)]
    ppermute x4, waiting for transfers between devices: 0.08 us -> 7.66 us  [the longest x3 6.43 us: local(): blocks[even], orders[even] = (lax.ppermute(block, axes, pairs), crossed)]
    unnamed x16 -> x6, local copies, waits for them, and re-layouts: 5.01 us -> 0.02 us
    ppermute x6 -> x5, waiting for transfers between devices: 4.47 us -> 3.13 us  [exchange(): return lax.ppermute(value, axes, pairs)]
    pallas_call x1, Pallas kernels: 5.28 us -> 4.37 us  [correlate(): pl.pallas_call(body, out_shape=jax.ShapeDtypeStruct((share, chans, lags),...]
    pallas_call x1, Pallas kernels: 1.05 us -> 1.78 us  [whiten(): pl.pallas_call(whiten_kernel, out_shape=(jax.ShapeDtypeStruct((TILES * ro...]
    ppermute x4, starting transfers between devices: 4.55 us -> 5.16 us  [the longest x3 3.86 us: local(): blocks[even], orders[even] = (lax.ppermute(block, axes, pairs), crossed)]
  transfers between devices with their start and end apart: 10 -> 9, of which waited for: 5 -> 5; matrix products, arithmetic and copies ran while one was open for 0% -> 0% of each run, Pallas kernels for 0% -> 0%
where the time goes in v2:
time: 26.1 us; the launch traced here: 25.9 us
  waiting for transfers between devices  10.8 us (41%)
  starting transfers between devices  8.84 us (34%)
  Pallas kernels  6.16 us (24%)
    ppermute x3, waiting for transfers between devices, local(): blocks[even], orders[even] = (lax.ppermute(block, axes, pairs), crossed)  6.43 us
    pallas_call x1, Pallas kernels, correlate(): pl.pallas_call(body, out_shape=jax.ShapeDtypeStruct((share, chans, lags),...  4.37 us
    ppermute x3, starting transfers between devices, local(): blocks[even], orders[even] = (lax.ppermute(block, axes, pairs), crossed)  3.86 us
    ppermute x5, starting transfers between devices, exchange(): return lax.ppermute(value, axes, pairs)  3.68 us
    ppermute x5, waiting for transfers between devices, exchange(): return lax.ppermute(value, axes, pairs)  3.13 us
    pallas_call x1, Pallas kernels, whiten(): pl.pallas_call(whiten_kernel, out_shape=(jax.ShapeDtypeStruct((TILES * ro...  1.78 us
    ppermute x1, starting transfers between devices, local(): blocks[1], orders[1] = (lax.ppermute(block, axes, ahead(1, 0, 0)), relative)  1.29 us
    ppermute x1, waiting for transfers between devices, local(): blocks[1], orders[1] = (lax.ppermute(block, axes, ahead(1, 0, 0)), relative)  1.23 us
  transfers between devices with their start and end apart: 9, of which 5 were waited for; matrix products, arithmetic and copies ran while one was open for 0% of the time, Pallas kernels for 0%

profile of v2, /device:TPU:0, one launch (start us, length us, event | category | flops | bytes accessed | tf_op | source)
XLA Modules:
  0.0 25.9 jit_solution(261278598729509251)
XLA Ops:
  0.0 0.0 copy-start
  0.0 0.0 copy-start.1
  0.0 1.8 %whiten.1 = (f32[64,128]{1,0:T(8,128)S(1)}, s32[8,128]{1,0:T(8,128)S(1)}) custom-call(s32[8]{0:T(128)} %alive_hbm.1, s32[8]{0:T(128)} %limit_hbm.1, f32[2,8,4096]{2,1,0:T(8,128)} %strain_hbm.1, bf16[512,512]{1,0:T(8,128)(2,1)} %constant.8.clone.table_hbm, f32[16,512]{1,0:T(8,128)} %constant.9.clone.twiddle_hbm), custom_call_target="tpu_custom_call" | custom-call | flops 201326592 | bytes 262144 | tf_op jit(solution)/shard_map/whiten/pallas_call | solution.py:128
  1.8 3.0 %collective-permute-start = (f32[64,128]{1,0:T(8,128)S(1)}, f32[64,128]{1,0:T(8,128)S(1)}, u32[]{:S(2)}, u32[]{:S(2)}) collective-permute-start(f32[64,128]{1,0:T(8,128)S(1)} %get-tuple-element.8), channel_id=1, source_target_pairs={{0,2},{1,3},{2,0},{3,1},{4,6},{5,7},{6,4},{7,5},{8,10},{9,11},{10,... | collective-permute-start | bytes 98312 | tf_op jit(solution)/shard_map/ppermute | solution.py:292
  4.8 1.9 %collective-permute-done = f32[64,128]{1,0:T(8,128)S(1)} collective-permute-done((f32[64,128]{1,0:T(8,128)S(1)}, f32[64,128]{1,0:T(8,128)S(1)}, u32[]{:S(2)}, u32[]{:S(2)}) %collective-permute-start) | collective-permute-done | bytes 32800 | tf_op jit(solution)/shard_map/ppermute | solution.py:292
  6.7 0.0 collective-permute-start.1
  6.7 1.2 %collective-permute-done.1 = f32[128,128]{1,0:T(8,128)S(1)} collective-permute-done((f32[128,128]{1,0:T(8,128)S(1)}, f32[128,128]{1,0:T(8,128)S(1)}, u32[]{:S(2)}, u32[]{:S(2)}) %collective-permute-start.1) | collective-permute-done | bytes 65568 | tf_op jit(solution)/shard_map/ppermute | solution.py:292
  8.0 1.3 %collective-permute-start.7 = (f32[256,128]{1,0:T(8,128)S(1)}, f32[256,128]{1,0:T(8,128)S(1)}, u32[]{:S(2)}, u32[]{:S(2)}) collective-permute-start(f32[256,128]{1,0:T(8,128)S(1)} %constant_dynamic-update-slice_fusion), channel_id=1, source_target_pairs={{27,0},{31,4},{28,1}} | collective-permute-start | bytes 393224 | tf_op jit(solution)/shard_map/ppermute | solution.py:307
  9.3 1.3 %collective-permute-start.5 = (f32[256,128]{1,0:T(8,128)S(1)}, f32[256,128]{1,0:T(8,128)S(1)}, u32[]{:S(2)}, u32[]{:S(2)}) collective-permute-start(f32[256,128]{1,0:T(8,128)S(1)} %constant_dynamic-update-slice_fusion), channel_id=1, source_target_pairs={{19,0},{23,4},{27,8},{31,12},{20,1},{24,5},{28,9}} | collective-permute-start | bytes 393224 | tf_op jit(solution)/shard_map/ppermute | solution.py:307
  10.6 1.3 %collective-permute-start.3 = (f32[256,128]{1,0:T(8,128)S(1)}, f32[256,128]{1,0:T(8,128)S(1)}, u32[]{:S(2)}, u32[]{:S(2)}) collective-permute-start(f32[256,128]{1,0:T(8,128)S(1)} %constant_dynamic-update-slice_fusion), channel_id=1, source_target_pairs={{11,0},{15,4},{19,8},{23,12},{27,16},{31,20},{12,1},{16,5},{20,9},... | collective-permute-start | bytes 393224 | tf_op jit(solution)/shard_map/ppermute | solution.py:307
  11.9 1.3 %collective-permute-start.2 = (f32[256,128]{1,0:T(8,128)S(1)}, f32[256,128]{1,0:T(8,128)S(1)}, u32[]{:S(2)}, u32[]{:S(2)}) collective-permute-start(f32[256,128]{1,0:T(8,128)S(1)} %constant_dynamic-update-slice_fusion), channel_id=1, source_target_pairs={{4,0},{8,4},{12,8},{16,12},{20,16},{24,20},{28,24}} | collective-permute-start | bytes 393224 | tf_op jit(solution)/shard_map/ppermute | solution.py:304
  13.2 4.0 %collective-permute-done.7 = f32[256,128]{1,0:T(8,128)S(1)} collective-permute-done((f32[256,128]{1,0:T(8,128)S(1)}, f32[256,128]{1,0:T(8,128)S(1)}, u32[]{:S(2)}, u32[]{:S(2)}) %collective-permute-start.7) | collective-permute-done | bytes 131104 | tf_op jit(solution)/shard_map/ppermute | solution.py:307
  17.1 0.2 collective-permute-start.8
  17.3 2.5 %collective-permute-done.5 = f32[256,128]{1,0:T(8,128)S(1)} collective-permute-done((f32[256,128]{1,0:T(8,128)S(1)}, f32[256,128]{1,0:T(8,128)S(1)}, u32[]{:S(2)}, u32[]{:S(2)}) %collective-permute-start.5) | collective-permute-done | bytes 131104 | tf_op jit(solution)/shard_map/ppermute | solution.py:307
  19.7 0.3 %collective-permute-start.6 = (f32[256,128]{1,0:T(8,128)S(1)}, f32[256,128]{1,0:T(8,128)S(1)}, u32[]{:S(2)}, u32[]{:S(2)}) collective-permute-start(f32[256,128]{1,0:T(8,128)S(1)} %collective-permute-done.5), channel_id=1, source_target_pairs={{0,1},{1,0},{2,3},{3,2},{4,5},{5,4},{6,7},{7,6},{8,9},{9,8},{10,11... | collective-permute-start | bytes 393224 | tf_op jit(solution)/shard_map/ppermute | solution.py:292
  20.0 0.0 collective-permute-done.3
  20.0 0.2 collective-permute-start.4
  20.3 1.2 %collective-permute-done.2 = f32[256,128]{1,0:T(8,128)S(1)} collective-permute-done((f32[256,128]{1,0:T(8,128)S(1)}, f32[256,128]{1,0:T(8,128)S(1)}, u32[]{:S(2)}, u32[]{:S(2)}) %collective-permute-start.2) | collective-permute-done | bytes 131104 | tf_op jit(solution)/shard_map/ppermute | solution.py:304
  21.5 0.0 collective-permute-done.8
  21.5 0.0 collective-permute-done.6
  21.5 0.0 collective-permute-done.4
  21.5 0.0 copy-done
  21.5 0.0 copy-done.1
  21.5 4.4 %correlate.1 = f32[64,8,400]{2,1,0:T(8,128)} custom-call(s32[8,128]{1,0:T(8,128)S(1)} %get-tuple-element.7.limit_ref, f32[4,4,2,8,128]{4,3,2,1,0:T(8,128)S(1)} %bitcast.8, f32[4,4,2,8,128]{4,3,2,1,0:T(8,128)S(1)} %bitcast.9, f32[4,4,2,8,128]{4,3,2,1,0:T(8,128)S(1)} %bitcast.13, f32[4,4,2,8,128]{4,3,2,1,0:T(8,128)S(1)} %bitcast.12, ...), custom_call_target="tpu_custom_call" | custom-call | flops 629145600 | bytes 819200 | tf_op jit(solution)/shard_map/correlate/pallas_call | solution.py:246
  (4 shorter events, 0.0 us)
Async XLA Ops:
  0.0 21.5 %copy-start = (bf16[512,400]{1,0:T(8,128)(2,1)S(1)}, bf16[512,400]{1,0:T(8,128)(2,1)}, u32[]{:S(2)}) copy-start(bf16[512,400]{1,0:T(8,128)(2,1)} %constant.11.clone.refs_10_) | copy-start | bytes 1228804
  0.0 21.5 %copy-start.1 = (bf16[512,400]{1,0:T(8,128)(2,1)S(1)}, bf16[512,400]{1,0:T(8,128)(2,1)}, u32[]{:S(2)}) copy-start(bf16[512,400]{1,0:T(8,128)(2,1)} %constant.10.clone.refs_9_) | copy-start | bytes 1228804
  1.8 4.9 %collective-permute-start = (f32[64,128]{1,0:T(8,128)S(1)}, f32[64,128]{1,0:T(8,128)S(1)}, u32[]{:S(2)}, u32[]{:S(2)}) collective-permute-start(f32[64,128]{1,0:T(8,128)S(1)} %get-tuple-element.8), channel_id=1, source_target_pairs={{0,2},{1,3},{2,0},{3,1},{4,6},{5,7},{6,4},{7,5},{8,10},{9,11},{10,... | collective-permute-start | bytes 98312 | tf_op jit(solution)/shard_map/ppermute | solution.py:292
  6.7 1.3 %collective-permute-start.1 = (f32[128,128]{1,0:T(8,128)S(1)}, f32[128,128]{1,0:T(8,128)S(1)}, u32[]{:S(2)}, u32[]{:S(2)}) collective-permute-start(f32[128,128]{1,0:T(8,128)S(1)} %pad_maximum_fusion), channel_id=1, source_target_pairs={{0,1},{1,0},{2,3},{3,2},{4,5},{5,4},{6,7},{7,6},{8,9},{9,8},{10,11... | collective-permute-start | bytes 196616 | tf_op jit(solution)/shard_map/ppermute | solution.py:292
  8.0 9.1 %collective-permute-start.7 = (f32[256,128]{1,0:T(8,128)S(1)}, f32[256,128]{1,0:T(8,128)S(1)}, u32[]{:S(2)}, u32[]{:S(2)}) collective-permute-start(f32[256,128]{1,0:T(8,128)S(1)} %constant_dynamic-update-slice_fusion), channel_id=1, source_target_pairs={{27,0},{31,4},{28,1}} | collective-permute-start | bytes 393224 | tf_op jit(solution)/shard_map/ppermute | solution.py:307
  9.3 10.5 %collective-permute-start.5 = (f32[256,128]{1,0:T(8,128)S(1)}, f32[256,128]{1,0:T(8,128)S(1)}, u32[]{:S(2)}, u32[]{:S(2)}) collective-permute-start(f32[256,128]{1,0:T(8,128)S(1)} %constant_dynamic-update-slice_fusion), channel_id=1, source_target_pairs={{19,0},{23,4},{27,8},{31,12},{20,1},{24,5},{28,9}} | collective-permute-start | bytes 393224 | tf_op jit(solution)/shard_map/ppermute | solution.py:307
  10.6 9.5 %collective-permute-start.3 = (f32[256,128]{1,0:T(8,128)S(1)}, f32[256,128]{1,0:T(8,128)S(1)}, u32[]{:S(2)}, u32[]{:S(2)}) collective-permute-start(f32[256,128]{1,0:T(8,128)S(1)} %constant_dynamic-update-slice_fusion), channel_id=1, source_target_pairs={{11,0},{15,4},{19,8},{23,12},{27,16},{31,20},{12,1},{16,5},{20,9},... | collective-permute-start | bytes 393224 | tf_op jit(solution)/shard_map/ppermute | solution.py:307
  11.9 9.6 %collective-permute-start.2 = (f32[256,128]{1,0:T(8,128)S(1)}, f32[256,128]{1,0:T(8,128)S(1)}, u32[]{:S(2)}, u32[]{:S(2)}) collective-permute-start(f32[256,128]{1,0:T(8,128)S(1)} %constant_dynamic-update-slice_fusion), channel_id=1, source_target_pairs={{4,0},{8,4},{12,8},{16,12},{20,16},{24,20},{28,24}} | collective-permute-start | bytes 393224 | tf_op jit(solution)/shard_map/ppermute | solution.py:304
  17.1 4.4 %collective-permute-start.8 = (f32[256,128]{1,0:T(8,128)S(1)}, f32[256,128]{1,0:T(8,128)S(1)}, u32[]{:S(2)}, u32[]{:S(2)}) collective-permute-start(f32[256,128]{1,0:T(8,128)S(1)} %collective-permute-done.7), channel_id=1, source_target_pairs={{0,1},{1,0},{2,3},{3,2},{4,5},{5,4},{6,7},{7,6},{8,9},{9,8},{10,11... | collective-permute-start | bytes 393224 | tf_op jit(solution)/shard_map/ppermute | solution.py:292
  19.7 1.7 %collective-permute-start.6 = (f32[256,128]{1,0:T(8,128)S(1)}, f32[256,128]{1,0:T(8,128)S(1)}, u32[]{:S(2)}, u32[]{:S(2)}) collective-permute-start(f32[256,128]{1,0:T(8,128)S(1)} %collective-permute-done.5), channel_id=1, source_target_pairs={{0,1},{1,0},{2,3},{3,2},{4,5},{5,4},{6,7},{7,6},{8,9},{9,8},{10,11... | collective-permute-start | bytes 393224 | tf_op jit(solution)/shard_map/ppermute | solution.py:292
  20.0 1.5 %collective-permute-start.4 = (f32[256,128]{1,0:T(8,128)S(1)}, f32[256,128]{1,0:T(8,128)S(1)}, u32[]{:S(2)}, u32[]{:S(2)}) collective-permute-start(f32[256,128]{1,0:T(8,128)S(1)} %collective-permute-done.3), channel_id=1, source_target_pairs={{0,1},{1,0},{2,3},{3,2},{4,5},{5,4},{6,7},{7,6},{8,9},{9,8},{10,11... | collective-permute-start | bytes 393224 | tf_op jit(solution)/shard_map/ppermute | solution.py:292

commit v3 on v2

--- a/solution.py
+++ b/solution.py
@@ -1,4 +1,5 @@
 import functools
+import itertools
 import math
 
 import jax
@@ -147,13 +148,17 @@
     )(*[pltpu.with_memory_space_constraint(jnp.asarray(x), pltpu.HBM) for x in (alive, offset_limit, strain, table, twiddle)])
 
 
-def correlate_kernel(orders, wins, chans, share, lead_only, limit_ref, *refs):
+def correlate_kernel(orders, ahead, wins, chans, share, octets, has_tail, *refs):
     count = len(orders)
-    blocks = refs[:count]
-    high_ref, low_ref, out_ref = refs[count : count + 3]
-    own, partner, x_high, x_low, lagged, in_sem, out_sem = refs[count + 3 :]
+    limit_ref = refs[0]
+    blocks = refs[1 : count + 1]
+    high_ref, low_ref = refs[count + 1 : count + 3]
+    rest = refs[count + 3 :]
+    tail_ref = rest[0] if has_tail else None
+    out_ref, own, partner, x_high, x_low, lagged, in_sem, out_sem = rest[has_tail:]
     groups = own.shape[0]
-    octets = share // SUB
+    first_octet, last_octet = octets
+    size = (last_octet - first_octet) * SUB
     place = lax.axis_index("win")
 
     def load(index):
@@ -164,24 +169,36 @@
             copies.append(pltpu.make_async_copy(blocks[index].at[position], target, in_sem.at[index, position]))
         return copies
 
-    def store(first, rows, source):
-        return pltpu.make_async_copy(source, out_ref.at[pl.ds(first, rows)], out_sem.at[first // SUB])
+    def store(source, first, rows, which):
+        return pltpu.make_async_copy(source, out_ref.at[pl.ds(first, rows)], out_sem.at[which])
 
     def work():
-        copies = [copy for index in range(count) for copy in load(index)]
-        for copy in copies:
-            copy.start()
+        copies = [load(index) for index in range(count)]
+        for group in copies:
+            for copy in group:
+                copy.start()
+        stores = []
+        if has_tail:
+            stores.append(store(tail_ref, size, tail_ref.shape[0], octets[1]))
+            stores[0].start()
         limit = limit_ref[...]
         have = (count - 1) * chans
         total = partner.shape[3]
         if have < total:
             partner[:, :, :, have:, :] = jnp.zeros(partner.shape[:3] + (total - have, LANES), F32)
-        for copy in copies:
-            copy.wait()
+        for index, group in enumerate(copies):
+            for copy in group:
+                copy.wait()
+            if ahead is not None and index > 0 and ahead[index - 1] > 0:
+
+                def clear(first=(index - 1) * chans):
+                    partner[:, :, :, first : first + chans, :] = jnp.zeros(partner.shape[:3] + (chans, LANES), F32)
+
+                pl.when(lax.axis_index("chan") + ahead[index - 1] >= lax.axis_size("chan"))(clear)
         half = TILES // 2
 
-        def octet(g, carry):
-            first = pl.multiple_of(g * SUB, SUB)
+        def octet(g):
+            first = g * SUB
             sums = [[jnp.zeros((chans, LANES), F32) for _ in range(TILES)] for _ in range(SUB)]
             for group in range(groups):
                 for w in range(wins):
@@ -192,77 +209,80 @@
                             a_re, a_im, b_re, b_im = mine[t], mine[t + half], theirs[t], theirs[t + half]
                             sums[j][t] = sums[j][t] + (a_re * b_re + a_im * b_im)
                             sums[j][t + half] = sums[j][t + half] + (a_im * b_re - a_re * b_im)
-            offset = place * share + first
+            offset = place * share + first_octet * SUB + first
             for j in range(0, SUB, 2):
                 pair = []
                 for k in (j, j + 1):
                     keep = limit > offset + k
                     pair.append(jnp.concatenate([jnp.where(keep, value, 0.0) for value in sums[k]], axis=1))
                 high, low = halves(jnp.concatenate(pair, axis=0))
-                rows = pl.ds(pl.multiple_of((first + j) * chans, 2 * chans), 2 * chans)
+                rows = slice((first + j) * chans, (first + j + 2) * chans)
                 x_high[rows, :] = high
                 x_low[rows, :] = low
-            return carry
-
-        step = octets // 2
-        stores = []
-        for part in range(2):
-            lax.fori_loop(part * step, (part + 1) * step, octet, 0)
-            rows = slice(part * step * SUB * chans, (part + 1) * step * SUB * chans)
+
+        step = math.gcd(last_octet - first_octet, 4)
+        for part in range(0, last_octet - first_octet, step):
+            for g in range(part, part + step):
+                octet(g)
+            rows = slice(part * SUB * chans, (part + step) * SUB * chans)
             result = (
                 mm(x_high[rows, :], high_ref[...]) + mm(x_high[rows, :], low_ref[...]) + mm(x_low[rows, :], high_ref[...])
             )
-            lagged[part * step * SUB : (part + 1) * step * SUB] = result.reshape(step * SUB, chans, result.shape[1])
-            copy = store(part * step * SUB, step * SUB, lagged.at[pl.ds(part * step * SUB, step * SUB)])
+            lagged[part * SUB : (part + step) * SUB] = result.reshape(step * SUB, chans, result.shape[1])
+            copy = store(lagged.at[pl.ds(part * SUB, step * SUB)], part * SUB, step * SUB, part)
             copy.start()
             stores.append(copy)
         for copy in stores:
             copy.wait()
 
     def blank():
-        step = octets // 2 * SUB
-        lagged[:step] = jnp.zeros((step,) + lagged.shape[1:], F32)
-        stores = [store(part * step, step, lagged.at[pl.ds(0, step)]) for part in range(2)]
+        lagged[...] = jnp.zeros(lagged.shape, F32)
+        stores = [store(lagged, 0, size, 0)]
+        if has_tail:
+            stores.append(store(tail_ref, size, tail_ref.shape[0], octets[1]))
         for copy in stores:
             copy.start()
         for copy in stores:
             copy.wait()
 
-    if lead_only:
+    if ahead is None:
+        work()
+    else:
         pl.when(place == 0)(work)
         pl.when(place != 0)(blank)
-    else:
-        work()
-
-
-def correlate(blocks, orders, limit, wins, chans, share, samples, scale, lead_only):
+
+
+def correlate(blocks, orders, ahead, octets, tail, limit, wins, chans, share, samples, scale):
     high, low = inverse_tables(samples, scale)
     groups = len(orders[0])
     shape = (groups, TILES, wins, chans, LANES)
-    octets = share // SUB
-    rows = share * chans
+    size = (octets[1] - octets[0]) * SUB
+    rows = size * chans
     lags = 2 * MAXLAG
-    body = functools.partial(correlate_kernel, orders, wins, chans, share, lead_only)
+    tails = [] if tail is None else [tail]
+    body = functools.partial(correlate_kernel, orders, ahead, wins, chans, share, octets, len(tails))
+    whole = size + sum(t.shape[0] for t in tails)
     return pl.pallas_call(
         body,
-        out_shape=jax.ShapeDtypeStruct((share, chans, lags), F32),
+        out_shape=jax.ShapeDtypeStruct((whole, chans, lags), F32),
         in_specs=[pl.BlockSpec(memory_space=pltpu.VMEM)]
         + [pl.BlockSpec(memory_space=pl.ANY)] * len(blocks)
-        + [pl.BlockSpec(memory_space=pltpu.VMEM)] * 2,
+        + [pl.BlockSpec(memory_space=pltpu.VMEM)] * 2
+        + [pl.BlockSpec(memory_space=pl.ANY)] * len(tails),
         out_specs=pl.BlockSpec(memory_space=pl.ANY),
         scratch_shapes=[
             pltpu.VMEM(shape, F32),
-            pltpu.VMEM((groups, TILES, wins, share + SUB, LANES), F32),
+            pltpu.VMEM((groups, TILES, wins, size + SUB, LANES), F32),
             pltpu.VMEM((rows, 2 * NF), BF16),
             pltpu.VMEM((rows, 2 * NF), BF16),
-            pltpu.VMEM((share, chans, lags), F32),
+            pltpu.VMEM((size, chans, lags), F32),
             pltpu.SemaphoreType.DMA((len(blocks), groups)),
-            pltpu.SemaphoreType.DMA((octets,)),
+            pltpu.SemaphoreType.DMA((share // SUB + 1,)),
         ],
         compiler_params=pltpu.CompilerParams(vmem_limit_bytes=32 * MIB),
         cost_estimate=pl.CostEstimate(flops=6 * rows * 2 * NF * lags, bytes_accessed=4 * rows * lags, transcendentals=0),
         name="correlate",
-    )(limit, *[block.reshape(shape) for block in blocks], high, low)
+    )(limit, *[block.reshape(shape) for block in blocks], high, low, *tails)
 
 
 def local(strain, offset_limit, alive):
@@ -291,24 +311,50 @@
         pairs = [(device(c, w), device(c, w ^ mask)) for c in range(chan_count) for w in range(win_count)]
         return lax.ppermute(value, axes, pairs)
 
-    def ahead(steps, source, target):
-        return [(device(c + steps, source), device(c, target)) for c in range(chan_count - steps)]
+    def shift(wanted):
+        sources = [w for w in range(win_count) if w not in [source for _, source in wanted.values()]]
+        targets = [w for w in range(win_count) if w not in wanted]
+
+        def cost(order):
+            return sum(100 if s == t else (s ^ t) // 2 for s, t in zip(order, targets))
+
+        idle = dict(zip(targets, min(itertools.permutations(sources), key=cost)))
+        moves = {**wanted, **{target: (0, source) for target, source in idle.items()}}
+        return [
+            (device((c + steps) % chan_count, source), device(c, target))
+            for target, (steps, source) in moves.items()
+            for c in range(chan_count)
+        ]
 
     if win_count == 4 and chan_count * ch_dev <= share:
         block = white
         for mask in (2, 1):
             block = jnp.concatenate([block, exchange(block, mask)], axis=0)
         relative = (0, 2, 1, 3)
-        crossed = tuple(3 ^ r for r in relative)
+        flip = lambda source: tuple(source ^ r for r in relative)
         blocks, orders = {0: block}, {0: relative}
-        blocks[1], orders[1] = lax.ppermute(block, axes, ahead(1, 0, 0)), relative
         for even in range(2, chan_count, 2):
-            pairs = ahead(even, 3, 0) + ahead(even + 1, 0, 1)
-            blocks[even], orders[even] = lax.ppermute(block, axes, pairs), crossed
+            wanted = {0: (even, 3)}
             if even + 1 < chan_count:
-                blocks[even + 1], orders[even + 1] = exchange(blocks[even], 1), relative
-        near = range(chan_count)
-        return finish([block] + [blocks[d] for d in near], [relative] + [orders[d] for d in near], lead_only=True)
+                wanted[1] = (even + 1, 1)
+            blocks[even], orders[even] = lax.ppermute(block, axes, shift(wanted)), flip(3)
+            if even + 1 < chan_count:
+                blocks[even + 1], orders[even + 1] = exchange(blocks[even], 1), flip(1)
+        if chan_count > 1:
+            blocks[1], orders[1] = lax.ppermute(block, axes, shift({0: (1, 1)})), flip(1)
+
+        def part(octets, tail):
+            near = [d for d in range(octets[0], octets[1] + 1) if d < chan_count]
+            return finish(
+                [block] + [blocks[d] for d in near],
+                [relative] + [orders[d] for d in near],
+                near,
+                octets,
+                tail,
+            )
+
+        cut = min(4, reach)
+        return part((0, cut), part((cut, reach), None) if cut < reach else None)
 
     gathered = lax.all_gather(white, "win", tiled=True)
     order = tuple(range(win_count))
@@ -321,7 +367,7 @@
             if c + reach * w + steps < chan_count
         ]
         blocks.append(lax.ppermute(gathered, axes, pairs) if pairs else jnp.zeros_like(gathered))
-    return finish(blocks, [order] * len(blocks), lead_only=False)
+    return finish(blocks, [order] * len(blocks), None, (0, reach), None)
 
 
 def solution(mesh):

time: 26.1 us -> 28.2 us (1.080)
  starting transfers between devices: 8.84 us -> 11.9 us
  waiting for transfers between devices: 10.8 us -> 9.79 us
    ppermute x5, starting transfers between devices: 3.68 us -> 7.8 us  [exchange(): return lax.ppermute(value, axes, pairs)]
    ppermute x4, starting transfers between devices: 5.16 us -> 4.13 us  [the longest x3 3.68 us: local(): lax.ppermute(block, axes, shift(wanted))]
    ppermute x4, waiting for transfers between devices: 7.66 us -> 6.66 us  [the longest x3 6.65 us: local(): lax.ppermute(block, axes, shift(wanted))]
    pallas_call x1 -> x2, Pallas kernels: 4.37 us -> 4.49 us  [correlate(): pl.pallas_call(body, out_shape=jax.ShapeDtypeStruct((whole, chans, lags),...]
  transfers between devices with their start and end apart: 9 -> 9, of which waited for: 5 -> 4; matrix products, arithmetic and copies ran while one was open for 0% -> 0% of each run, Pallas kernels for 0% -> 7%
where the time goes in v3:
time: 28.2 us; the launch traced here: 28.1 us
  starting transfers between devices  11.9 us (42%)
  waiting for transfers between devices  9.79 us (35%)
  Pallas kernels  6.27 us (22%)
    ppermute x5, starting transfers between devices, exchange(): return lax.ppermute(value, axes, pairs)  7.8 us
    ppermute x3, waiting for transfers between devices, local(): lax.ppermute(block, axes, shift(wanted))  6.65 us
    pallas_call x2, Pallas kernels, correlate(): pl.pallas_call(body, out_shape=jax.ShapeDtypeStruct((whole, chans, lags),...  4.49 us
    ppermute x3, starting transfers between devices, local(): lax.ppermute(block, axes, shift(wanted))  3.68 us
    ppermute x5, waiting for transfers between devices, exchange(): return lax.ppermute(value, axes, pairs)  3.13 us
    pallas_call x1, Pallas kernels, whiten(): pl.pallas_call(whiten_kernel, out_shape=(jax.ShapeDtypeStruct((TILES * ro...  1.78 us
  transfers between devices with their start and end apart: 9, of which 4 were waited for; matrix products, arithmetic and copies ran while one was open for 0% of the time, Pallas kernels for 7%

profile of v3, /device:TPU:0, one launch (start us, length us, event | category | flops | bytes accessed | tf_op | source)
XLA Modules:
  0.0 28.1 jit_solution(14423550539813223054)
XLA Ops:
  0.0 0.0 copy-start
  0.0 0.0 copy-start.1
  0.0 1.8 %whiten.1 = (f32[64,128]{1,0:T(8,128)S(1)}, s32[8,128]{1,0:T(8,128)S(1)}) custom-call(s32[8]{0:T(128)} %alive_hbm.1, s32[8]{0:T(128)} %limit_hbm.1, f32[2,8,4096]{2,1,0:T(8,128)} %strain_hbm.1, bf16[512,512]{1,0:T(8,128)(2,1)} %constant.8.clone.table_hbm, f32[16,512]{1,0:T(8,128)} %constant.9.clone.twiddle_hbm), custom_call_target="tpu_custom_call" | custom-call | flops 201326592 | bytes 262144 | tf_op jit(solution)/shard_map/whiten/pallas_call | solution.py:129
  1.8 3.0 %collective-permute-start = (f32[64,128]{1,0:T(8,128)S(1)}, f32[64,128]{1,0:T(8,128)S(1)}, u32[]{:S(2)}, u32[]{:S(2)}) collective-permute-start(f32[64,128]{1,0:T(8,128)S(1)} %get-tuple-element.8), channel_id=1, source_target_pairs={{0,2},{1,3},{2,0},{3,1},{4,6},{5,7},{6,4},{7,5},{8,10},{9,11},{10,... | collective-permute-start | bytes 98312 | tf_op jit(solution)/shard_map/ppermute | solution.py:312
  4.8 1.9 %collective-permute-done = f32[64,128]{1,0:T(8,128)S(1)} collective-permute-done((f32[64,128]{1,0:T(8,128)S(1)}, f32[64,128]{1,0:T(8,128)S(1)}, u32[]{:S(2)}, u32[]{:S(2)}) %collective-permute-start) | collective-permute-done | bytes 32800 | tf_op jit(solution)/shard_map/ppermute | solution.py:312
  6.7 0.0 collective-permute-start.1
  6.7 1.2 %collective-permute-done.1 = f32[128,128]{1,0:T(8,128)S(1)} collective-permute-done((f32[128,128]{1,0:T(8,128)S(1)}, f32[128,128]{1,0:T(8,128)S(1)}, u32[]{:S(2)}, u32[]{:S(2)}) %collective-permute-start.1) | collective-permute-done | bytes 65568 | tf_op jit(solution)/shard_map/ppermute | solution.py:312
  8.0 2.0 %collective-permute-start.7 = (f32[256,128]{1,0:T(8,128)S(1)}, f32[256,128]{1,0:T(8,128)S(1)}, u32[]{:S(2)}, u32[]{:S(2)}) collective-permute-start(f32[256,128]{1,0:T(8,128)S(1)} %constant_dynamic-update-slice_fusion), channel_id=1, source_target_pairs={{27,0},{31,4},{3,8},{7,12},{11,16},{15,20},{19,24},{23,28},{29,1},... | collective-permute-start | bytes 393224 | tf_op jit(solution)/shard_map/ppermute | solution.py:340
  10.0 0.2 collective-permute-start.5
  10.1 1.5 %collective-permute-start.3 = (f32[256,128]{1,0:T(8,128)S(1)}, f32[256,128]{1,0:T(8,128)S(1)}, u32[]{:S(2)}, u32[]{:S(2)}) collective-permute-start(f32[256,128]{1,0:T(8,128)S(1)} %constant_dynamic-update-slice_fusion), channel_id=1, source_target_pairs={{11,0},{15,4},{19,8},{23,12},{27,16},{31,20},{3,24},{7,28},{13,1},... | collective-permute-start | bytes 393224 | tf_op jit(solution)/shard_map/ppermute | solution.py:340
  11.6 3.9 %collective-permute-done.7 = f32[256,128]{1,0:T(8,128)S(1)} collective-permute-done((f32[256,128]{1,0:T(8,128)S(1)}, f32[256,128]{1,0:T(8,128)S(1)}, u32[]{:S(2)}, u32[]{:S(2)}) %collective-permute-start.7) | collective-permute-done | bytes 131104 | tf_op jit(solution)/shard_map/ppermute | solution.py:340
  15.5 0.0 collective-permute-start.8
  15.6 2.8 %collective-permute-done.5 = f32[256,128]{1,0:T(8,128)S(1)} collective-permute-done((f32[256,128]{1,0:T(8,128)S(1)}, f32[256,128]{1,0:T(8,128)S(1)}, u32[]{:S(2)}, u32[]{:S(2)}) %collective-permute-start.5) | collective-permute-done | bytes 131104 | tf_op jit(solution)/shard_map/ppermute | solution.py:340
  18.3 0.1 collective-permute-start.6
  18.4 0.5 %collective-permute-start.2 = (f32[256,128]{1,0:T(8,128)S(1)}, f32[256,128]{1,0:T(8,128)S(1)}, u32[]{:S(2)}, u32[]{:S(2)}) collective-permute-start(f32[256,128]{1,0:T(8,128)S(1)} %constant_dynamic-update-slice_fusion), channel_id=1, source_target_pairs={{5,0},{9,4},{13,8},{17,12},{21,16},{25,20},{29,24},{1,28},{0,1},{4... | collective-permute-start | bytes 393224 | tf_op jit(solution)/shard_map/ppermute | solution.py:344
  18.9 0.0 collective-permute-done.3
  18.9 4.7 %collective-permute-start.4 = (f32[256,128]{1,0:T(8,128)S(1)}, f32[256,128]{1,0:T(8,128)S(1)}, u32[]{:S(2)}, u32[]{:S(2)}) collective-permute-start(f32[256,128]{1,0:T(8,128)S(1)} %collective-permute-done.3), channel_id=1, source_target_pairs={{0,1},{1,0},{2,3},{3,2},{4,5},{5,4},{6,7},{7,6},{8,9},{9,8},{10,11... | collective-permute-start | bytes 393224 | tf_op jit(solution)/shard_map/ppermute | solution.py:312
  23.6 0.0 collective-permute-done.8
  23.6 0.0 collective-permute-done.6
  23.6 0.0 copy-done
  23.6 0.0 copy-done.1
  23.6 1.8 %correlate.2.refs_9_ = f32[32,8,400]{2,1,0:T(8,128)S(1)} custom-call(s32[8,128]{1,0:T(8,128)S(1)} %get-tuple-element.7.refs_0_, f32[4,4,2,8,128]{4,3,2,1,0:T(8,128)S(1)} %bitcast.8, f32[4,4,2,8,128]{4,3,2,1,0:T(8,128)S(1)} %bitcast.11, f32[4,4,2,8,128]{4,3,2,1,0:T(8,128)S(1)} %bitcast.15, f32[4,4,2,8,128]{4,3,2,1,0:T(8,128)S(1)} %bitcast.13, ...), custom_call_target="tpu_custom_call" | custom-call | flops 314572800 | bytes 409600 | tf_op jit(solution)/shard_map/correlate/pallas_call | solution.py:265
  25.4 0.0 collective-permute-done.2
  25.4 0.0 collective-permute-done.4
  25.4 2.6 %correlate.3 = f32[64,8,400]{2,1,0:T(8,128)} custom-call(s32[8,128]{1,0:T(8,128)S(1)} %get-tuple-element.7.refs_0_, f32[4,4,2,8,128]{4,3,2,1,0:T(8,128)S(1)} %bitcast.9, f32[4,4,2,8,128]{4,3,2,1,0:T(8,128)S(1)} %bitcast.10, f32[4,4,2,8,128]{4,3,2,1,0:T(8,128)S(1)} %bitcast.17, f32[4,4,2,8,128]{4,3,2,1,0:T(8,128)S(1)} %bitcast.16, ...), custom_call_target="tpu_custom_call" | custom-call | flops 314572800 | bytes 409600 | tf_op jit(solution)/shard_map/correlate/pallas_call | solution.py:265
  (4 shorter events, 0.0 us)
Async XLA Ops:
  0.0 23.6 %copy-start = (bf16[512,400]{1,0:T(8,128)(2,1)S(1)}, bf16[512,400]{1,0:T(8,128)(2,1)}, u32[]{:S(2)}) copy-start(bf16[512,400]{1,0:T(8,128)(2,1)} %constant.11.clone.refs_7_.refs_8_) | copy-start | bytes 1228804
  0.0 23.6 %copy-start.1 = (bf16[512,400]{1,0:T(8,128)(2,1)S(1)}, bf16[512,400]{1,0:T(8,128)(2,1)}, u32[]{:S(2)}) copy-start(bf16[512,400]{1,0:T(8,128)(2,1)} %constant.10.clone.refs_6_.refs_7_) | copy-start | bytes 1228804
  1.8 4.9 %collective-permute-start = (f32[64,128]{1,0:T(8,128)S(1)}, f32[64,128]{1,0:T(8,128)S(1)}, u32[]{:S(2)}, u32[]{:S(2)}) collective-permute-start(f32[64,128]{1,0:T(8,128)S(1)} %get-tuple-element.8), channel_id=1, source_target_pairs={{0,2},{1,3},{2,0},{3,1},{4,6},{5,7},{6,4},{7,5},{8,10},{9,11},{10,... | collective-permute-start | bytes 98312 | tf_op jit(solution)/shard_map/ppermute | solution.py:312
  6.7 1.3 %collective-permute-start.1 = (f32[128,128]{1,0:T(8,128)S(1)}, f32[128,128]{1,0:T(8,128)S(1)}, u32[]{:S(2)}, u32[]{:S(2)}) collective-permute-start(f32[128,128]{1,0:T(8,128)S(1)} %pad_maximum_fusion), channel_id=1, source_target_pairs={{0,1},{1,0},{2,3},{3,2},{4,5},{5,4},{6,7},{7,6},{8,9},{9,8},{10,11... | collective-permute-start | bytes 196616 | tf_op jit(solution)/shard_map/ppermute | solution.py:312
  8.0 7.5 %collective-permute-start.7 = (f32[256,128]{1,0:T(8,128)S(1)}, f32[256,128]{1,0:T(8,128)S(1)}, u32[]{:S(2)}, u32[]{:S(2)}) collective-permute-start(f32[256,128]{1,0:T(8,128)S(1)} %constant_dynamic-update-slice_fusion), channel_id=1, source_target_pairs={{27,0},{31,4},{3,8},{7,12},{11,16},{15,20},{19,24},{23,28},{29,1},... | collective-permute-start | bytes 393224 | tf_op jit(solution)/shard_map/ppermute | solution.py:340
  10.0 8.4 %collective-permute-start.5 = (f32[256,128]{1,0:T(8,128)S(1)}, f32[256,128]{1,0:T(8,128)S(1)}, u32[]{:S(2)}, u32[]{:S(2)}) collective-permute-start(f32[256,128]{1,0:T(8,128)S(1)} %constant_dynamic-update-slice_fusion), channel_id=1, source_target_pairs={{19,0},{23,4},{27,8},{31,12},{3,16},{7,20},{11,24},{15,28},{21,1},... | collective-permute-start | bytes 393224 | tf_op jit(solution)/shard_map/ppermute | solution.py:340
  10.1 8.7 %collective-permute-start.3 = (f32[256,128]{1,0:T(8,128)S(1)}, f32[256,128]{1,0:T(8,128)S(1)}, u32[]{:S(2)}, u32[]{:S(2)}) collective-permute-start(f32[256,128]{1,0:T(8,128)S(1)} %constant_dynamic-update-slice_fusion), channel_id=1, source_target_pairs={{11,0},{15,4},{19,8},{23,12},{27,16},{31,20},{3,24},{7,28},{13,1},... | collective-permute-start | bytes 393224 | tf_op jit(solution)/shard_map/ppermute | solution.py:340
  15.5 8.0 %collective-permute-start.8 = (f32[256,128]{1,0:T(8,128)S(1)}, f32[256,128]{1,0:T(8,128)S(1)}, u32[]{:S(2)}, u32[]{:S(2)}) collective-permute-start(f32[256,128]{1,0:T(8,128)S(1)} %collective-permute-done.7), channel_id=1, source_target_pairs={{0,1},{1,0},{2,3},{3,2},{4,5},{5,4},{6,7},{7,6},{8,9},{9,8},{10,11... | collective-permute-start | bytes 393224 | tf_op jit(solution)/shard_map/ppermute | solution.py:312
  18.3 5.2 %collective-permute-start.6 = (f32[256,128]{1,0:T(8,128)S(1)}, f32[256,128]{1,0:T(8,128)S(1)}, u32[]{:S(2)}, u32[]{:S(2)}) collective-permute-start(f32[256,128]{1,0:T(8,128)S(1)} %collective-permute-done.5), channel_id=1, source_target_pairs={{0,1},{1,0},{2,3},{3,2},{4,5},{5,4},{6,7},{7,6},{8,9},{9,8},{10,11... | collective-permute-start | bytes 393224 | tf_op jit(solution)/shard_map/ppermute | solution.py:312
  18.4 7.0 %collective-permute-start.2 = (f32[256,128]{1,0:T(8,128)S(1)}, f32[256,128]{1,0:T(8,128)S(1)}, u32[]{:S(2)}, u32[]{:S(2)}) collective-permute-start(f32[256,128]{1,0:T(8,128)S(1)} %constant_dynamic-update-slice_fusion), channel_id=1, source_target_pairs={{5,0},{9,4},{13,8},{17,12},{21,16},{25,20},{29,24},{1,28},{0,1},{4... | collective-permute-start | bytes 393224 | tf_op jit(solution)/shard_map/ppermute | solution.py:344
  18.9 6.6 %collective-permute-start.4 = (f32[256,128]{1,0:T(8,128)S(1)}, f32[256,128]{1,0:T(8,128)S(1)}, u32[]{:S(2)}, u32[]{:S(2)}) collective-permute-start(f32[256,128]{1,0:T(8,128)S(1)} %collective-permute-done.3), channel_id=1, source_target_pairs={{0,1},{1,0},{2,3},{3,2},{4,5},{5,4},{6,7},{7,6},{8,9},{9,8},{10,11... | collective-permute-start | bytes 393224 | tf_op jit(solution)/shard_map/ppermute | solution.py:312

commit v4 on v3

--- a/solution.py
+++ b/solution.py
@@ -148,141 +148,135 @@
     )(*[pltpu.with_memory_space_constraint(jnp.asarray(x), pltpu.HBM) for x in (alive, offset_limit, strain, table, twiddle)])
 
 
-def correlate_kernel(orders, ahead, wins, chans, share, octets, has_tail, *refs):
+def runs(octets):
+    found = []
+    for index, octet in enumerate(octets):
+        if found and found[-1][1] + found[-1][2] == octet:
+            found[-1][2] += 1
+        else:
+            found.append([index, octet, 1])
+    return found
+
+
+def correlate_kernel(orders, needed, octets, early, wins, chans, share, lead, *refs):
     count = len(orders)
     limit_ref = refs[0]
     blocks = refs[1 : count + 1]
     high_ref, low_ref = refs[count + 1 : count + 3]
     rest = refs[count + 3 :]
-    tail_ref = rest[0] if has_tail else None
-    out_ref, own, partner, x_high, x_low, lagged, in_sem, out_sem = rest[has_tail:]
-    groups = own.shape[0]
-    first_octet, last_octet = octets
-    size = (last_octet - first_octet) * SUB
+    early_ref = rest[0] if early else None
+    out_ref, partner, x_high, x_low, lagged, out_sem, early_sem = rest[1 if early else 0 :]
+    groups = partner.shape[0]
     place = lax.axis_index("win")
 
-    def load(index):
-        copies = []
-        for position in range(groups):
-            group = orders[index][position]
-            target = own.at[group] if index == 0 else partner.at[group, :, :, pl.ds((index - 1) * chans, chans), :]
-            copies.append(pltpu.make_async_copy(blocks[index].at[position], target, in_sem.at[index, position]))
-        return copies
-
-    def store(source, first, rows, which):
-        return pltpu.make_async_copy(source, out_ref.at[pl.ds(first, rows)], out_sem.at[which])
+    def out_rows(first, length):
+        return out_ref.at[pl.ds(first * SUB, length * SUB)]
+
+    def early_stores():
+        return [
+            pltpu.make_async_copy(early_ref.at[pl.ds(at * SUB, length * SUB)], out_rows(octet, length), early_sem.at[at])
+            for at, octet, length in runs(early)
+        ]
+
+    def stores():
+        places = runs(octets) if early else [(0, 0, len(octets))]
+        return [
+            pltpu.make_async_copy(lagged.at[pl.ds(at * SUB, length * SUB)], out_rows(octet, length), out_sem.at[at])
+            for at, octet, length in places
+        ]
 
     def work():
-        copies = [load(index) for index in range(count)]
-        for group in copies:
-            for copy in group:
-                copy.start()
-        stores = []
-        if has_tail:
-            stores.append(store(tail_ref, size, tail_ref.shape[0], octets[1]))
-            stores[0].start()
+        for copy in early_stores():
+            copy.start()
         limit = limit_ref[...]
-        have = (count - 1) * chans
-        total = partner.shape[3]
-        if have < total:
-            partner[:, :, :, have:, :] = jnp.zeros(partner.shape[:3] + (total - have, LANES), F32)
-        for index, group in enumerate(copies):
-            for copy in group:
-                copy.wait()
-            if ahead is not None and index > 0 and ahead[index - 1] > 0:
-
-                def clear(first=(index - 1) * chans):
-                    partner[:, :, :, first : first + chans, :] = jnp.zeros(partner.shape[:3] + (chans, LANES), F32)
-
-                pl.when(lax.axis_index("chan") + ahead[index - 1] >= lax.axis_size("chan"))(clear)
+        chan, chan_count = lax.axis_index("chan"), lax.axis_size("chan")
+        for index, steps in enumerate(needed):
+            rows = slice(index * chans, (index + 1) * chans)
+            if index + 1 >= count:
+                partner[:, :, :, rows, :] = jnp.zeros(partner.shape[:3] + (chans, LANES), F32)
+                continue
+            for position in range(groups):
+                value = blocks[index + 1][position]
+                if lead and steps > 0:
+                    value = jnp.where(chan + steps < chan_count, value, 0.0)
+                partner[orders[index + 1][position], :, :, rows, :] = value
+        own = {orders[0][position]: blocks[0].at[position] for position in range(groups)}
         half = TILES // 2
-
-        def octet(g):
-            first = g * SUB
+        for at, octet in enumerate(octets):
+            first = needed.index(octet) * SUB
             sums = [[jnp.zeros((chans, LANES), F32) for _ in range(TILES)] for _ in range(SUB)]
             for group in range(groups):
                 for w in range(wins):
-                    mine = [own[group, t, w] for t in range(TILES)]
+                    mine = [own[group][t, w] for t in range(TILES)]
                     for j in range(SUB):
                         theirs = [partner[group, t, w, pl.ds(first + j + 1, SUB), :] for t in range(TILES)]
                         for t in range(half):
                             a_re, a_im, b_re, b_im = mine[t], mine[t + half], theirs[t], theirs[t + half]
                             sums[j][t] = sums[j][t] + (a_re * b_re + a_im * b_im)
                             sums[j][t + half] = sums[j][t + half] + (a_im * b_re - a_re * b_im)
-            offset = place * share + first_octet * SUB + first
+            offset = place * share + octet * SUB
             for j in range(0, SUB, 2):
                 pair = []
                 for k in (j, j + 1):
                     keep = limit > offset + k
                     pair.append(jnp.concatenate([jnp.where(keep, value, 0.0) for value in sums[k]], axis=1))
                 high, low = halves(jnp.concatenate(pair, axis=0))
-                rows = slice((first + j) * chans, (first + j + 2) * chans)
+                rows = slice((at * SUB + j) * chans, (at * SUB + j + 2) * chans)
                 x_high[rows, :] = high
                 x_low[rows, :] = low
-
-        step = math.gcd(last_octet - first_octet, 4)
-        for part in range(0, last_octet - first_octet, step):
-            for g in range(part, part + step):
-                octet(g)
-            rows = slice(part * SUB * chans, (part + step) * SUB * chans)
-            result = (
-                mm(x_high[rows, :], high_ref[...]) + mm(x_high[rows, :], low_ref[...]) + mm(x_low[rows, :], high_ref[...])
-            )
-            lagged[part * SUB : (part + step) * SUB] = result.reshape(step * SUB, chans, result.shape[1])
-            copy = store(lagged.at[pl.ds(part * SUB, step * SUB)], part * SUB, step * SUB, part)
+        result = mm(x_high[...], high_ref[...]) + mm(x_high[...], low_ref[...]) + mm(x_low[...], high_ref[...])
+        lagged[...] = result.reshape(lagged.shape)
+        for copy in stores():
             copy.start()
-            stores.append(copy)
-        for copy in stores:
+        for copy in early_stores() + stores():
             copy.wait()
 
     def blank():
         lagged[...] = jnp.zeros(lagged.shape, F32)
-        stores = [store(lagged, 0, size, 0)]
-        if has_tail:
-            stores.append(store(tail_ref, size, tail_ref.shape[0], octets[1]))
-        for copy in stores:
+        for copy in early_stores() + stores():
             copy.start()
-        for copy in stores:
+        for copy in early_stores() + stores():
             copy.wait()
 
-    if ahead is None:
-        work()
-    else:
+    if lead:
         pl.when(place == 0)(work)
         pl.when(place != 0)(blank)
-
-
-def correlate(blocks, orders, ahead, octets, tail, limit, wins, chans, share, samples, scale):
+    else:
+        work()
+
+
+def correlate(own, partners, octets, early, limit, wins, chans, share, samples, scale, lead):
     high, low = inverse_tables(samples, scale)
+    needed = sorted({octet + step for octet in octets for step in (0, 1)})
+    given = [own] + [partners[d] for d in needed if d in partners]
+    orders = tuple(order for _, order in given)
     groups = len(orders[0])
     shape = (groups, TILES, wins, chans, LANES)
-    size = (octets[1] - octets[0]) * SUB
+    size = len(octets) * SUB
     rows = size * chans
     lags = 2 * MAXLAG
-    tails = [] if tail is None else [tail]
-    body = functools.partial(correlate_kernel, orders, ahead, wins, chans, share, octets, len(tails))
-    whole = size + sum(t.shape[0] for t in tails)
+    early_octets, early_result = early if early else ((), None)
+    body = functools.partial(correlate_kernel, orders, needed, octets, early_octets, wins, chans, share, lead)
     return pl.pallas_call(
         body,
-        out_shape=jax.ShapeDtypeStruct((whole, chans, lags), F32),
+        out_shape=jax.ShapeDtypeStruct((size + len(early_octets) * SUB, chans, lags), F32),
         in_specs=[pl.BlockSpec(memory_space=pltpu.VMEM)]
-        + [pl.BlockSpec(memory_space=pl.ANY)] * len(blocks)
+        + [pl.BlockSpec(memory_space=pltpu.VMEM)] * len(given)
         + [pl.BlockSpec(memory_space=pltpu.VMEM)] * 2
-        + [pl.BlockSpec(memory_space=pl.ANY)] * len(tails),
+        + [pl.BlockSpec(memory_space=pl.ANY)] * bool(early),
         out_specs=pl.BlockSpec(memory_space=pl.ANY),
         scratch_shapes=[
-            pltpu.VMEM(shape, F32),
-            pltpu.VMEM((groups, TILES, wins, size + SUB, LANES), F32),
+            pltpu.VMEM((groups, TILES, wins, len(needed) * SUB, LANES), F32),
             pltpu.VMEM((rows, 2 * NF), BF16),
             pltpu.VMEM((rows, 2 * NF), BF16),
             pltpu.VMEM((size, chans, lags), F32),
-            pltpu.SemaphoreType.DMA((len(blocks), groups)),
-            pltpu.SemaphoreType.DMA((share // SUB + 1,)),
+            pltpu.SemaphoreType.DMA((len(octets),)),
+            pltpu.SemaphoreType.DMA((max(1, len(early_octets)),)),
         ],
         compiler_params=pltpu.CompilerParams(vmem_limit_bytes=32 * MIB),
         cost_estimate=pl.CostEstimate(flops=6 * rows * 2 * NF * lags, bytes_accessed=4 * rows * lags, transcendentals=0),
         name="correlate",
-    )(limit, *[block.reshape(shape) for block in blocks], high, low, *tails)
+    )(limit, *[block.reshape(shape) for block, _ in given], high, low, *([early_result] if early else []))
 
 
 def local(strain, offset_limit, alive):
@@ -330,35 +324,26 @@
         block = white
         for mask in (2, 1):
             block = jnp.concatenate([block, exchange(block, mask)], axis=0)
-        relative = (0, 2, 1, 3)
-        flip = lambda source: tuple(source ^ r for r in relative)
-        blocks, orders = {0: block}, {0: relative}
+
+        def order(source):
+            return tuple(source ^ r for r in (0, 2, 1, 3))
+
+        partners = {0: (block, order(0))}
         for even in range(2, chan_count, 2):
             wanted = {0: (even, 3)}
             if even + 1 < chan_count:
                 wanted[1] = (even + 1, 1)
-            blocks[even], orders[even] = lax.ppermute(block, axes, shift(wanted)), flip(3)
+            got = lax.ppermute(block, axes, shift(wanted))
+            partners[even] = got, order(3)
             if even + 1 < chan_count:
-                blocks[even + 1], orders[even + 1] = exchange(blocks[even], 1), flip(1)
+                partners[even + 1] = exchange(got, 1), order(1)
         if chan_count > 1:
-            blocks[1], orders[1] = lax.ppermute(block, axes, shift({0: (1, 1)})), flip(1)
-
-        def part(octets, tail):
-            near = [d for d in range(octets[0], octets[1] + 1) if d < chan_count]
-            return finish(
-                [block] + [blocks[d] for d in near],
-                [relative] + [orders[d] for d in near],
-                near,
-                octets,
-                tail,
-            )
-
-        cut = min(4, reach)
-        return part((0, cut), part((cut, reach), None) if cut < reach else None)
+            partners[1] = lax.ppermute(block, axes, shift({0: (1, 1)})), order(1)
+        return finish(partners[0], partners, list(range(reach)), None, lead=True)
 
     gathered = lax.all_gather(white, "win", tiled=True)
     order = tuple(range(win_count))
-    blocks = [gathered]
+    partners = {}
     for steps in range(reach + 1):
         pairs = [
             (device(c + reach * w + steps, w), device(c, w))
@@ -366,8 +351,9 @@
             for c in range(chan_count)
             if c + reach * w + steps < chan_count
         ]
-        blocks.append(lax.ppermute(gathered, axes, pairs) if pairs else jnp.zeros_like(gathered))
-    return finish(blocks, [order] * len(blocks), None, (0, reach), None)
+        if pairs:
+            partners[steps] = lax.ppermute(gathered, axes, pairs), order
+    return finish((gathered, order), partners, list(range(reach)), None, lead=False)
 
 
 def solution(mesh):

time: 28.2 us -> 23.3 us (0.83)
  starting transfers between devices: 11.9 us -> 8.69 us
  Pallas kernels: 6.27 us -> 5.04 us
  waiting for transfers between devices: 9.79 us -> 9.35 us
    ppermute x5, starting transfers between devices: 7.8 us -> 3.5 us  [exchange(): return lax.ppermute(value, axes, pairs)]
    pallas_call x2 -> x1, Pallas kernels: 4.49 us -> 3.25 us  [correlate(): pl.pallas_call(body, out_shape=jax.ShapeDtypeStruct((size + len(early_oct...]
    ppermute x4, starting transfers between devices: 4.13 us -> 5.19 us  [the longest x3 3.68 us: local(): got = lax.ppermute(block, axes, shift(wanted))]
    ppermute x4, waiting for transfers between devices: 6.66 us -> 6.1 us  [the longest x3 5.21 us: local(): got = lax.ppermute(block, axes, shift(wanted))]
  transfers between devices with their start and end apart: 9 -> 9, of which waited for: 4 -> 7; matrix products, arithmetic and copies ran while one was open for 0% -> 0% of each run, Pallas kernels for 7% -> 0%
where the time goes in v4:
time: 23.3 us; the launch traced here: 23.1 us
  waiting for transfers between devices  9.35 us (40%)
  starting transfers between devices  8.69 us (37%)
  Pallas kernels  5.04 us (22%)
    ppermute x3, waiting for transfers between devices, local(): got = lax.ppermute(block, axes, shift(wanted))  5.21 us
    ppermute x3, starting transfers between devices, local(): got = lax.ppermute(block, axes, shift(wanted))  3.68 us
    ppermute x5, starting transfers between devices, exchange(): return lax.ppermute(value, axes, pairs)  3.5 us
    ppermute x5, waiting for transfers between devices, exchange(): return lax.ppermute(value, axes, pairs)  3.25 us
    pallas_call x1, Pallas kernels, correlate(): pl.pallas_call(body, out_shape=jax.ShapeDtypeStruct((size + len(early_oct...  3.25 us
    pallas_call x1, Pallas kernels, whiten(): pl.pallas_call(whiten_kernel, out_shape=(jax.ShapeDtypeStruct((TILES * ro...  1.78 us
    ppermute x1, starting transfers between devices, local(): partners[1] = (lax.ppermute(block, axes, shift({0: (1, 1)})), order(1))  1.51 us
    ppermute x1, waiting for transfers between devices, local(): partners[1] = (lax.ppermute(block, axes, shift({0: (1, 1)})), order(1))  0.89 us
  transfers between devices with their start and end apart: 9, of which 7 were waited for; matrix products, arithmetic and copies ran while one was open for 0% of the time, Pallas kernels for 0%

profile of v4, /device:TPU:0, one launch (start us, length us, event | category | flops | bytes accessed | tf_op | source)
XLA Modules:
  0.0 23.1 jit_solution(2224721307022676112)
XLA Ops:
  0.0 0.0 copy-start
  0.0 0.0 copy-start.1
  0.0 1.8 %whiten.1 = (f32[64,128]{1,0:T(8,128)S(1)}, s32[8,128]{1,0:T(8,128)S(1)}) custom-call(s32[8]{0:T(128)} %alive_hbm.1, s32[8]{0:T(128)} %limit_hbm.1, f32[2,8,4096]{2,1,0:T(8,128)} %strain_hbm.1, bf16[512,512]{1,0:T(8,128)(2,1)} %constant.8.clone.table_hbm, f32[16,512]{1,0:T(8,128)} %constant.9.clone.twiddle_hbm), custom_call_target="tpu_custom_call" | custom-call | flops 201326592 | bytes 262144 | tf_op jit(solution)/shard_map/whiten/pallas_call | solution.py:129
  1.8 3.0 %collective-permute-start = (f32[64,128]{1,0:T(8,128)S(1)}, f32[64,128]{1,0:T(8,128)S(1)}, u32[]{:S(2)}, u32[]{:S(2)}) collective-permute-start(f32[64,128]{1,0:T(8,128)S(1)} %get-tuple-element.8), channel_id=1, source_target_pairs={{0,2},{1,3},{2,0},{3,1},{4,6},{5,7},{6,4},{7,5},{8,10},{9,11},{10,... | collective-permute-start | bytes 98312 | tf_op jit(solution)/shard_map/ppermute | solution.py:306
  4.8 1.9 %collective-permute-done = f32[64,128]{1,0:T(8,128)S(1)} collective-permute-done((f32[64,128]{1,0:T(8,128)S(1)}, f32[64,128]{1,0:T(8,128)S(1)}, u32[]{:S(2)}, u32[]{:S(2)}) %collective-permute-start) | collective-permute-done | bytes 32800 | tf_op jit(solution)/shard_map/ppermute | solution.py:306
  6.7 0.0 collective-permute-start.1
  6.7 1.2 %collective-permute-done.1 = f32[128,128]{1,0:T(8,128)S(1)} collective-permute-done((f32[128,128]{1,0:T(8,128)S(1)}, f32[128,128]{1,0:T(8,128)S(1)}, u32[]{:S(2)}, u32[]{:S(2)}) %collective-permute-start.1) | collective-permute-done | bytes 65568 | tf_op jit(solution)/shard_map/ppermute | solution.py:306
  8.0 2.0 %collective-permute-start.7 = (f32[256,128]{1,0:T(8,128)S(1)}, f32[256,128]{1,0:T(8,128)S(1)}, u32[]{:S(2)}, u32[]{:S(2)}) collective-permute-start(f32[256,128]{1,0:T(8,128)S(1)} %constant_dynamic-update-slice_fusion), channel_id=1, source_target_pairs={{27,0},{31,4},{3,8},{7,12},{11,16},{15,20},{19,24},{23,28},{29,1},... | collective-permute-start | bytes 393224 | tf_op jit(solution)/shard_map/ppermute | solution.py:336
  10.0 0.2 collective-permute-start.5
  10.1 1.5 %collective-permute-start.3 = (f32[256,128]{1,0:T(8,128)S(1)}, f32[256,128]{1,0:T(8,128)S(1)}, u32[]{:S(2)}, u32[]{:S(2)}) collective-permute-start(f32[256,128]{1,0:T(8,128)S(1)} %constant_dynamic-update-slice_fusion), channel_id=1, source_target_pairs={{11,0},{15,4},{19,8},{23,12},{27,16},{31,20},{3,24},{7,28},{13,1},... | collective-permute-start | bytes 393224 | tf_op jit(solution)/shard_map/ppermute | solution.py:336
  11.6 1.5 %collective-permute-start.2 = (f32[256,128]{1,0:T(8,128)S(1)}, f32[256,128]{1,0:T(8,128)S(1)}, u32[]{:S(2)}, u32[]{:S(2)}) collective-permute-start(f32[256,128]{1,0:T(8,128)S(1)} %constant_dynamic-update-slice_fusion), channel_id=1, source_target_pairs={{5,0},{9,4},{13,8},{17,12},{21,16},{25,20},{29,24},{1,28},{0,1},{4... | collective-permute-start | bytes 393224 | tf_op jit(solution)/shard_map/ppermute | solution.py:341
  13.2 2.3 %collective-permute-done.7 = f32[256,128]{1,0:T(8,128)S(1)} collective-permute-done((f32[256,128]{1,0:T(8,128)S(1)}, f32[256,128]{1,0:T(8,128)S(1)}, u32[]{:S(2)}, u32[]{:S(2)}) %collective-permute-start.7) | collective-permute-done | bytes 131104 | tf_op jit(solution)/shard_map/ppermute | solution.py:336
  15.5 0.0 collective-permute-start.8
  15.6 2.8 %collective-permute-done.5 = f32[256,128]{1,0:T(8,128)S(1)} collective-permute-done((f32[256,128]{1,0:T(8,128)S(1)}, f32[256,128]{1,0:T(8,128)S(1)}, u32[]{:S(2)}, u32[]{:S(2)}) %collective-permute-start.5) | collective-permute-done | bytes 131104 | tf_op jit(solution)/shard_map/ppermute | solution.py:336
  18.3 0.1 collective-permute-start.6
  18.4 0.1 collective-permute-done.3
  18.5 0.4 %collective-permute-start.4 = (f32[256,128]{1,0:T(8,128)S(1)}, f32[256,128]{1,0:T(8,128)S(1)}, u32[]{:S(2)}, u32[]{:S(2)}) collective-permute-start(f32[256,128]{1,0:T(8,128)S(1)} %collective-permute-done.3), channel_id=1, source_target_pairs={{0,1},{1,0},{2,3},{3,2},{4,5},{5,4},{6,7},{7,6},{8,9},{9,8},{10,11... | collective-permute-start | bytes 393224 | tf_op jit(solution)/shard_map/ppermute | solution.py:306
  18.9 0.9 %collective-permute-done.2 = f32[256,128]{1,0:T(8,128)S(1)} collective-permute-done((f32[256,128]{1,0:T(8,128)S(1)}, f32[256,128]{1,0:T(8,128)S(1)}, u32[]{:S(2)}, u32[]{:S(2)}) %collective-permute-start.2) | collective-permute-done | bytes 131104 | tf_op jit(solution)/shard_map/ppermute | solution.py:341
  19.8 0.0 collective-permute-done.8
  19.8 0.0 collective-permute-done.6
  19.8 0.1 collective-permute-done.4
  19.9 0.0 copy-done
  19.9 0.0 copy-done.1
  19.9 3.3 %correlate.1 = f32[64,8,400]{2,1,0:T(8,128)} custom-call(s32[8,128]{1,0:T(8,128)S(1)} %get-tuple-element.7.refs_0_, f32[4,4,2,8,128]{4,3,2,1,0:T(8,128)S(1)} %bitcast.8, f32[4,4,2,8,128]{4,3,2,1,0:T(8,128)S(1)} %bitcast.9, f32[4,4,2,8,128]{4,3,2,1,0:T(8,128)S(1)} %bitcast.13, f32[4,4,2,8,128]{4,3,2,1,0:T(8,128)S(1)} %bitcast.12, ...), custom_call_target="tpu_custom_call" | custom-call | flops 629145600 | bytes 819200 | tf_op jit(solution)/shard_map/correlate/pallas_call | solution.py:260
  (4 shorter events, 0.0 us)
Async XLA Ops:
  0.0 19.9 %copy-start = (bf16[512,400]{1,0:T(8,128)(2,1)S(1)}, bf16[512,400]{1,0:T(8,128)(2,1)}, u32[]{:S(2)}) copy-start(bf16[512,400]{1,0:T(8,128)(2,1)} %constant.11.clone.refs_11_) | copy-start | bytes 1228804
  0.0 19.9 %copy-start.1 = (bf16[512,400]{1,0:T(8,128)(2,1)S(1)}, bf16[512,400]{1,0:T(8,128)(2,1)}, u32[]{:S(2)}) copy-start(bf16[512,400]{1,0:T(8,128)(2,1)} %constant.10.clone.refs_10_) | copy-start | bytes 1228804
  1.8 4.9 %collective-permute-start = (f32[64,128]{1,0:T(8,128)S(1)}, f32[64,128]{1,0:T(8,128)S(1)}, u32[]{:S(2)}, u32[]{:S(2)}) collective-permute-start(f32[64,128]{1,0:T(8,128)S(1)} %get-tuple-element.8), channel_id=1, source_target_pairs={{0,2},{1,3},{2,0},{3,1},{4,6},{5,7},{6,4},{7,5},{8,10},{9,11},{10,... | collective-permute-start | bytes 98312 | tf_op jit(solution)/shard_map/ppermute | solution.py:306
  6.7 1.3 %collective-permute-start.1 = (f32[128,128]{1,0:T(8,128)S(1)}, f32[128,128]{1,0:T(8,128)S(1)}, u32[]{:S(2)}, u32[]{:S(2)}) collective-permute-start(f32[128,128]{1,0:T(8,128)S(1)} %pad_maximum_fusion), channel_id=1, source_target_pairs={{0,1},{1,0},{2,3},{3,2},{4,5},{5,4},{6,7},{7,6},{8,9},{9,8},{10,11... | collective-permute-start | bytes 196616 | tf_op jit(solution)/shard_map/ppermute | solution.py:306
  8.0 7.5 %collective-permute-start.7 = (f32[256,128]{1,0:T(8,128)S(1)}, f32[256,128]{1,0:T(8,128)S(1)}, u32[]{:S(2)}, u32[]{:S(2)}) collective-permute-start(f32[256,128]{1,0:T(8,128)S(1)} %constant_dynamic-update-slice_fusion), channel_id=1, source_target_pairs={{27,0},{31,4},{3,8},{7,12},{11,16},{15,20},{19,24},{23,28},{29,1},... | collective-permute-start | bytes 393224 | tf_op jit(solution)/shard_map/ppermute | solution.py:336
  10.0 8.4 %collective-permute-start.5 = (f32[256,128]{1,0:T(8,128)S(1)}, f32[256,128]{1,0:T(8,128)S(1)}, u32[]{:S(2)}, u32[]{:S(2)}) collective-permute-start(f32[256,128]{1,0:T(8,128)S(1)} %constant_dynamic-update-slice_fusion), channel_id=1, source_target_pairs={{19,0},{23,4},{27,8},{31,12},{3,16},{7,20},{11,24},{15,28},{21,1},... | collective-permute-start | bytes 393224 | tf_op jit(solution)/shard_map/ppermute | solution.py:336
  10.1 8.3 %collective-permute-start.3 = (f32[256,128]{1,0:T(8,128)S(1)}, f32[256,128]{1,0:T(8,128)S(1)}, u32[]{:S(2)}, u32[]{:S(2)}) collective-permute-start(f32[256,128]{1,0:T(8,128)S(1)} %constant_dynamic-update-slice_fusion), channel_id=1, source_target_pairs={{11,0},{15,4},{19,8},{23,12},{27,16},{31,20},{3,24},{7,28},{13,1},... | collective-permute-start | bytes 393224 | tf_op jit(solution)/shard_map/ppermute | solution.py:336
  11.6 8.1 %collective-permute-start.2 = (f32[256,128]{1,0:T(8,128)S(1)}, f32[256,128]{1,0:T(8,128)S(1)}, u32[]{:S(2)}, u32[]{:S(2)}) collective-permute-start(f32[256,128]{1,0:T(8,128)S(1)} %constant_dynamic-update-slice_fusion), channel_id=1, source_target_pairs={{5,0},{9,4},{13,8},{17,12},{21,16},{25,20},{29,24},{1,28},{0,1},{4... | collective-permute-start | bytes 393224 | tf_op jit(solution)/shard_map/ppermute | solution.py:341
  15.5 4.2 %collective-permute-start.8 = (f32[256,128]{1,0:T(8,128)S(1)}, f32[256,128]{1,0:T(8,128)S(1)}, u32[]{:S(2)}, u32[]{:S(2)}) collective-permute-start(f32[256,128]{1,0:T(8,128)S(1)} %collective-permute-done.7), channel_id=1, source_target_pairs={{0,1},{1,0},{2,3},{3,2},{4,5},{5,4},{6,7},{7,6},{8,9},{9,8},{10,11... | collective-permute-start | bytes 393224 | tf_op jit(solution)/shard_map/ppermute | solution.py:306
  18.3 1.4 %collective-permute-start.6 = (f32[256,128]{1,0:T(8,128)S(1)}, f32[256,128]{1,0:T(8,128)S(1)}, u32[]{:S(2)}, u32[]{:S(2)}) collective-permute-start(f32[256,128]{1,0:T(8,128)S(1)} %collective-permute-done.5), channel_id=1, source_target_pairs={{0,1},{1,0},{2,3},{3,2},{4,5},{5,4},{6,7},{7,6},{8,9},{9,8},{10,11... | collective-permute-start | bytes 393224 | tf_op jit(solution)/shard_map/ppermute | solution.py:306
  18.5 1.4 %collective-permute-start.4 = (f32[256,128]{1,0:T(8,128)S(1)}, f32[256,128]{1,0:T(8,128)S(1)}, u32[]{:S(2)}, u32[]{:S(2)}) collective-permute-start(f32[256,128]{1,0:T(8,128)S(1)} %collective-permute-done.3), channel_id=1, source_target_pairs={{0,1},{1,0},{2,3},{3,2},{4,5},{5,4},{6,7},{7,6},{8,9},{9,8},{10,11... | collective-permute-start | bytes 393224 | tf_op jit(solution)/shard_map/ppermute | solution.py:306

commit v5 on v4

--- a/solution.py
+++ b/solution.py
@@ -148,18 +148,21 @@
     )(*[pltpu.with_memory_space_constraint(jnp.asarray(x), pltpu.HBM) for x in (alive, offset_limit, strain, table, twiddle)])
 
 
-def runs(octets):
+CHUNK = 4
+
+
+def runs(octets, most):
     found = []
     for index, octet in enumerate(octets):
-        if found and found[-1][1] + found[-1][2] == octet:
+        if found and found[-1][1] + found[-1][2] == octet and found[-1][2] < most:
             found[-1][2] += 1
         else:
             found.append([index, octet, 1])
     return found
 
 
-def correlate_kernel(orders, needed, octets, early, wins, chans, share, lead, *refs):
-    count = len(orders)
+def correlate_kernel(places, needed, octets, early, wins, chans, share, lead, *refs):
+    count = len(places)
     limit_ref = refs[0]
     blocks = refs[1 : count + 1]
     high_ref, low_ref = refs[count + 1 : count + 3]
@@ -168,74 +171,86 @@
     out_ref, partner, x_high, x_low, lagged, out_sem, early_sem = rest[1 if early else 0 :]
     groups = partner.shape[0]
     place = lax.axis_index("win")
-
-    def out_rows(first, length):
-        return out_ref.at[pl.ds(first * SUB, length * SUB)]
+    half = TILES // 2
+
+    def rows_of(first, length):
+        return pl.ds(first * SUB, length * SUB)
 
     def early_stores():
         return [
-            pltpu.make_async_copy(early_ref.at[pl.ds(at * SUB, length * SUB)], out_rows(octet, length), early_sem.at[at])
-            for at, octet, length in runs(early)
+            pltpu.make_async_copy(early_ref.at[rows_of(at, length)], out_ref.at[rows_of(octet, length)], early_sem.at[at])
+            for at, octet, length in runs(early, len(early))
         ]
 
-    def stores():
-        places = runs(octets) if early else [(0, 0, len(octets))]
-        return [
-            pltpu.make_async_copy(lagged.at[pl.ds(at * SUB, length * SUB)], out_rows(octet, length), out_sem.at[at])
-            for at, octet, length in places
-        ]
+    def store(at, octet, length):
+        target = out_ref.at[rows_of(octet if early else at, length)]
+        return pltpu.make_async_copy(lagged.at[rows_of(at, length)], target, out_sem.at[at])
+
+    pieces = runs(octets, CHUNK)
+
+    def gather():
+        chan, chan_count = lax.axis_index("chan"), lax.axis_size("chan")
+        empty = {(steps, group) for steps in needed for group in range(groups)}
+        for index in range(0 if lead else 1, count):
+            for part, (steps, group) in enumerate(places[index]):
+                if steps not in needed:
+                    continue
+                value = blocks[index][part]
+                if lead and steps > 0:
+                    value = jnp.where(chan + steps < chan_count, value, 0.0)
+                first = needed.index(steps) * chans
+                partner[group, :, :, first : first + chans, :] = value
+                empty.remove((steps, group))
+        for steps, group in sorted(empty):
+            first = needed.index(steps) * chans
+            partner[group, :, :, first : first + chans, :] = jnp.zeros((TILES, wins, chans, LANES), F32)
+
+    def cross(octet):
+        first = needed.index(octet) * SUB
+        sums = [[jnp.zeros((chans, LANES), F32) for _ in range(TILES)] for _ in range(SUB)]
+        for part, (_, group) in enumerate(places[0]):
+            for w in range(wins):
+                mine = [blocks[0][part, t, w] for t in range(TILES)]
+                for j in range(SUB):
+                    theirs = [partner[group, t, w, pl.ds(first + j + 1, SUB), :] for t in range(TILES)]
+                    for t in range(half):
+                        a_re, a_im, b_re, b_im = mine[t], mine[t + half], theirs[t], theirs[t + half]
+                        sums[j][t] = sums[j][t] + (a_re * b_re + a_im * b_im)
+                        sums[j][t + half] = sums[j][t + half] + (a_im * b_re - a_re * b_im)
+        return sums
 
     def work():
         for copy in early_stores():
             copy.start()
+        gather()
         limit = limit_ref[...]
-        chan, chan_count = lax.axis_index("chan"), lax.axis_size("chan")
-        for index, steps in enumerate(needed):
-            rows = slice(index * chans, (index + 1) * chans)
-            if index + 1 >= count:
-                partner[:, :, :, rows, :] = jnp.zeros(partner.shape[:3] + (chans, LANES), F32)
-                continue
-            for position in range(groups):
-                value = blocks[index + 1][position]
-                if lead and steps > 0:
-                    value = jnp.where(chan + steps < chan_count, value, 0.0)
-                partner[orders[index + 1][position], :, :, rows, :] = value
-        own = {orders[0][position]: blocks[0].at[position] for position in range(groups)}
-        half = TILES // 2
-        for at, octet in enumerate(octets):
-            first = needed.index(octet) * SUB
-            sums = [[jnp.zeros((chans, LANES), F32) for _ in range(TILES)] for _ in range(SUB)]
-            for group in range(groups):
-                for w in range(wins):
-                    mine = [own[group][t, w] for t in range(TILES)]
-                    for j in range(SUB):
-                        theirs = [partner[group, t, w, pl.ds(first + j + 1, SUB), :] for t in range(TILES)]
-                        for t in range(half):
-                            a_re, a_im, b_re, b_im = mine[t], mine[t + half], theirs[t], theirs[t + half]
-                            sums[j][t] = sums[j][t] + (a_re * b_re + a_im * b_im)
-                            sums[j][t + half] = sums[j][t + half] + (a_im * b_re - a_re * b_im)
-            offset = place * share + octet * SUB
-            for j in range(0, SUB, 2):
-                pair = []
-                for k in (j, j + 1):
-                    keep = limit > offset + k
-                    pair.append(jnp.concatenate([jnp.where(keep, value, 0.0) for value in sums[k]], axis=1))
-                high, low = halves(jnp.concatenate(pair, axis=0))
-                rows = slice((at * SUB + j) * chans, (at * SUB + j + 2) * chans)
-                x_high[rows, :] = high
-                x_low[rows, :] = low
-        result = mm(x_high[...], high_ref[...]) + mm(x_high[...], low_ref[...]) + mm(x_low[...], high_ref[...])
-        lagged[...] = result.reshape(lagged.shape)
-        for copy in stores():
-            copy.start()
-        for copy in early_stores() + stores():
+        for at, octet, length in pieces:
+            for k in range(length):
+                sums = cross(octet + k)
+                offset = place * share + (octet + k) * SUB
+                for j in range(0, SUB, 2):
+                    pair = [
+                        jnp.concatenate([jnp.where(limit > offset + i, value, 0.0) for value in sums[i]], axis=1)
+                        for i in (j, j + 1)
+                    ]
+                    high, low = halves(jnp.concatenate(pair, axis=0))
+                    first = ((at + k) * SUB + j) * chans
+                    x_high[first : first + 2 * chans, :] = high
+                    x_low[first : first + 2 * chans, :] = low
+            rows = slice(at * SUB * chans, (at + length) * SUB * chans)
+            high, low = x_high[rows, :], x_low[rows, :]
+            result = mm(high, high_ref[...]) + mm(high, low_ref[...]) + mm(low, high_ref[...])
+            lagged[at * SUB : (at + length) * SUB] = result.reshape(length * SUB, chans, result.shape[1])
+            store(at, octet, length).start()
+        for copy in early_stores() + [store(*piece) for piece in pieces]:
             copy.wait()
 
     def blank():
         lagged[...] = jnp.zeros(lagged.shape, F32)
-        for copy in early_stores() + stores():
+        copies = early_stores() + [store(*piece) for piece in pieces]
+        for copy in copies:
             copy.start()
-        for copy in early_stores() + stores():
+        for copy in copies:
             copy.wait()
 
     if lead:
@@ -245,24 +260,22 @@
         work()
 
 
-def correlate(own, partners, octets, early, limit, wins, chans, share, samples, scale, lead):
+def correlate(given, octets, early, limit, wins, chans, share, samples, scale, lead):
     high, low = inverse_tables(samples, scale)
     needed = sorted({octet + step for octet in octets for step in (0, 1)})
-    given = [own] + [partners[d] for d in needed if d in partners]
-    orders = tuple(order for _, order in given)
-    groups = len(orders[0])
-    shape = (groups, TILES, wins, chans, LANES)
+    used = [item for index, item in enumerate(given) if index == 0 or any(steps in needed for steps, _ in item[1])]
+    groups = len(given[0][1])
     size = len(octets) * SUB
     rows = size * chans
     lags = 2 * MAXLAG
     early_octets, early_result = early if early else ((), None)
-    body = functools.partial(correlate_kernel, orders, needed, octets, early_octets, wins, chans, share, lead)
+    places = [item[1] for item in used]
+    body = functools.partial(correlate_kernel, places, needed, octets, early_octets, wins, chans, share, lead)
+    done = early is not None or len(octets) * SUB == share
     return pl.pallas_call(
         body,
         out_shape=jax.ShapeDtypeStruct((size + len(early_octets) * SUB, chans, lags), F32),
-        in_specs=[pl.BlockSpec(memory_space=pltpu.VMEM)]
-        + [pl.BlockSpec(memory_space=pltpu.VMEM)] * len(given)
-        + [pl.BlockSpec(memory_space=pltpu.VMEM)] * 2
+        in_specs=[pl.BlockSpec(memory_space=pltpu.VMEM)] * (len(used) + 3)
         + [pl.BlockSpec(memory_space=pl.ANY)] * bool(early),
         out_specs=pl.BlockSpec(memory_space=pl.ANY),
         scratch_shapes=[
@@ -274,9 +287,19 @@
             pltpu.SemaphoreType.DMA((max(1, len(early_octets)),)),
         ],
         compiler_params=pltpu.CompilerParams(vmem_limit_bytes=32 * MIB),
-        cost_estimate=pl.CostEstimate(flops=6 * rows * 2 * NF * lags, bytes_accessed=4 * rows * lags, transcendentals=0),
+        cost_estimate=pl.CostEstimate(
+            flops=6 * rows * 2 * NF * lags if done else 0,
+            bytes_accessed=4 * rows * lags if done else 0,
+            transcendentals=0,
+        ),
         name="correlate",
-    )(limit, *[block.reshape(shape) for block, _ in given], high, low, *([early_result] if early else []))
+    )(
+        limit,
+        *[block.reshape(-1, TILES, wins, chans, LANES) for block, _ in used],
+        high,
+        low,
+        *([early_result] if early else []),
+    )
 
 
 def local(strain, offset_limit, alive):
@@ -321,29 +344,45 @@
         ]
 
     if win_count == 4 and chan_count * ch_dev <= share:
-        block = white
-        for mask in (2, 1):
-            block = jnp.concatenate([block, exchange(block, mask)], axis=0)
-
-        def order(source):
-            return tuple(source ^ r for r in (0, 2, 1, 3))
-
-        partners = {0: (block, order(0))}
-        for even in range(2, chan_count, 2):
+        def held(steps, source, parts):
+            return [(steps, source ^ part) for part in range(parts)]
+
+        def join(value, mask):
+            return jnp.concatenate([value, exchange(value, mask)], axis=0)
+
+        chip = join(white, 1)
+        far = [chan_count - 2, chan_count - 1] if chan_count >= 4 else []
+        block = join(chip, 2)
+        far_got = [lax.ppermute(chip, axes, shift({0: (steps, 3), 1: (steps, 1)})) for steps in reversed(far)][::-1]
+        given = [(block, held(0, 0, 4))]
+        last = chan_count - 1 - len(far)
+        if chan_count > 1:
+            given.append((lax.ppermute(block, axes, shift({0: (1, 1)})), held(1, 1, 4)))
+        for even in range(2, last + 1, 2):
             wanted = {0: (even, 3)}
-            if even + 1 < chan_count:
+            if even + 1 <= last:
                 wanted[1] = (even + 1, 1)
             got = lax.ppermute(block, axes, shift(wanted))
-            partners[even] = got, order(3)
-            if even + 1 < chan_count:
-                partners[even + 1] = exchange(got, 1), order(1)
-        if chan_count > 1:
-            partners[1] = lax.ppermute(block, axes, shift({0: (1, 1)})), order(1)
-        return finish(partners[0], partners, list(range(reach)), None, lead=True)
+            given.append((got, held(even, 3, 4)))
+            if even + 1 <= last:
+                given.append((exchange(got, 1), held(even + 1, 1, 4)))
+        if far:
+            given += [(got, held(steps, 3, 2)) for got, steps in zip(far_got, far)]
+            handed = exchange(jnp.concatenate(far_got, axis=0), 1)
+            given.append((handed, [place for steps in far for place in held(steps, 1, 2)]))
+        octets = range(reach)
+        if not far:
+            return finish(given, list(octets), None, lead=True)
+        first = [octet for octet in octets if octet >= far[0]]
+        early = first, finish(given, first, None, lead=True)
+        return finish(given, [octet for octet in octets if octet < far[0]], early, lead=True)
 
     gathered = lax.all_gather(white, "win", tiled=True)
-    order = tuple(range(win_count))
-    partners = {}
+
+    def whole(steps):
+        return [(steps, group) for group in range(win_count)]
+
+    given = [(gathered, whole(0))]
     for steps in range(reach + 1):
         pairs = [
             (device(c + reach * w + steps, w), device(c, w))
@@ -352,8 +391,8 @@
             if c + reach * w + steps < chan_count
         ]
         if pairs:
-            partners[steps] = lax.ppermute(gathered, axes, pairs), order
-    return finish((gathered, order), partners, list(range(reach)), None, lead=False)
+            given.append((lax.ppermute(gathered, axes, pairs), whole(steps)))
+    return finish(given, list(range(reach)), None, lead=False)
 
 
 def solution(mesh):

time: 23.3 us -> 21 us (0.901)
  starting transfers between devices: 8.69 us -> 6.56 us
  waiting for transfers between devices: 9.35 us -> 9.11 us
    ppermute x3 -> x2, waiting for transfers between devices: 5.21 us -> 2.3 us  [local(): got = lax.ppermute(block, axes, shift(wanted))]
    ppermute x1 -> x3, waiting for transfers between devices: 0.89 us -> 3.76 us  [the longest x2 3.39 us: local(): lax.ppermute(chip, axes, shift({0: (steps, 3), 1: (steps, 1)}))]
    ppermute x3 -> x2, starting transfers between devices: 3.68 us -> 1.92 us  [local(): got = lax.ppermute(block, axes, shift(wanted))]
    ppermute x1 -> x3, starting transfers between devices: 1.51 us -> 0.73 us  [the longest x1 0.5 us: local(): given.append((lax.ppermute(block, axes, shift({0: (1, 1)})), held(1, 1, 4)))]
    ppermute x5, starting transfers between devices: 3.5 us -> 3.91 us  [exchange(): return lax.ppermute(value, axes, pairs)]
    pallas_call x1 -> x2, Pallas kernels: 3.25 us -> 3.35 us  [correlate(): pl.pallas_call(body, out_shape=jax.ShapeDtypeStruct((size + len(early_oct...]
  transfers between devices with their start and end apart: 9 -> 10, of which waited for: 7 -> 6; matrix products, arithmetic and copies ran while one was open for 0% -> 0% of each run, Pallas kernels for 0% -> 4%
where the time goes in v5:
time: 21 us; the launch traced here: 20.9 us
  waiting for transfers between devices  9.11 us (43%)
  starting transfers between devices  6.56 us (31%)
  Pallas kernels  5.14 us (24%)
    ppermute x5, starting transfers between devices, exchange(): return lax.ppermute(value, axes, pairs)  3.91 us
    ppermute x2, waiting for transfers between devices, local(): lax.ppermute(chip, axes, shift({0: (steps, 3), 1: (steps, 1)}))  3.39 us
    pallas_call x2, Pallas kernels, correlate(): pl.pallas_call(body, out_shape=jax.ShapeDtypeStruct((size + len(early_oct...  3.35 us
    ppermute x5, waiting for transfers between devices, exchange(): return lax.ppermute(value, axes, pairs)  3.05 us
    ppermute x2, waiting for transfers between devices, local(): got = lax.ppermute(block, axes, shift(wanted))  2.3 us
    ppermute x2, starting transfers between devices, local(): got = lax.ppermute(block, axes, shift(wanted))  1.92 us
    pallas_call x1, Pallas kernels, whiten(): pl.pallas_call(whiten_kernel, out_shape=(jax.ShapeDtypeStruct((TILES * ro...  1.78 us
    ppermute x1, starting transfers between devices, local(): given.append((lax.ppermute(block, axes, shift({0: (1, 1)})), held(1, 1, 4)))  0.5 us
  transfers between devices with their start and end apart: 10, of which 6 were waited for; matrix products, arithmetic and copies ran while one was open for 0% of the time, Pallas kernels for 4%

profile of v5, /device:TPU:0, one launch (start us, length us, event | category | flops | bytes accessed | tf_op | source)
XLA Modules:
  0.0 20.9 jit_solution(3949823136520318472)
XLA Ops:
  0.0 0.0 copy-start
  0.0 0.0 copy-start.1
  0.0 1.8 %whiten.1 = (f32[64,128]{1,0:T(8,128)S(1)}, s32[8,128]{1,0:T(8,128)S(1)}) custom-call(s32[8]{0:T(128)} %alive_hbm.1, s32[8]{0:T(128)} %limit_hbm.1, f32[2,8,4096]{2,1,0:T(8,128)} %strain_hbm.1, bf16[512,512]{1,0:T(8,128)(2,1)} %constant.8.clone.table_hbm, f32[16,512]{1,0:T(8,128)} %constant.9.clone.twiddle_hbm), custom_call_target="tpu_custom_call" | custom-call | flops 201326592 | bytes 262144 | tf_op jit(solution)/shard_map/whiten/pallas_call | solution.py:129
  1.8 0.5 %collective-permute-start = (f32[64,128]{1,0:T(8,128)S(1)}, f32[64,128]{1,0:T(8,128)S(1)}, u32[]{:S(2)}, u32[]{:S(2)}) collective-permute-start(f32[64,128]{1,0:T(8,128)S(1)} %get-tuple-element.8), channel_id=1, source_target_pairs={{0,1},{1,0},{2,3},{3,2},{4,5},{5,4},{6,7},{7,6},{8,9},{9,8},{10,11... | collective-permute-start | bytes 98312 | tf_op jit(solution)/shard_map/ppermute | solution.py:329
  2.3 0.9 %collective-permute-done = f32[64,128]{1,0:T(8,128)S(1)} collective-permute-done((f32[64,128]{1,0:T(8,128)S(1)}, f32[64,128]{1,0:T(8,128)S(1)}, u32[]{:S(2)}, u32[]{:S(2)}) %collective-permute-start) | collective-permute-done | bytes 32800 | tf_op jit(solution)/shard_map/ppermute | solution.py:329
  3.2 2.8 %collective-permute-start.1 = (f32[128,128]{1,0:T(8,128)S(1)}, f32[128,128]{1,0:T(8,128)S(1)}, u32[]{:S(2)}, u32[]{:S(2)}) collective-permute-start(f32[128,128]{1,0:T(8,128)S(1)} %get-tuple-element.9), channel_id=1, source_target_pairs={{0,2},{1,3},{2,0},{3,1},{4,6},{5,7},{6,4},{7,5},{8,10},{9,11},{10,... | collective-permute-start | bytes 196616 | tf_op jit(solution)/shard_map/ppermute | solution.py:329
  6.0 0.1 collective-permute-start.8
  6.1 0.2 collective-permute-start.7
  6.2 2.2 %collective-permute-done.1 = f32[128,128]{1,0:T(8,128)S(1)} collective-permute-done((f32[128,128]{1,0:T(8,128)S(1)}, f32[128,128]{1,0:T(8,128)S(1)}, u32[]{:S(2)}, u32[]{:S(2)}) %collective-permute-start.1) | collective-permute-done | bytes 65568 | tf_op jit(solution)/shard_map/ppermute | solution.py:329
  8.4 1.8 %collective-permute-start.5 = (f32[256,128]{1,0:T(8,128)S(1)}, f32[256,128]{1,0:T(8,128)S(1)}, u32[]{:S(2)}, u32[]{:S(2)}) collective-permute-start(f32[256,128]{1,0:T(8,128)S(1)} %constant_dynamic-update-slice_fusion.2), channel_id=1, source_target_pairs={{19,0},{23,4},{27,8},{31,12},{3,16},{7,20},{11,24},{15,28},{21,1},... | collective-permute-start | bytes 393224 | tf_op jit(solution)/shard_map/ppermute | solution.py:365
  10.3 0.1 collective-permute-start.3
  10.4 3.1 %collective-permute-done.8 = f32[128,128]{1,0:T(8,128)S(1)} collective-permute-done((f32[128,128]{1,0:T(8,128)S(1)}, f32[128,128]{1,0:T(8,128)S(1)}, u32[]{:S(2)}, u32[]{:S(2)}) %collective-permute-start.8) | collective-permute-done | bytes 65568 | tf_op jit(solution)/shard_map/ppermute | solution.py:356
  13.4 0.3 %collective-permute-done.7 = f32[128,128]{1,0:T(8,128)S(1)} collective-permute-done((f32[128,128]{1,0:T(8,128)S(1)}, f32[128,128]{1,0:T(8,128)S(1)}, u32[]{:S(2)}, u32[]{:S(2)}) %collective-permute-start.7) | collective-permute-done | bytes 65568 | tf_op jit(solution)/shard_map/ppermute | solution.py:356
  13.8 0.1 collective-permute-start.9
  13.8 0.5 %collective-permute-start.2 = (f32[256,128]{1,0:T(8,128)S(1)}, f32[256,128]{1,0:T(8,128)S(1)}, u32[]{:S(2)}, u32[]{:S(2)}) collective-permute-start(f32[256,128]{1,0:T(8,128)S(1)} %constant_dynamic-update-slice_fusion.2), channel_id=1, source_target_pairs={{5,0},{9,4},{13,8},{17,12},{21,16},{25,20},{29,24},{1,28},{0,1},{4... | collective-permute-start | bytes 393224 | tf_op jit(solution)/shard_map/ppermute | solution.py:360
  14.3 2.3 %collective-permute-done.5 = f32[256,128]{1,0:T(8,128)S(1)} collective-permute-done((f32[256,128]{1,0:T(8,128)S(1)}, f32[256,128]{1,0:T(8,128)S(1)}, u32[]{:S(2)}, u32[]{:S(2)}) %collective-permute-start.5) | collective-permute-done | bytes 131104 | tf_op jit(solution)/shard_map/ppermute | solution.py:365
  16.6 0.0 collective-permute-start.6
  16.6 0.0 collective-permute-done.3
  16.6 0.5 %collective-permute-start.4 = (f32[256,128]{1,0:T(8,128)S(1)}, f32[256,128]{1,0:T(8,128)S(1)}, u32[]{:S(2)}, u32[]{:S(2)}) collective-permute-start(f32[256,128]{1,0:T(8,128)S(1)} %collective-permute-done.3), channel_id=1, source_target_pairs={{0,1},{1,0},{2,3},{3,2},{4,5},{5,4},{6,7},{7,6},{8,9},{9,8},{10,11... | collective-permute-start | bytes 393224 | tf_op jit(solution)/shard_map/ppermute | solution.py:329
  17.1 0.0 collective-permute-done.9
  17.1 0.0 copy-done
  17.1 0.0 copy-done.1
  17.1 0.8 %correlate.2.refs_11_ = f32[16,8,400]{2,1,0:T(8,128)S(1)} custom-call(s32[8,128]{1,0:T(8,128)S(1)} %get-tuple-element.7.refs_0_, f32[4,4,2,8,128]{4,3,2,1,0:T(8,128)S(1)} %bitcast.9, f32[2,4,2,8,128]{4,3,2,1,0:T(8,128)S(1)} %bitcast.11, f32[2,4,2,8,128]{4,3,2,1,0:T(8,128)S(1)} %bitcast.15, f32[4,4,2,8,128]{4,3,2,1,0:T(8,128)S(1)} %bitcast.13, ...), custom_call_target="tpu_custom_call" | custom-call | tf_op jit(solution)/shard_map/correlate/pallas_call | solution.py:275
  17.9 0.4 %collective-permute-done.2 = f32[256,128]{1,0:T(8,128)S(1)} collective-permute-done((f32[256,128]{1,0:T(8,128)S(1)}, f32[256,128]{1,0:T(8,128)S(1)}, u32[]{:S(2)}, u32[]{:S(2)}) %collective-permute-start.2) | collective-permute-done | bytes 131104 | tf_op jit(solution)/shard_map/ppermute | solution.py:360
  18.3 0.0 collective-permute-done.6
  18.3 0.0 collective-permute-done.4
  18.3 2.6 %correlate.3 = f32[64,8,400]{2,1,0:T(8,128)} custom-call(s32[8,128]{1,0:T(8,128)S(1)} %get-tuple-element.7.refs_0_, f32[4,4,2,8,128]{4,3,2,1,0:T(8,128)S(1)} %bitcast.10, f32[4,4,2,8,128]{4,3,2,1,0:T(8,128)S(1)} %bitcast.18, f32[4,4,2,8,128]{4,3,2,1,0:T(8,128)S(1)} %bitcast.17, f32[4,4,2,8,128]{4,3,2,1,0:T(8,128)S(1)} %bitcast.20, ...), custom_call_target="tpu_custom_call" | custom-call | flops 471859200 | bytes 614400 | tf_op jit(solution)/shard_map/correlate/pallas_call | solution.py:275
  (4 shorter events, 0.0 us)
Async XLA Ops:
  0.0 17.1 %copy-start = (bf16[512,400]{1,0:T(8,128)(2,1)S(1)}, bf16[512,400]{1,0:T(8,128)(2,1)}, u32[]{:S(2)}) copy-start(bf16[512,400]{1,0:T(8,128)(2,1)} %constant.11.clone.refs_6_.refs_10_) | copy-start | bytes 1228804
  0.0 17.1 %copy-start.1 = (bf16[512,400]{1,0:T(8,128)(2,1)S(1)}, bf16[512,400]{1,0:T(8,128)(2,1)}, u32[]{:S(2)}) copy-start(bf16[512,400]{1,0:T(8,128)(2,1)} %constant.10.clone.refs_5_.refs_9_) | copy-start | bytes 1228804
  1.8 1.4 %collective-permute-start = (f32[64,128]{1,0:T(8,128)S(1)}, f32[64,128]{1,0:T(8,128)S(1)}, u32[]{:S(2)}, u32[]{:S(2)}) collective-permute-start(f32[64,128]{1,0:T(8,128)S(1)} %get-tuple-element.8), channel_id=1, source_target_pairs={{0,1},{1,0},{2,3},{3,2},{4,5},{5,4},{6,7},{7,6},{8,9},{9,8},{10,11... | collective-permute-start | bytes 98312 | tf_op jit(solution)/shard_map/ppermute | solution.py:329
  3.2 5.3 %collective-permute-start.1 = (f32[128,128]{1,0:T(8,128)S(1)}, f32[128,128]{1,0:T(8,128)S(1)}, u32[]{:S(2)}, u32[]{:S(2)}) collective-permute-start(f32[128,128]{1,0:T(8,128)S(1)} %get-tuple-element.9), channel_id=1, source_target_pairs={{0,2},{1,3},{2,0},{3,1},{4,6},{5,7},{6,4},{7,5},{8,10},{9,11},{10,... | collective-permute-start | bytes 196616 | tf_op jit(solution)/shard_map/ppermute | solution.py:329
  6.0 7.4 %collective-permute-start.8 = (f32[128,128]{1,0:T(8,128)S(1)}, f32[128,128]{1,0:T(8,128)S(1)}, u32[]{:S(2)}, u32[]{:S(2)}) collective-permute-start(f32[128,128]{1,0:T(8,128)S(1)} %get-tuple-element.9), channel_id=1, source_target_pairs={{31,0},{3,4},{7,8},{11,12},{15,16},{19,20},{23,24},{27,28},{29,1},... | collective-permute-start | bytes 196616 | tf_op jit(solution)/shard_map/ppermute | solution.py:356
  6.1 7.7 %collective-permute-start.7 = (f32[128,128]{1,0:T(8,128)S(1)}, f32[128,128]{1,0:T(8,128)S(1)}, u32[]{:S(2)}, u32[]{:S(2)}) collective-permute-start(f32[128,128]{1,0:T(8,128)S(1)} %get-tuple-element.9), channel_id=1, source_target_pairs={{27,0},{31,4},{3,8},{7,12},{11,16},{15,20},{19,24},{23,28},{25,1},... | collective-permute-start | bytes 196616 | tf_op jit(solution)/shard_map/ppermute | solution.py:356
  8.4 8.2 %collective-permute-start.5 = (f32[256,128]{1,0:T(8,128)S(1)}, f32[256,128]{1,0:T(8,128)S(1)}, u32[]{:S(2)}, u32[]{:S(2)}) collective-permute-start(f32[256,128]{1,0:T(8,128)S(1)} %constant_dynamic-update-slice_fusion.2), channel_id=1, source_target_pairs={{19,0},{23,4},{27,8},{31,12},{3,16},{7,20},{11,24},{15,28},{21,1},... | collective-permute-start | bytes 393224 | tf_op jit(solution)/shard_map/ppermute | solution.py:365
  10.3 6.4 %collective-permute-start.3 = (f32[256,128]{1,0:T(8,128)S(1)}, f32[256,128]{1,0:T(8,128)S(1)}, u32[]{:S(2)}, u32[]{:S(2)}) collective-permute-start(f32[256,128]{1,0:T(8,128)S(1)} %constant_dynamic-update-slice_fusion.2), channel_id=1, source_target_pairs={{11,0},{15,4},{19,8},{23,12},{27,16},{31,20},{3,24},{7,28},{13,1},... | collective-permute-start | bytes 393224 | tf_op jit(solution)/shard_map/ppermute | solution.py:365
  13.8 3.4 %collective-permute-start.9 = (f32[256,128]{1,0:T(8,128)S(1)}, f32[256,128]{1,0:T(8,128)S(1)}, u32[]{:S(2)}, u32[]{:S(2)}) collective-permute-start(f32[256,128]{1,0:T(8,128)S(1)} %pad_maximum_fusion), channel_id=1, source_target_pairs={{0,1},{1,0},{2,3},{3,2},{4,5},{5,4},{6,7},{7,6},{8,9},{9,8},{10,11... | collective-permute-start | bytes 393224 | tf_op jit(solution)/shard_map/ppermute | solution.py:329
  13.8 4.4 %collective-permute-start.2 = (f32[256,128]{1,0:T(8,128)S(1)}, f32[256,128]{1,0:T(8,128)S(1)}, u32[]{:S(2)}, u32[]{:S(2)}) collective-permute-start(f32[256,128]{1,0:T(8,128)S(1)} %constant_dynamic-update-slice_fusion.2), channel_id=1, source_target_pairs={{5,0},{9,4},{13,8},{17,12},{21,16},{25,20},{29,24},{1,28},{0,1},{4... | collective-permute-start | bytes 393224 | tf_op jit(solution)/shard_map/ppermute | solution.py:360
  16.6 1.7 %collective-permute-start.6 = (f32[256,128]{1,0:T(8,128)S(1)}, f32[256,128]{1,0:T(8,128)S(1)}, u32[]{:S(2)}, u32[]{:S(2)}) collective-permute-start(f32[256,128]{1,0:T(8,128)S(1)} %collective-permute-done.5), channel_id=1, source_target_pairs={{0,1},{1,0},{2,3},{3,2},{4,5},{5,4},{6,7},{7,6},{8,9},{9,8},{10,11... | collective-permute-start | bytes 393224 | tf_op jit(solution)/shard_map/ppermute | solution.py:329
  16.6 1.7 %collective-permute-start.4 = (f32[256,128]{1,0:T(8,128)S(1)}, f32[256,128]{1,0:T(8,128)S(1)}, u32[]{:S(2)}, u32[]{:S(2)}) collective-permute-start(f32[256,128]{1,0:T(8,128)S(1)} %collective-permute-done.3), channel_id=1, source_target_pairs={{0,1},{1,0},{2,3},{3,2},{4,5},{5,4},{6,7},{7,6},{8,9},{9,8},{10,11... | collective-permute-start | bytes 393224 | tf_op jit(solution)/shard_map/ppermute | solution.py:329

commit v6 on v5

--- a/solution.py
+++ b/solution.py
@@ -84,13 +84,17 @@
     ]
     for copy in copies:
         copy.start()
-    for copy in copies:
-        copy.wait()
+    block_r = lax.broadcasted_iota(jnp.int32, (NF, NF), 0) // WHITEN_BINS
+    block_c = lax.broadcasted_iota(jnp.int32, (NF, NF), 1) // WHITEN_BINS
+    mean = jnp.where(block_r == block_c, 1.0 / WHITEN_BINS, 0.0).astype(BF16)
     rows = wins * chans
+    copies[0].wait()
     strain = strain_ref[...].reshape(rows, samples)
     pieces = samples // chunk
     stacked = jnp.concatenate([strain[:, a * chunk : (a + 1) * chunk] for a in range(pieces)], axis=0)
     x_high, x_low = halves(stacked)
+    for copy in copies[1:]:
+        copy.wait()
     high = table_ref[:chunk, :]
     part = mm(x_high, high) + mm(x_high, table_ref[chunk:, :]) + mm(x_low, high)
     real = jnp.zeros((rows, NF), F32)
@@ -103,9 +107,6 @@
         real = real + p_re * cos + p_im * sin
         imag = imag + p_im * cos - p_re * sin
     magnitude = jnp.sqrt(real * real + imag * imag)
-    block_r = lax.broadcasted_iota(jnp.int32, (NF, NF), 0) // WHITEN_BINS
-    block_c = lax.broadcasted_iota(jnp.int32, (NF, NF), 1) // WHITEN_BINS
-    mean = jnp.where(block_r == block_c, 1.0 / WHITEN_BINS, 0.0).astype(BF16)
     m_high, m_low = halves(magnitude)
     level = mm(m_high, mean) + mm(m_low, mean) + EPS
     live = column(alive_ref, chans).astype(F32)
@@ -199,25 +200,31 @@
                 if lead and steps > 0:
                     value = jnp.where(chan + steps < chan_count, value, 0.0)
                 first = needed.index(steps) * chans
-                partner[group, :, :, first : first + chans, :] = value
+                for t in range(half):
+                    re, im = value[t], value[t + half]
+                    partner[group, 3 * t, :, first : first + chans, :] = re
+                    partner[group, 3 * t + 1, :, first : first + chans, :] = re + im
+                    partner[group, 3 * t + 2, :, first : first + chans, :] = re - im
                 empty.remove((steps, group))
         for steps, group in sorted(empty):
             first = needed.index(steps) * chans
-            partner[group, :, :, first : first + chans, :] = jnp.zeros((TILES, wins, chans, LANES), F32)
+            partner[group, :, :, first : first + chans, :] = jnp.zeros((3 * half, wins, chans, LANES), F32)
 
     def cross(octet):
         first = needed.index(octet) * SUB
-        sums = [[jnp.zeros((chans, LANES), F32) for _ in range(TILES)] for _ in range(SUB)]
+        sums = [[jnp.zeros((chans, LANES), F32) for _ in range(3 * half)] for _ in range(SUB)]
         for part, (_, group) in enumerate(places[0]):
             for w in range(wins):
-                mine = [blocks[0][part, t, w] for t in range(TILES)]
-                for j in range(SUB):
-                    theirs = [partner[group, t, w, pl.ds(first + j + 1, SUB), :] for t in range(TILES)]
-                    for t in range(half):
-                        a_re, a_im, b_re, b_im = mine[t], mine[t + half], theirs[t], theirs[t + half]
-                        sums[j][t] = sums[j][t] + (a_re * b_re + a_im * b_im)
-                        sums[j][t + half] = sums[j][t + half] + (a_im * b_re - a_re * b_im)
-        return sums
+                for t in range(half):
+                    a_re, a_im = blocks[0][part, t, w], blocks[0][part, t + half, w]
+                    mine = (a_re + a_im, a_re, a_im)
+                    for j in range(SUB):
+                        for k in range(3):
+                            theirs = partner[group, 3 * t + k, w, pl.ds(first + j + 1, SUB), :]
+                            sums[j][3 * t + k] = sums[j][3 * t + k] + mine[k] * theirs
+        return [
+            [s[3 * t] - s[3 * t + 2] for t in range(half)] + [s[3 * t] - s[3 * t + 1] for t in range(half)] for s in sums
+        ]
 
     def work():
         for copy in early_stores():
@@ -279,7 +286,7 @@
         + [pl.BlockSpec(memory_space=pl.ANY)] * bool(early),
         out_specs=pl.BlockSpec(memory_space=pl.ANY),
         scratch_shapes=[
-            pltpu.VMEM((groups, TILES, wins, len(needed) * SUB, LANES), F32),
+            pltpu.VMEM((groups, 3 * TILES // 2, wins, len(needed) * SUB, LANES), F32),
             pltpu.VMEM((rows, 2 * NF), BF16),
             pltpu.VMEM((rows, 2 * NF), BF16),
             pltpu.VMEM((size, chans, lags), F32),

time: 21 us -> 20.8 us (level)
  Pallas kernels: 5.14 us -> 4.87 us
    pallas_call x2, Pallas kernels: 3.35 us -> 3.08 us  [correlate(): pl.pallas_call(body, out_shape=jax.ShapeDtypeStruct((size + len(early_oct...]
where the time goes in v6:
time: 20.8 us; the launch traced here: 20.7 us
  waiting for transfers between devices  9.15 us (44%)
  starting transfers between devices  6.56 us (32%)
  Pallas kernels  4.87 us (23%)
    ppermute x5, starting transfers between devices, exchange(): return lax.ppermute(value, axes, pairs)  3.91 us
    ppermute x2, waiting for transfers between devices, local(): lax.ppermute(chip, axes, shift({0: (steps, 3), 1: (steps, 1)}))  3.39 us
    pallas_call x2, Pallas kernels, correlate(): pl.pallas_call(body, out_shape=jax.ShapeDtypeStruct((size + len(early_oct...  3.08 us
    ppermute x5, waiting for transfers between devices, exchange(): return lax.ppermute(value, axes, pairs)  3.05 us
    ppermute x2, waiting for transfers between devices, local(): got = lax.ppermute(block, axes, shift(wanted))  2.3 us
    ppermute x2, starting transfers between devices, local(): got = lax.ppermute(block, axes, shift(wanted))  1.92 us
    pallas_call x1, Pallas kernels, whiten(): pl.pallas_call(whiten_kernel, out_shape=(jax.ShapeDtypeStruct((TILES * ro...  1.79 us
    ppermute x1, starting transfers between devices, local(): given.append((lax.ppermute(block, axes, shift({0: (1, 1)})), held(1, 1, 4)))  0.5 us
  transfers between devices with their start and end apart: 10, of which 6 were waited for; matrix products, arithmetic and copies ran while one was open for 0% of the time, Pallas kernels for 4%

profile of v6, /device:TPU:0, one launch (start us, length us, event | category | flops | bytes accessed | tf_op | source)
XLA Modules:
  0.0 20.7 jit_solution(4679874356868604568)
XLA Ops:
  0.0 0.0 copy-start
  0.0 0.0 copy-start.1
  0.0 1.8 %whiten.1 = (f32[64,128]{1,0:T(8,128)S(1)}, s32[8,128]{1,0:T(8,128)S(1)}) custom-call(s32[8]{0:T(128)} %alive_hbm.1, s32[8]{0:T(128)} %limit_hbm.1, f32[2,8,4096]{2,1,0:T(8,128)} %strain_hbm.1, bf16[512,512]{1,0:T(8,128)(2,1)} %constant.8.clone.table_hbm, f32[16,512]{1,0:T(8,128)} %constant.9.clone.twiddle_hbm), custom_call_target="tpu_custom_call" | custom-call | flops 201326592 | bytes 262144 | tf_op jit(solution)/shard_map/whiten/pallas_call | solution.py:130
  1.8 0.5 %collective-permute-start = (f32[64,128]{1,0:T(8,128)S(1)}, f32[64,128]{1,0:T(8,128)S(1)}, u32[]{:S(2)}, u32[]{:S(2)}) collective-permute-start(f32[64,128]{1,0:T(8,128)S(1)} %get-tuple-element.8), channel_id=1, source_target_pairs={{0,1},{1,0},{2,3},{3,2},{4,5},{5,4},{6,7},{7,6},{8,9},{9,8},{10,11... | collective-permute-start | bytes 98312 | tf_op jit(solution)/shard_map/ppermute | solution.py:336
  2.3 0.9 %collective-permute-done = f32[64,128]{1,0:T(8,128)S(1)} collective-permute-done((f32[64,128]{1,0:T(8,128)S(1)}, f32[64,128]{1,0:T(8,128)S(1)}, u32[]{:S(2)}, u32[]{:S(2)}) %collective-permute-start) | collective-permute-done | bytes 32800 | tf_op jit(solution)/shard_map/ppermute | solution.py:336
  3.2 2.8 %collective-permute-start.1 = (f32[128,128]{1,0:T(8,128)S(1)}, f32[128,128]{1,0:T(8,128)S(1)}, u32[]{:S(2)}, u32[]{:S(2)}) collective-permute-start(f32[128,128]{1,0:T(8,128)S(1)} %get-tuple-element.9), channel_id=1, source_target_pairs={{0,2},{1,3},{2,0},{3,1},{4,6},{5,7},{6,4},{7,5},{8,10},{9,11},{10,... | collective-permute-start | bytes 196616 | tf_op jit(solution)/shard_map/ppermute | solution.py:336
  6.0 0.1 collective-permute-start.8
  6.1 0.2 collective-permute-start.7
  6.2 2.2 %collective-permute-done.1 = f32[128,128]{1,0:T(8,128)S(1)} collective-permute-done((f32[128,128]{1,0:T(8,128)S(1)}, f32[128,128]{1,0:T(8,128)S(1)}, u32[]{:S(2)}, u32[]{:S(2)}) %collective-permute-start.1) | collective-permute-done | bytes 65568 | tf_op jit(solution)/shard_map/ppermute | solution.py:336
  8.4 1.8 %collective-permute-start.5 = (f32[256,128]{1,0:T(8,128)S(1)}, f32[256,128]{1,0:T(8,128)S(1)}, u32[]{:S(2)}, u32[]{:S(2)}) collective-permute-start(f32[256,128]{1,0:T(8,128)S(1)} %constant_dynamic-update-slice_fusion.2), channel_id=1, source_target_pairs={{19,0},{23,4},{27,8},{31,12},{3,16},{7,20},{11,24},{15,28},{21,1},... | collective-permute-start | bytes 393224 | tf_op jit(solution)/shard_map/ppermute | solution.py:372
  10.3 0.1 collective-permute-start.3
  10.4 3.1 %collective-permute-done.8 = f32[128,128]{1,0:T(8,128)S(1)} collective-permute-done((f32[128,128]{1,0:T(8,128)S(1)}, f32[128,128]{1,0:T(8,128)S(1)}, u32[]{:S(2)}, u32[]{:S(2)}) %collective-permute-start.8) | collective-permute-done | bytes 65568 | tf_op jit(solution)/shard_map/ppermute | solution.py:363
  13.4 0.3 %collective-permute-done.7 = f32[128,128]{1,0:T(8,128)S(1)} collective-permute-done((f32[128,128]{1,0:T(8,128)S(1)}, f32[128,128]{1,0:T(8,128)S(1)}, u32[]{:S(2)}, u32[]{:S(2)}) %collective-permute-start.7) | collective-permute-done | bytes 65568 | tf_op jit(solution)/shard_map/ppermute | solution.py:363
  13.8 0.1 collective-permute-start.9
  13.8 0.5 %collective-permute-start.2 = (f32[256,128]{1,0:T(8,128)S(1)}, f32[256,128]{1,0:T(8,128)S(1)}, u32[]{:S(2)}, u32[]{:S(2)}) collective-permute-start(f32[256,128]{1,0:T(8,128)S(1)} %constant_dynamic-update-slice_fusion.2), channel_id=1, source_target_pairs={{5,0},{9,4},{13,8},{17,12},{21,16},{25,20},{29,24},{1,28},{0,1},{4... | collective-permute-start | bytes 393224 | tf_op jit(solution)/shard_map/ppermute | solution.py:367
  14.3 2.3 %collective-permute-done.5 = f32[256,128]{1,0:T(8,128)S(1)} collective-permute-done((f32[256,128]{1,0:T(8,128)S(1)}, f32[256,128]{1,0:T(8,128)S(1)}, u32[]{:S(2)}, u32[]{:S(2)}) %collective-permute-start.5) | collective-permute-done | bytes 131104 | tf_op jit(solution)/shard_map/ppermute | solution.py:372
  16.6 0.0 collective-permute-start.6
  16.6 0.0 collective-permute-done.3
  16.6 0.5 %collective-permute-start.4 = (f32[256,128]{1,0:T(8,128)S(1)}, f32[256,128]{1,0:T(8,128)S(1)}, u32[]{:S(2)}, u32[]{:S(2)}) collective-permute-start(f32[256,128]{1,0:T(8,128)S(1)} %collective-permute-done.3), channel_id=1, source_target_pairs={{0,1},{1,0},{2,3},{3,2},{4,5},{5,4},{6,7},{7,6},{8,9},{9,8},{10,11... | collective-permute-start | bytes 393224 | tf_op jit(solution)/shard_map/ppermute | solution.py:336
  17.1 0.0 collective-permute-done.9
  17.1 0.0 copy-done
  17.1 0.0 copy-done.1
  17.1 0.7 %correlate.2.refs_11_ = f32[16,8,400]{2,1,0:T(8,128)S(1)} custom-call(s32[8,128]{1,0:T(8,128)S(1)} %get-tuple-element.7.refs_0_, f32[4,4,2,8,128]{4,3,2,1,0:T(8,128)S(1)} %bitcast.9, f32[2,4,2,8,128]{4,3,2,1,0:T(8,128)S(1)} %bitcast.11, f32[2,4,2,8,128]{4,3,2,1,0:T(8,128)S(1)} %bitcast.15, f32[4,4,2,8,128]{4,3,2,1,0:T(8,128)S(1)} %bitcast.13, ...), custom_call_target="tpu_custom_call" | custom-call | tf_op jit(solution)/shard_map/correlate/pallas_call | solution.py:282
  17.9 0.4 %collective-permute-done.2 = f32[256,128]{1,0:T(8,128)S(1)} collective-permute-done((f32[256,128]{1,0:T(8,128)S(1)}, f32[256,128]{1,0:T(8,128)S(1)}, u32[]{:S(2)}, u32[]{:S(2)}) %collective-permute-start.2) | collective-permute-done | bytes 131104 | tf_op jit(solution)/shard_map/ppermute | solution.py:367
  18.3 0.0 collective-permute-done.6
  18.3 0.0 collective-permute-done.4
  18.3 2.4 %correlate.3 = f32[64,8,400]{2,1,0:T(8,128)} custom-call(s32[8,128]{1,0:T(8,128)S(1)} %get-tuple-element.7.refs_0_, f32[4,4,2,8,128]{4,3,2,1,0:T(8,128)S(1)} %bitcast.10, f32[4,4,2,8,128]{4,3,2,1,0:T(8,128)S(1)} %bitcast.18, f32[4,4,2,8,128]{4,3,2,1,0:T(8,128)S(1)} %bitcast.17, f32[4,4,2,8,128]{4,3,2,1,0:T(8,128)S(1)} %bitcast.20, ...), custom_call_target="tpu_custom_call" | custom-call | flops 471859200 | bytes 614400 | tf_op jit(solution)/shard_map/correlate/pallas_call | solution.py:282
  (4 shorter events, 0.0 us)
Async XLA Ops:
  0.0 17.1 %copy-start = (bf16[512,400]{1,0:T(8,128)(2,1)S(1)}, bf16[512,400]{1,0:T(8,128)(2,1)}, u32[]{:S(2)}) copy-start(bf16[512,400]{1,0:T(8,128)(2,1)} %constant.11.clone.refs_6_.refs_10_) | copy-start | bytes 1228804
  0.0 17.1 %copy-start.1 = (bf16[512,400]{1,0:T(8,128)(2,1)S(1)}, bf16[512,400]{1,0:T(8,128)(2,1)}, u32[]{:S(2)}) copy-start(bf16[512,400]{1,0:T(8,128)(2,1)} %constant.10.clone.refs_5_.refs_9_) | copy-start | bytes 1228804
  1.8 1.4 %collective-permute-start = (f32[64,128]{1,0:T(8,128)S(1)}, f32[64,128]{1,0:T(8,128)S(1)}, u32[]{:S(2)}, u32[]{:S(2)}) collective-permute-start(f32[64,128]{1,0:T(8,128)S(1)} %get-tuple-element.8), channel_id=1, source_target_pairs={{0,1},{1,0},{2,3},{3,2},{4,5},{5,4},{6,7},{7,6},{8,9},{9,8},{10,11... | collective-permute-start | bytes 98312 | tf_op jit(solution)/shard_map/ppermute | solution.py:336
  3.2 5.3 %collective-permute-start.1 = (f32[128,128]{1,0:T(8,128)S(1)}, f32[128,128]{1,0:T(8,128)S(1)}, u32[]{:S(2)}, u32[]{:S(2)}) collective-permute-start(f32[128,128]{1,0:T(8,128)S(1)} %get-tuple-element.9), channel_id=1, source_target_pairs={{0,2},{1,3},{2,0},{3,1},{4,6},{5,7},{6,4},{7,5},{8,10},{9,11},{10,... | collective-permute-start | bytes 196616 | tf_op jit(solution)/shard_map/ppermute | solution.py:336
  6.0 7.4 %collective-permute-start.8 = (f32[128,128]{1,0:T(8,128)S(1)}, f32[128,128]{1,0:T(8,128)S(1)}, u32[]{:S(2)}, u32[]{:S(2)}) collective-permute-start(f32[128,128]{1,0:T(8,128)S(1)} %get-tuple-element.9), channel_id=1, source_target_pairs={{31,0},{3,4},{7,8},{11,12},{15,16},{19,20},{23,24},{27,28},{29,1},... | collective-permute-start | bytes 196616 | tf_op jit(solution)/shard_map/ppermute | solution.py:363
  6.1 7.7 %collective-permute-start.7 = (f32[128,128]{1,0:T(8,128)S(1)}, f32[128,128]{1,0:T(8,128)S(1)}, u32[]{:S(2)}, u32[]{:S(2)}) collective-permute-start(f32[128,128]{1,0:T(8,128)S(1)} %get-tuple-element.9), channel_id=1, source_target_pairs={{27,0},{31,4},{3,8},{7,12},{11,16},{15,20},{19,24},{23,28},{25,1},... | collective-permute-start | bytes 196616 | tf_op jit(solution)/shard_map/ppermute | solution.py:363
  8.4 8.2 %collective-permute-start.5 = (f32[256,128]{1,0:T(8,128)S(1)}, f32[256,128]{1,0:T(8,128)S(1)}, u32[]{:S(2)}, u32[]{:S(2)}) collective-permute-start(f32[256,128]{1,0:T(8,128)S(1)} %constant_dynamic-update-slice_fusion.2), channel_id=1, source_target_pairs={{19,0},{23,4},{27,8},{31,12},{3,16},{7,20},{11,24},{15,28},{21,1},... | collective-permute-start | bytes 393224 | tf_op jit(solution)/shard_map/ppermute | solution.py:372
  10.3 6.4 %collective-permute-start.3 = (f32[256,128]{1,0:T(8,128)S(1)}, f32[256,128]{1,0:T(8,128)S(1)}, u32[]{:S(2)}, u32[]{:S(2)}) collective-permute-start(f32[256,128]{1,0:T(8,128)S(1)} %constant_dynamic-update-slice_fusion.2), channel_id=1, source_target_pairs={{11,0},{15,4},{19,8},{23,12},{27,16},{31,20},{3,24},{7,28},{13,1},... | collective-permute-start | bytes 393224 | tf_op jit(solution)/shard_map/ppermute | solution.py:372
  13.8 3.4 %collective-permute-start.9 = (f32[256,128]{1,0:T(8,128)S(1)}, f32[256,128]{1,0:T(8,128)S(1)}, u32[]{:S(2)}, u32[]{:S(2)}) collective-permute-start(f32[256,128]{1,0:T(8,128)S(1)} %pad_maximum_fusion), channel_id=1, source_target_pairs={{0,1},{1,0},{2,3},{3,2},{4,5},{5,4},{6,7},{7,6},{8,9},{9,8},{10,11... | collective-permute-start | bytes 393224 | tf_op jit(solution)/shard_map/ppermute | solution.py:336
  13.8 4.4 %collective-permute-start.2 = (f32[256,128]{1,0:T(8,128)S(1)}, f32[256,128]{1,0:T(8,128)S(1)}, u32[]{:S(2)}, u32[]{:S(2)}) collective-permute-start(f32[256,128]{1,0:T(8,128)S(1)} %constant_dynamic-update-slice_fusion.2), channel_id=1, source_target_pairs={{5,0},{9,4},{13,8},{17,12},{21,16},{25,20},{29,24},{1,28},{0,1},{4... | collective-permute-start | bytes 393224 | tf_op jit(solution)/shard_map/ppermute | solution.py:367
  16.6 1.7 %collective-permute-start.6 = (f32[256,128]{1,0:T(8,128)S(1)}, f32[256,128]{1,0:T(8,128)S(1)}, u32[]{:S(2)}, u32[]{:S(2)}) collective-permute-start(f32[256,128]{1,0:T(8,128)S(1)} %collective-permute-done.5), channel_id=1, source_target_pairs={{0,1},{1,0},{2,3},{3,2},{4,5},{5,4},{6,7},{7,6},{8,9},{9,8},{10,11... | collective-permute-start | bytes 393224 | tf_op jit(solution)/shard_map/ppermute | solution.py:336
  16.6 1.7 %collective-permute-start.4 = (f32[256,128]{1,0:T(8,128)S(1)}, f32[256,128]{1,0:T(8,128)S(1)}, u32[]{:S(2)}, u32[]{:S(2)}) collective-permute-start(f32[256,128]{1,0:T(8,128)S(1)} %collective-permute-done.3), channel_id=1, source_target_pairs={{0,1},{1,0},{2,3},{3,2},{4,5},{5,4},{6,7},{7,6},{8,9},{9,8},{10,11... | collective-permute-start | bytes 393224 | tf_op jit(solution)/shard_map/ppermute | solution.py:336

commit v7 on v6

--- a/solution.py
+++ b/solution.py
@@ -360,7 +360,7 @@
         chip = join(white, 1)
         far = [chan_count - 2, chan_count - 1] if chan_count >= 4 else []
         block = join(chip, 2)
-        far_got = [lax.ppermute(chip, axes, shift({0: (steps, 3), 1: (steps, 1)})) for steps in reversed(far)][::-1]
+        far_got = [lax.ppermute(chip, axes, shift({0: (steps, 1), 1: (steps, 3)})) for steps in reversed(far)][::-1]
         given = [(block, held(0, 0, 4))]
         last = chan_count - 1 - len(far)
         if chan_count > 1:
@@ -374,9 +374,9 @@
             if even + 1 <= last:
                 given.append((exchange(got, 1), held(even + 1, 1, 4)))
         if far:
-            given += [(got, held(steps, 3, 2)) for got, steps in zip(far_got, far)]
+            given += [(got, held(steps, 1, 2)) for got, steps in zip(far_got, far)]
             handed = exchange(jnp.concatenate(far_got, axis=0), 1)
-            given.append((handed, [place for steps in far for place in held(steps, 1, 2)]))
+            given.append((handed, [place for steps in far for place in held(steps, 3, 2)]))
         octets = range(reach)
         if not far:
             return finish(given, list(octets), None, lead=True)

time: 20.8 us -> 20.6 us (level)
  waiting for transfers between devices: 9.15 us -> 8.58 us
  starting transfers between devices: 6.56 us -> 6.93 us
    ppermute x2, waiting for transfers between devices: 3.39 us -> 2.32 us  [local(): lax.ppermute(chip, axes, shift({0: (steps, 1), 1: (steps, 3)}))]
    ppermute x5, starting transfers between devices: 3.91 us -> 4.59 us  [exchange(): return lax.ppermute(value, axes, pairs)]
    ppermute x2, waiting for transfers between devices: 2.3 us -> 2.94 us  [local(): got = lax.ppermute(block, axes, shift(wanted))]
    ppermute x1, starting transfers between devices: 0.5 us -> 0.06 us  [local(): given.append((lax.ppermute(block, axes, shift({0: (1, 1)})), held(1, 1, 4)))]
    ppermute x1, waiting for transfers between devices: 0.41 us -> 0.15 us  [local(): given.append((lax.ppermute(block, axes, shift({0: (1, 1)})), held(1, 1, 4)))]
  transfers between devices with their start and end apart: 10 -> 10, of which waited for: 6 -> 7; matrix products, arithmetic and copies ran while one was open for 0% -> 0% of each run, Pallas kernels for 4% -> 4%
where the time goes in v7:
time: 20.6 us; the launch traced here: 20.4 us
  waiting for transfers between devices  8.58 us (42%)
  starting transfers between devices  6.93 us (34%)
  Pallas kernels  4.87 us (24%)
    ppermute x5, starting transfers between devices, exchange(): return lax.ppermute(value, axes, pairs)  4.59 us
    ppermute x5, waiting for transfers between devices, exchange(): return lax.ppermute(value, axes, pairs)  3.17 us
    pallas_call x2, Pallas kernels, correlate(): pl.pallas_call(body, out_shape=jax.ShapeDtypeStruct((size + len(early_oct...  3.08 us
    ppermute x2, waiting for transfers between devices, local(): got = lax.ppermute(block, axes, shift(wanted))  2.94 us
    ppermute x2, waiting for transfers between devices, local(): lax.ppermute(chip, axes, shift({0: (steps, 1), 1: (steps, 3)}))  2.32 us
    ppermute x2, starting transfers between devices, local(): got = lax.ppermute(block, axes, shift(wanted))  2.05 us
    pallas_call x1, Pallas kernels, whiten(): pl.pallas_call(whiten_kernel, out_shape=(jax.ShapeDtypeStruct((TILES * ro...  1.79 us
  transfers between devices with their start and end apart: 10, of which 7 were waited for; matrix products, arithmetic and copies ran while one was open for 0% of the time, Pallas kernels for 4%

profile of v7, /device:TPU:0, one launch (start us, length us, event | category | flops | bytes accessed | tf_op | source)
XLA Modules:
  0.0 20.4 jit_solution(13781812800603999282)
XLA Ops:
  0.0 0.0 copy-start
  0.0 0.0 copy-start.1
  0.0 1.8 %whiten.1 = (f32[64,128]{1,0:T(8,128)S(1)}, s32[8,128]{1,0:T(8,128)S(1)}) custom-call(s32[8]{0:T(128)} %alive_hbm.1, s32[8]{0:T(128)} %limit_hbm.1, f32[2,8,4096]{2,1,0:T(8,128)} %strain_hbm.1, bf16[512,512]{1,0:T(8,128)(2,1)} %constant.8.clone.table_hbm, f32[16,512]{1,0:T(8,128)} %constant.9.clone.twiddle_hbm), custom_call_target="tpu_custom_call" | custom-call | flops 201326592 | bytes 262144 | tf_op jit(solution)/shard_map/whiten/pallas_call | solution.py:130
  1.8 0.5 %collective-permute-start = (f32[64,128]{1,0:T(8,128)S(1)}, f32[64,128]{1,0:T(8,128)S(1)}, u32[]{:S(2)}, u32[]{:S(2)}) collective-permute-start(f32[64,128]{1,0:T(8,128)S(1)} %get-tuple-element.8), channel_id=1, source_target_pairs={{0,1},{1,0},{2,3},{3,2},{4,5},{5,4},{6,7},{7,6},{8,9},{9,8},{10,11... | collective-permute-start | bytes 98312 | tf_op jit(solution)/shard_map/ppermute | solution.py:336
  2.3 0.9 %collective-permute-done = f32[64,128]{1,0:T(8,128)S(1)} collective-permute-done((f32[64,128]{1,0:T(8,128)S(1)}, f32[64,128]{1,0:T(8,128)S(1)}, u32[]{:S(2)}, u32[]{:S(2)}) %collective-permute-start) | collective-permute-done | bytes 32800 | tf_op jit(solution)/shard_map/ppermute | solution.py:336
  3.2 2.8 %collective-permute-start.1 = (f32[128,128]{1,0:T(8,128)S(1)}, f32[128,128]{1,0:T(8,128)S(1)}, u32[]{:S(2)}, u32[]{:S(2)}) collective-permute-start(f32[128,128]{1,0:T(8,128)S(1)} %get-tuple-element.9), channel_id=1, source_target_pairs={{0,2},{1,3},{2,0},{3,1},{4,6},{5,7},{6,4},{7,5},{8,10},{9,11},{10,... | collective-permute-start | bytes 196616 | tf_op jit(solution)/shard_map/ppermute | solution.py:336
  6.0 0.1 collective-permute-start.8
  6.1 0.2 collective-permute-start.7
  6.2 2.2 %collective-permute-done.1 = f32[128,128]{1,0:T(8,128)S(1)} collective-permute-done((f32[128,128]{1,0:T(8,128)S(1)}, f32[128,128]{1,0:T(8,128)S(1)}, u32[]{:S(2)}, u32[]{:S(2)}) %collective-permute-start.1) | collective-permute-done | bytes 65568 | tf_op jit(solution)/shard_map/ppermute | solution.py:336
  8.4 1.8 %collective-permute-start.5 = (f32[256,128]{1,0:T(8,128)S(1)}, f32[256,128]{1,0:T(8,128)S(1)}, u32[]{:S(2)}, u32[]{:S(2)}) collective-permute-start(f32[256,128]{1,0:T(8,128)S(1)} %constant_dynamic-update-slice_fusion.2), channel_id=1, source_target_pairs={{19,0},{23,4},{27,8},{31,12},{3,16},{7,20},{11,24},{15,28},{21,1},... | collective-permute-start | bytes 393224 | tf_op jit(solution)/shard_map/ppermute | solution.py:372
  10.3 0.2 collective-permute-start.3
  10.5 2.2 %collective-permute-done.8 = f32[128,128]{1,0:T(8,128)S(1)} collective-permute-done((f32[128,128]{1,0:T(8,128)S(1)}, f32[128,128]{1,0:T(8,128)S(1)}, u32[]{:S(2)}, u32[]{:S(2)}) %collective-permute-start.8) | collective-permute-done | bytes 65568 | tf_op jit(solution)/shard_map/ppermute | solution.py:363
  12.7 0.1 collective-permute-done.7
  12.8 0.8 %collective-permute-start.9 = (f32[256,128]{1,0:T(8,128)S(1)}, f32[256,128]{1,0:T(8,128)S(1)}, u32[]{:S(2)}, u32[]{:S(2)}) collective-permute-start(f32[256,128]{1,0:T(8,128)S(1)} %pad_maximum_fusion), channel_id=1, source_target_pairs={{0,1},{1,0},{2,3},{3,2},{4,5},{5,4},{6,7},{7,6},{8,9},{9,8},{10,11... | collective-permute-start | bytes 393224 | tf_op jit(solution)/shard_map/ppermute | solution.py:336
  13.6 0.1 collective-permute-start.2
  13.6 2.9 %collective-permute-done.5 = f32[256,128]{1,0:T(8,128)S(1)} collective-permute-done((f32[256,128]{1,0:T(8,128)S(1)}, f32[256,128]{1,0:T(8,128)S(1)}, u32[]{:S(2)}, u32[]{:S(2)}) %collective-permute-start.5) | collective-permute-done | bytes 131104 | tf_op jit(solution)/shard_map/ppermute | solution.py:372
  16.6 0.0 collective-permute-start.6
  16.6 0.0 collective-permute-done.3
  16.6 0.5 %collective-permute-start.4 = (f32[256,128]{1,0:T(8,128)S(1)}, f32[256,128]{1,0:T(8,128)S(1)}, u32[]{:S(2)}, u32[]{:S(2)}) collective-permute-start(f32[256,128]{1,0:T(8,128)S(1)} %collective-permute-done.3), channel_id=1, source_target_pairs={{0,1},{1,0},{2,3},{3,2},{4,5},{5,4},{6,7},{7,6},{8,9},{9,8},{10,11... | collective-permute-start | bytes 393224 | tf_op jit(solution)/shard_map/ppermute | solution.py:336
  17.1 0.0 collective-permute-done.9
  17.1 0.0 copy-done
  17.1 0.0 copy-done.1
  17.1 0.7 %correlate.2.refs_11_ = f32[16,8,400]{2,1,0:T(8,128)S(1)} custom-call(s32[8,128]{1,0:T(8,128)S(1)} %get-tuple-element.7.refs_0_, f32[4,4,2,8,128]{4,3,2,1,0:T(8,128)S(1)} %bitcast.9, f32[2,4,2,8,128]{4,3,2,1,0:T(8,128)S(1)} %bitcast.11, f32[2,4,2,8,128]{4,3,2,1,0:T(8,128)S(1)} %bitcast.15, f32[4,4,2,8,128]{4,3,2,1,0:T(8,128)S(1)} %bitcast.13, ...), custom_call_target="tpu_custom_call" | custom-call | tf_op jit(solution)/shard_map/correlate/pallas_call | solution.py:282
  17.8 0.1 collective-permute-done.2
  18.0 0.0 collective-permute-done.6
  18.0 0.1 collective-permute-done.4
  18.1 2.4 %correlate.3 = f32[64,8,400]{2,1,0:T(8,128)} custom-call(s32[8,128]{1,0:T(8,128)S(1)} %get-tuple-element.7.refs_0_, f32[4,4,2,8,128]{4,3,2,1,0:T(8,128)S(1)} %bitcast.10, f32[4,4,2,8,128]{4,3,2,1,0:T(8,128)S(1)} %bitcast.18, f32[4,4,2,8,128]{4,3,2,1,0:T(8,128)S(1)} %bitcast.17, f32[4,4,2,8,128]{4,3,2,1,0:T(8,128)S(1)} %bitcast.20, ...), custom_call_target="tpu_custom_call" | custom-call | flops 471859200 | bytes 614400 | tf_op jit(solution)/shard_map/correlate/pallas_call | solution.py:282
  (4 shorter events, 0.0 us)
Async XLA Ops:
  0.0 17.1 %copy-start = (bf16[512,400]{1,0:T(8,128)(2,1)S(1)}, bf16[512,400]{1,0:T(8,128)(2,1)}, u32[]{:S(2)}) copy-start(bf16[512,400]{1,0:T(8,128)(2,1)} %constant.11.clone.refs_6_.refs_10_) | copy-start | bytes 1228804
  0.0 17.1 %copy-start.1 = (bf16[512,400]{1,0:T(8,128)(2,1)S(1)}, bf16[512,400]{1,0:T(8,128)(2,1)}, u32[]{:S(2)}) copy-start(bf16[512,400]{1,0:T(8,128)(2,1)} %constant.10.clone.refs_5_.refs_9_) | copy-start | bytes 1228804
  1.8 1.4 %collective-permute-start = (f32[64,128]{1,0:T(8,128)S(1)}, f32[64,128]{1,0:T(8,128)S(1)}, u32[]{:S(2)}, u32[]{:S(2)}) collective-permute-start(f32[64,128]{1,0:T(8,128)S(1)} %get-tuple-element.8), channel_id=1, source_target_pairs={{0,1},{1,0},{2,3},{3,2},{4,5},{5,4},{6,7},{7,6},{8,9},{9,8},{10,11... | collective-permute-start | bytes 98312 | tf_op jit(solution)/shard_map/ppermute | solution.py:336
  3.2 5.3 %collective-permute-start.1 = (f32[128,128]{1,0:T(8,128)S(1)}, f32[128,128]{1,0:T(8,128)S(1)}, u32[]{:S(2)}, u32[]{:S(2)}) collective-permute-start(f32[128,128]{1,0:T(8,128)S(1)} %get-tuple-element.9), channel_id=1, source_target_pairs={{0,2},{1,3},{2,0},{3,1},{4,6},{5,7},{6,4},{7,5},{8,10},{9,11},{10,... | collective-permute-start | bytes 196616 | tf_op jit(solution)/shard_map/ppermute | solution.py:336
  6.0 6.7 %collective-permute-start.8 = (f32[128,128]{1,0:T(8,128)S(1)}, f32[128,128]{1,0:T(8,128)S(1)}, u32[]{:S(2)}, u32[]{:S(2)}) collective-permute-start(f32[128,128]{1,0:T(8,128)S(1)} %get-tuple-element.9), channel_id=1, source_target_pairs={{29,0},{1,4},{5,8},{9,12},{13,16},{17,20},{21,24},{25,28},{31,1},{... | collective-permute-start | bytes 196616 | tf_op jit(solution)/shard_map/ppermute | solution.py:363
  6.1 6.7 %collective-permute-start.7 = (f32[128,128]{1,0:T(8,128)S(1)}, f32[128,128]{1,0:T(8,128)S(1)}, u32[]{:S(2)}, u32[]{:S(2)}) collective-permute-start(f32[128,128]{1,0:T(8,128)S(1)} %get-tuple-element.9), channel_id=1, source_target_pairs={{25,0},{29,4},{1,8},{5,12},{9,16},{13,20},{17,24},{21,28},{27,1},{... | collective-permute-start | bytes 196616 | tf_op jit(solution)/shard_map/ppermute | solution.py:363
  8.4 8.1 %collective-permute-start.5 = (f32[256,128]{1,0:T(8,128)S(1)}, f32[256,128]{1,0:T(8,128)S(1)}, u32[]{:S(2)}, u32[]{:S(2)}) collective-permute-start(f32[256,128]{1,0:T(8,128)S(1)} %constant_dynamic-update-slice_fusion.2), channel_id=1, source_target_pairs={{19,0},{23,4},{27,8},{31,12},{3,16},{7,20},{11,24},{15,28},{21,1},... | collective-permute-start | bytes 393224 | tf_op jit(solution)/shard_map/ppermute | solution.py:372
  10.3 6.3 %collective-permute-start.3 = (f32[256,128]{1,0:T(8,128)S(1)}, f32[256,128]{1,0:T(8,128)S(1)}, u32[]{:S(2)}, u32[]{:S(2)}) collective-permute-start(f32[256,128]{1,0:T(8,128)S(1)} %constant_dynamic-update-slice_fusion.2), channel_id=1, source_target_pairs={{11,0},{15,4},{19,8},{23,12},{27,16},{31,20},{3,24},{7,28},{13,1},... | collective-permute-start | bytes 393224 | tf_op jit(solution)/shard_map/ppermute | solution.py:372
  12.8 4.3 %collective-permute-start.9 = (f32[256,128]{1,0:T(8,128)S(1)}, f32[256,128]{1,0:T(8,128)S(1)}, u32[]{:S(2)}, u32[]{:S(2)}) collective-permute-start(f32[256,128]{1,0:T(8,128)S(1)} %pad_maximum_fusion), channel_id=1, source_target_pairs={{0,1},{1,0},{2,3},{3,2},{4,5},{5,4},{6,7},{7,6},{8,9},{9,8},{10,11... | collective-permute-start | bytes 393224 | tf_op jit(solution)/shard_map/ppermute | solution.py:336
  13.6 4.4 %collective-permute-start.2 = (f32[256,128]{1,0:T(8,128)S(1)}, f32[256,128]{1,0:T(8,128)S(1)}, u32[]{:S(2)}, u32[]{:S(2)}) collective-permute-start(f32[256,128]{1,0:T(8,128)S(1)} %constant_dynamic-update-slice_fusion.2), channel_id=1, source_target_pairs={{5,0},{9,4},{13,8},{17,12},{21,16},{25,20},{29,24},{1,28},{0,1},{4... | collective-permute-start | bytes 393224 | tf_op jit(solution)/shard_map/ppermute | solution.py:367
  16.6 1.4 %collective-permute-start.6 = (f32[256,128]{1,0:T(8,128)S(1)}, f32[256,128]{1,0:T(8,128)S(1)}, u32[]{:S(2)}, u32[]{:S(2)}) collective-permute-start(f32[256,128]{1,0:T(8,128)S(1)} %collective-permute-done.5), channel_id=1, source_target_pairs={{0,1},{1,0},{2,3},{3,2},{4,5},{5,4},{6,7},{7,6},{8,9},{9,8},{10,11... | collective-permute-start | bytes 393224 | tf_op jit(solution)/shard_map/ppermute | solution.py:336
  16.6 1.5 %collective-permute-start.4 = (f32[256,128]{1,0:T(8,128)S(1)}, f32[256,128]{1,0:T(8,128)S(1)}, u32[]{:S(2)}, u32[]{:S(2)}) collective-permute-start(f32[256,128]{1,0:T(8,128)S(1)} %collective-permute-done.3), channel_id=1, source_target_pairs={{0,1},{1,0},{2,3},{3,2},{4,5},{5,4},{6,7},{7,6},{8,9},{9,8},{10,11... | collective-permute-start | bytes 393224 | tf_op jit(solution)/shard_map/ppermute | solution.py:336

commit v8 on v7

--- a/solution.py
+++ b/solution.py
@@ -96,7 +96,8 @@
     for copy in copies[1:]:
         copy.wait()
     high = table_ref[:chunk, :]
-    part = mm(x_high, high) + mm(x_high, table_ref[chunk:, :]) + mm(x_low, high)
+    table = jnp.concatenate([high, table_ref[chunk:, :], high], axis=0)
+    part = mm(jnp.concatenate([x_high, x_high, x_low], axis=1), table)
     real = jnp.zeros((rows, NF), F32)
     imag = jnp.zeros((rows, NF), F32)
     for a in range(pieces):
@@ -246,7 +247,8 @@
                     x_low[first : first + 2 * chans, :] = low
             rows = slice(at * SUB * chans, (at + length) * SUB * chans)
             high, low = x_high[rows, :], x_low[rows, :]
-            result = mm(high, high_ref[...]) + mm(high, low_ref[...]) + mm(low, high_ref[...])
+            table = jnp.concatenate([high_ref[...], low_ref[...], high_ref[...]], axis=0)
+            result = mm(jnp.concatenate([high, high, low], axis=1), table)
             lagged[at * SUB : (at + length) * SUB] = result.reshape(length * SUB, chans, result.shape[1])
             store(at, octet, length).start()
         for copy in early_stores() + [store(*piece) for piece in pieces]:

time: 20.6 us -> 20.6 us (level)
  transfers between devices with their start and end apart: 10 -> 10, of which waited for: 7 -> 7; matrix products, arithmetic and copies ran while one was open for 0% -> 0% of each run, Pallas kernels for 4% -> 3%
where the time goes in v8:
time: 20.6 us; the launch traced here: 20.4 us
  waiting for transfers between devices  8.59 us (42%)
  starting transfers between devices  6.93 us (34%)
  Pallas kernels  4.85 us (24%)
    ppermute x5, starting transfers between devices, exchange(): return lax.ppermute(value, axes, pairs)  4.59 us
    ppermute x5, waiting for transfers between devices, exchange(): return lax.ppermute(value, axes, pairs)  3.17 us
    pallas_call x2, Pallas kernels, correlate(): pl.pallas_call(body, out_shape=jax.ShapeDtypeStruct((size + len(early_oct...  3.06 us
    ppermute x2, waiting for transfers between devices, local(): got = lax.ppermute(block, axes, shift(wanted))  2.94 us
    ppermute x2, waiting for transfers between devices, local(): lax.ppermute(chip, axes, shift({0: (steps, 1), 1: (steps, 3)}))  2.32 us
    ppermute x2, starting transfers between devices, local(): got = lax.ppermute(block, axes, shift(wanted))  2.05 us
    pallas_call x1, Pallas kernels, whiten(): pl.pallas_call(whiten_kernel, out_shape=(jax.ShapeDtypeStruct((TILES * ro...  1.79 us
  transfers between devices with their start and end apart: 10, of which 7 were waited for; matrix products, arithmetic and copies ran while one was open for 0% of the time, Pallas kernels for 3%

profile of v8, /device:TPU:0, one launch (start us, length us, event | category | flops | bytes accessed | tf_op | source)
XLA Modules:
  0.0 20.4 jit_solution(14747839112270071631)
XLA Ops:
  0.0 0.0 copy-start
  0.0 0.0 copy-start.1
  0.0 1.8 %whiten.1 = (f32[64,128]{1,0:T(8,128)S(1)}, s32[8,128]{1,0:T(8,128)S(1)}) custom-call(s32[8]{0:T(128)} %alive_hbm.1, s32[8]{0:T(128)} %limit_hbm.1, f32[2,8,4096]{2,1,0:T(8,128)} %strain_hbm.1, bf16[512,512]{1,0:T(8,128)(2,1)} %constant.8.clone.table_hbm, f32[16,512]{1,0:T(8,128)} %constant.9.clone.twiddle_hbm), custom_call_target="tpu_custom_call" | custom-call | flops 201326592 | bytes 262144 | tf_op jit(solution)/shard_map/whiten/pallas_call | solution.py:131
  1.8 0.5 %collective-permute-start = (f32[64,128]{1,0:T(8,128)S(1)}, f32[64,128]{1,0:T(8,128)S(1)}, u32[]{:S(2)}, u32[]{:S(2)}) collective-permute-start(f32[64,128]{1,0:T(8,128)S(1)} %get-tuple-element.8), channel_id=1, source_target_pairs={{0,1},{1,0},{2,3},{3,2},{4,5},{5,4},{6,7},{7,6},{8,9},{9,8},{10,11... | collective-permute-start | bytes 98312 | tf_op jit(solution)/shard_map/ppermute | solution.py:338
  2.3 0.9 %collective-permute-done = f32[64,128]{1,0:T(8,128)S(1)} collective-permute-done((f32[64,128]{1,0:T(8,128)S(1)}, f32[64,128]{1,0:T(8,128)S(1)}, u32[]{:S(2)}, u32[]{:S(2)}) %collective-permute-start) | collective-permute-done | bytes 32800 | tf_op jit(solution)/shard_map/ppermute | solution.py:338
  3.2 2.8 %collective-permute-start.1 = (f32[128,128]{1,0:T(8,128)S(1)}, f32[128,128]{1,0:T(8,128)S(1)}, u32[]{:S(2)}, u32[]{:S(2)}) collective-permute-start(f32[128,128]{1,0:T(8,128)S(1)} %get-tuple-element.9), channel_id=1, source_target_pairs={{0,2},{1,3},{2,0},{3,1},{4,6},{5,7},{6,4},{7,5},{8,10},{9,11},{10,... | collective-permute-start | bytes 196616 | tf_op jit(solution)/shard_map/ppermute | solution.py:338
  6.0 0.1 collective-permute-start.8
  6.1 0.2 collective-permute-start.7
  6.2 2.2 %collective-permute-done.1 = f32[128,128]{1,0:T(8,128)S(1)} collective-permute-done((f32[128,128]{1,0:T(8,128)S(1)}, f32[128,128]{1,0:T(8,128)S(1)}, u32[]{:S(2)}, u32[]{:S(2)}) %collective-permute-start.1) | collective-permute-done | bytes 65568 | tf_op jit(solution)/shard_map/ppermute | solution.py:338
  8.4 1.8 %collective-permute-start.5 = (f32[256,128]{1,0:T(8,128)S(1)}, f32[256,128]{1,0:T(8,128)S(1)}, u32[]{:S(2)}, u32[]{:S(2)}) collective-permute-start(f32[256,128]{1,0:T(8,128)S(1)} %constant_dynamic-update-slice_fusion.2), channel_id=1, source_target_pairs={{19,0},{23,4},{27,8},{31,12},{3,16},{7,20},{11,24},{15,28},{21,1},... | collective-permute-start | bytes 393224 | tf_op jit(solution)/shard_map/ppermute | solution.py:374
  10.3 0.2 collective-permute-start.3
  10.5 2.2 %collective-permute-done.8 = f32[128,128]{1,0:T(8,128)S(1)} collective-permute-done((f32[128,128]{1,0:T(8,128)S(1)}, f32[128,128]{1,0:T(8,128)S(1)}, u32[]{:S(2)}, u32[]{:S(2)}) %collective-permute-start.8) | collective-permute-done | bytes 65568 | tf_op jit(solution)/shard_map/ppermute | solution.py:365
  12.7 0.1 collective-permute-done.7
  12.8 0.8 %collective-permute-start.9 = (f32[256,128]{1,0:T(8,128)S(1)}, f32[256,128]{1,0:T(8,128)S(1)}, u32[]{:S(2)}, u32[]{:S(2)}) collective-permute-start(f32[256,128]{1,0:T(8,128)S(1)} %pad_maximum_fusion), channel_id=1, source_target_pairs={{0,1},{1,0},{2,3},{3,2},{4,5},{5,4},{6,7},{7,6},{8,9},{9,8},{10,11... | collective-permute-start | bytes 393224 | tf_op jit(solution)/shard_map/ppermute | solution.py:338
  13.6 0.1 collective-permute-start.2
  13.6 2.9 %collective-permute-done.5 = f32[256,128]{1,0:T(8,128)S(1)} collective-permute-done((f32[256,128]{1,0:T(8,128)S(1)}, f32[256,128]{1,0:T(8,128)S(1)}, u32[]{:S(2)}, u32[]{:S(2)}) %collective-permute-start.5) | collective-permute-done | bytes 131104 | tf_op jit(solution)/shard_map/ppermute | solution.py:374
  16.6 0.0 collective-permute-start.6
  16.6 0.0 collective-permute-done.3
  16.6 0.5 %collective-permute-start.4 = (f32[256,128]{1,0:T(8,128)S(1)}, f32[256,128]{1,0:T(8,128)S(1)}, u32[]{:S(2)}, u32[]{:S(2)}) collective-permute-start(f32[256,128]{1,0:T(8,128)S(1)} %collective-permute-done.3), channel_id=1, source_target_pairs={{0,1},{1,0},{2,3},{3,2},{4,5},{5,4},{6,7},{7,6},{8,9},{9,8},{10,11... | collective-permute-start | bytes 393224 | tf_op jit(solution)/shard_map/ppermute | solution.py:338
  17.1 0.0 collective-permute-done.9
  17.1 0.0 copy-done
  17.1 0.0 copy-done.1
  17.1 0.7 %correlate.2.refs_11_ = f32[16,8,400]{2,1,0:T(8,128)S(1)} custom-call(s32[8,128]{1,0:T(8,128)S(1)} %get-tuple-element.7.refs_0_, f32[4,4,2,8,128]{4,3,2,1,0:T(8,128)S(1)} %bitcast.9, f32[2,4,2,8,128]{4,3,2,1,0:T(8,128)S(1)} %bitcast.11, f32[2,4,2,8,128]{4,3,2,1,0:T(8,128)S(1)} %bitcast.15, f32[4,4,2,8,128]{4,3,2,1,0:T(8,128)S(1)} %bitcast.13, ...), custom_call_target="tpu_custom_call" | custom-call | tf_op jit(solution)/shard_map/correlate/pallas_call | solution.py:284
  17.8 0.2 collective-permute-done.2
  18.0 0.0 collective-permute-done.6
  18.0 0.1 collective-permute-done.4
  18.1 2.3 %correlate.3 = f32[64,8,400]{2,1,0:T(8,128)} custom-call(s32[8,128]{1,0:T(8,128)S(1)} %get-tuple-element.7.refs_0_, f32[4,4,2,8,128]{4,3,2,1,0:T(8,128)S(1)} %bitcast.10, f32[4,4,2,8,128]{4,3,2,1,0:T(8,128)S(1)} %bitcast.18, f32[4,4,2,8,128]{4,3,2,1,0:T(8,128)S(1)} %bitcast.17, f32[4,4,2,8,128]{4,3,2,1,0:T(8,128)S(1)} %bitcast.20, ...), custom_call_target="tpu_custom_call" | custom-call | flops 471859200 | bytes 614400 | tf_op jit(solution)/shard_map/correlate/pallas_call | solution.py:284
  (4 shorter events, 0.0 us)
Async XLA Ops:
  0.0 17.1 %copy-start = (bf16[512,400]{1,0:T(8,128)(2,1)S(1)}, bf16[512,400]{1,0:T(8,128)(2,1)}, u32[]{:S(2)}) copy-start(bf16[512,400]{1,0:T(8,128)(2,1)} %constant.11.clone.refs_6_.refs_10_) | copy-start | bytes 1228804
  0.0 17.1 %copy-start.1 = (bf16[512,400]{1,0:T(8,128)(2,1)S(1)}, bf16[512,400]{1,0:T(8,128)(2,1)}, u32[]{:S(2)}) copy-start(bf16[512,400]{1,0:T(8,128)(2,1)} %constant.10.clone.refs_5_.refs_9_) | copy-start | bytes 1228804
  1.8 1.4 %collective-permute-start = (f32[64,128]{1,0:T(8,128)S(1)}, f32[64,128]{1,0:T(8,128)S(1)}, u32[]{:S(2)}, u32[]{:S(2)}) collective-permute-start(f32[64,128]{1,0:T(8,128)S(1)} %get-tuple-element.8), channel_id=1, source_target_pairs={{0,1},{1,0},{2,3},{3,2},{4,5},{5,4},{6,7},{7,6},{8,9},{9,8},{10,11... | collective-permute-start | bytes 98312 | tf_op jit(solution)/shard_map/ppermute | solution.py:338
  3.2 5.3 %collective-permute-start.1 = (f32[128,128]{1,0:T(8,128)S(1)}, f32[128,128]{1,0:T(8,128)S(1)}, u32[]{:S(2)}, u32[]{:S(2)}) collective-permute-start(f32[128,128]{1,0:T(8,128)S(1)} %get-tuple-element.9), channel_id=1, source_target_pairs={{0,2},{1,3},{2,0},{3,1},{4,6},{5,7},{6,4},{7,5},{8,10},{9,11},{10,... | collective-permute-start | bytes 196616 | tf_op jit(solution)/shard_map/ppermute | solution.py:338
  6.0 6.7 %collective-permute-start.8 = (f32[128,128]{1,0:T(8,128)S(1)}, f32[128,128]{1,0:T(8,128)S(1)}, u32[]{:S(2)}, u32[]{:S(2)}) collective-permute-start(f32[128,128]{1,0:T(8,128)S(1)} %get-tuple-element.9), channel_id=1, source_target_pairs={{29,0},{1,4},{5,8},{9,12},{13,16},{17,20},{21,24},{25,28},{31,1},{... | collective-permute-start | bytes 196616 | tf_op jit(solution)/shard_map/ppermute | solution.py:365
  6.1 6.7 %collective-permute-start.7 = (f32[128,128]{1,0:T(8,128)S(1)}, f32[128,128]{1,0:T(8,128)S(1)}, u32[]{:S(2)}, u32[]{:S(2)}) collective-permute-start(f32[128,128]{1,0:T(8,128)S(1)} %get-tuple-element.9), channel_id=1, source_target_pairs={{25,0},{29,4},{1,8},{5,12},{9,16},{13,20},{17,24},{21,28},{27,1},{... | collective-permute-start | bytes 196616 | tf_op jit(solution)/shard_map/ppermute | solution.py:365
  8.4 8.1 %collective-permute-start.5 = (f32[256,128]{1,0:T(8,128)S(1)}, f32[256,128]{1,0:T(8,128)S(1)}, u32[]{:S(2)}, u32[]{:S(2)}) collective-permute-start(f32[256,128]{1,0:T(8,128)S(1)} %constant_dynamic-update-slice_fusion.2), channel_id=1, source_target_pairs={{19,0},{23,4},{27,8},{31,12},{3,16},{7,20},{11,24},{15,28},{21,1},... | collective-permute-start | bytes 393224 | tf_op jit(solution)/shard_map/ppermute | solution.py:374
  10.3 6.3 %collective-permute-start.3 = (f32[256,128]{1,0:T(8,128)S(1)}, f32[256,128]{1,0:T(8,128)S(1)}, u32[]{:S(2)}, u32[]{:S(2)}) collective-permute-start(f32[256,128]{1,0:T(8,128)S(1)} %constant_dynamic-update-slice_fusion.2), channel_id=1, source_target_pairs={{11,0},{15,4},{19,8},{23,12},{27,16},{31,20},{3,24},{7,28},{13,1},... | collective-permute-start | bytes 393224 | tf_op jit(solution)/shard_map/ppermute | solution.py:374
  12.8 4.3 %collective-permute-start.9 = (f32[256,128]{1,0:T(8,128)S(1)}, f32[256,128]{1,0:T(8,128)S(1)}, u32[]{:S(2)}, u32[]{:S(2)}) collective-permute-start(f32[256,128]{1,0:T(8,128)S(1)} %pad_maximum_fusion), channel_id=1, source_target_pairs={{0,1},{1,0},{2,3},{3,2},{4,5},{5,4},{6,7},{7,6},{8,9},{9,8},{10,11... | collective-permute-start | bytes 393224 | tf_op jit(solution)/shard_map/ppermute | solution.py:338
  13.6 4.4 %collective-permute-start.2 = (f32[256,128]{1,0:T(8,128)S(1)}, f32[256,128]{1,0:T(8,128)S(1)}, u32[]{:S(2)}, u32[]{:S(2)}) collective-permute-start(f32[256,128]{1,0:T(8,128)S(1)} %constant_dynamic-update-slice_fusion.2), channel_id=1, source_target_pairs={{5,0},{9,4},{13,8},{17,12},{21,16},{25,20},{29,24},{1,28},{0,1},{4... | collective-permute-start | bytes 393224 | tf_op jit(solution)/shard_map/ppermute | solution.py:369
  16.6 1.4 %collective-permute-start.6 = (f32[256,128]{1,0:T(8,128)S(1)}, f32[256,128]{1,0:T(8,128)S(1)}, u32[]{:S(2)}, u32[]{:S(2)}) collective-permute-start(f32[256,128]{1,0:T(8,128)S(1)} %collective-permute-done.5), channel_id=1, source_target_pairs={{0,1},{1,0},{2,3},{3,2},{4,5},{5,4},{6,7},{7,6},{8,9},{9,8},{10,11... | collective-permute-start | bytes 393224 | tf_op jit(solution)/shard_map/ppermute | solution.py:338
  16.6 1.5 %collective-permute-start.4 = (f32[256,128]{1,0:T(8,128)S(1)}, f32[256,128]{1,0:T(8,128)S(1)}, u32[]{:S(2)}, u32[]{:S(2)}) collective-permute-start(f32[256,128]{1,0:T(8,128)S(1)} %collective-permute-done.3), channel_id=1, source_target_pairs={{0,1},{1,0},{2,3},{3,2},{4,5},{5,4},{6,7},{7,6},{8,9},{9,8},{10,11... | collective-permute-start | bytes 393224 | tf_op jit(solution)/shard_map/ppermute | solution.py:338

commit v9 on v7

--- a/solution.py
+++ b/solution.py
@@ -44,7 +44,7 @@
 
 def inverse_tables(samples, scale):
     freq = np.arange(1, NF + 1, dtype=np.int64)
-    lags = np.arange(-MAXLAG, MAXLAG, dtype=np.int64)
+    lags = np.arange(-MAXLAG, 2 * LANES - MAXLAG, dtype=np.int64)
     angles = phase(freq[:, None] * lags[None, :], samples)
     return split(scale * np.concatenate([np.cos(angles), -np.sin(angles)], axis=0))
 
@@ -226,6 +226,27 @@
             [s[3 * t] - s[3 * t + 2] for t in range(half)] + [s[3 * t] - s[3 * t + 1] for t in range(half)] for s in sums
         ]
 
+    def all_lags(high, low):
+        def product(rows):
+            table_high, table_low = high_ref[rows, :], low_ref[rows, :]
+            x_h, x_l = high[:, rows], low[:, rows]
+            table = jnp.concatenate([table_high, table_low, table_high], axis=0)
+            return mm(jnp.concatenate([x_h, x_h, x_l], axis=1), table)
+
+        even, odd = product(slice(0, NF)), product(slice(NF, 2 * NF))
+        ahead, behind = even + odd, even - odd
+        lane = lax.broadcasted_iota(jnp.int32, (high.shape[0], LANES), 1)
+        tiles = [ahead]
+        for tile in range(2, pl.cdiv(2 * MAXLAG, LANES)):
+            fold = 2 * MAXLAG - tile * LANES
+            source = behind[:, :LANES]
+            index = fold - lane
+            if fold >= LANES:
+                source = jnp.where(lane <= fold - LANES, behind[:, LANES:], source)
+                index = jnp.where(lane <= fold - LANES, index - LANES, index)
+            tiles.append(jnp.take_along_axis(source, jnp.clip(index, 0, LANES - 1), axis=1))
+        return jnp.concatenate(tiles, axis=1)[:, : 2 * MAXLAG]
+
     def work():
         for copy in early_stores():
             copy.start()
@@ -246,7 +267,7 @@
                     x_low[first : first + 2 * chans, :] = low
             rows = slice(at * SUB * chans, (at + length) * SUB * chans)
             high, low = x_high[rows, :], x_low[rows, :]
-            result = mm(high, high_ref[...]) + mm(high, low_ref[...]) + mm(low, high_ref[...])
+            result = all_lags(high, low)
             lagged[at * SUB : (at + length) * SUB] = result.reshape(length * SUB, chans, result.shape[1])
             store(at, octet, length).start()
         for copy in early_stores() + [store(*piece) for piece in pieces]:

time: 20.6 us -> 20.5 us (level)
  no operation moved by 1% of the time
where the time goes in v9:
time: 20.5 us; the launch traced here: 20.4 us
  waiting for transfers between devices  8.58 us (42%)
  starting transfers between devices  6.93 us (34%)
  Pallas kernels  4.78 us (23%)
    ppermute x5, starting transfers between devices, exchange(): return lax.ppermute(value, axes, pairs)  4.59 us
    ppermute x5, waiting for transfers between devices, exchange(): return lax.ppermute(value, axes, pairs)  3.16 us
    pallas_call x2, Pallas kernels, correlate(): pl.pallas_call(body, out_shape=jax.ShapeDtypeStruct((size + len(early_oct...  3.08 us
    ppermute x2, waiting for transfers between devices, local(): got = lax.ppermute(block, axes, shift(wanted))  2.94 us
    ppermute x2, waiting for transfers between devices, local(): lax.ppermute(chip, axes, shift({0: (steps, 1), 1: (steps, 3)}))  2.32 us
    ppermute x2, starting transfers between devices, local(): got = lax.ppermute(block, axes, shift(wanted))  2.05 us
    pallas_call x1, Pallas kernels, whiten(): pl.pallas_call(whiten_kernel, out_shape=(jax.ShapeDtypeStruct((TILES * ro...  1.7 us
  transfers between devices with their start and end apart: 10, of which 7 were waited for; matrix products, arithmetic and copies ran while one was open for 0% of the time, Pallas kernels for 4%

profile of v9, /device:TPU:0, one launch (start us, length us, event | category | flops | bytes accessed | tf_op | source)
XLA Modules:
  0.0 20.4 jit_solution(13223218904825232648)
XLA Ops:
  0.0 1.7 %whiten.1 = (f32[64,128]{1,0:T(8,128)S(1)}, s32[8,128]{1,0:T(8,128)S(1)}) custom-call(s32[8]{0:T(128)} %alive_hbm.1, s32[8]{0:T(128)} %limit_hbm.1, f32[2,8,4096]{2,1,0:T(8,128)} %strain_hbm.1, bf16[512,512]{1,0:T(8,128)(2,1)} %constant.8.clone.table_hbm, f32[16,512]{1,0:T(8,128)} %constant.9.clone.twiddle_hbm), custom_call_target="tpu_custom_call" | custom-call | flops 201326592 | bytes 262144 | tf_op jit(solution)/shard_map/whiten/pallas_call | solution.py:130
  1.7 0.5 %collective-permute-start = (f32[64,128]{1,0:T(8,128)S(1)}, f32[64,128]{1,0:T(8,128)S(1)}, u32[]{:S(2)}, u32[]{:S(2)}) collective-permute-start(f32[64,128]{1,0:T(8,128)S(1)} %get-tuple-element.8), channel_id=1, source_target_pairs={{0,1},{1,0},{2,3},{3,2},{4,5},{5,4},{6,7},{7,6},{8,9},{9,8},{10,11... | collective-permute-start | bytes 98312 | tf_op jit(solution)/shard_map/ppermute | solution.py:357
  2.2 0.0 copy-start.1
  2.2 0.0 copy-start
  2.2 0.8 %collective-permute-done = f32[64,128]{1,0:T(8,128)S(1)} collective-permute-done((f32[64,128]{1,0:T(8,128)S(1)}, f32[64,128]{1,0:T(8,128)S(1)}, u32[]{:S(2)}, u32[]{:S(2)}) %collective-permute-start) | collective-permute-done | bytes 32800 | tf_op jit(solution)/shard_map/ppermute | solution.py:357
  3.1 2.8 %collective-permute-start.1 = (f32[128,128]{1,0:T(8,128)S(1)}, f32[128,128]{1,0:T(8,128)S(1)}, u32[]{:S(2)}, u32[]{:S(2)}) collective-permute-start(f32[128,128]{1,0:T(8,128)S(1)} %get-tuple-element.9), channel_id=1, source_target_pairs={{0,2},{1,3},{2,0},{3,1},{4,6},{5,7},{6,4},{7,5},{8,10},{9,11},{10,... | collective-permute-start | bytes 196616 | tf_op jit(solution)/shard_map/ppermute | solution.py:357
  5.9 0.1 collective-permute-start.8
  6.0 0.2 collective-permute-start.7
  6.2 2.2 %collective-permute-done.1 = f32[128,128]{1,0:T(8,128)S(1)} collective-permute-done((f32[128,128]{1,0:T(8,128)S(1)}, f32[128,128]{1,0:T(8,128)S(1)}, u32[]{:S(2)}, u32[]{:S(2)}) %collective-permute-start.1) | collective-permute-done | bytes 65568 | tf_op jit(solution)/shard_map/ppermute | solution.py:357
  8.4 1.8 %collective-permute-start.5 = (f32[256,128]{1,0:T(8,128)S(1)}, f32[256,128]{1,0:T(8,128)S(1)}, u32[]{:S(2)}, u32[]{:S(2)}) collective-permute-start(f32[256,128]{1,0:T(8,128)S(1)} %constant_dynamic-update-slice_fusion.2), channel_id=1, source_target_pairs={{19,0},{23,4},{27,8},{31,12},{3,16},{7,20},{11,24},{15,28},{21,1},... | collective-permute-start | bytes 393224 | tf_op jit(solution)/shard_map/ppermute | solution.py:393
  10.2 0.2 collective-permute-start.3
  10.4 2.2 %collective-permute-done.8 = f32[128,128]{1,0:T(8,128)S(1)} collective-permute-done((f32[128,128]{1,0:T(8,128)S(1)}, f32[128,128]{1,0:T(8,128)S(1)}, u32[]{:S(2)}, u32[]{:S(2)}) %collective-permute-start.8) | collective-permute-done | bytes 65568 | tf_op jit(solution)/shard_map/ppermute | solution.py:384
  12.6 0.1 collective-permute-done.7
  12.7 0.8 %collective-permute-start.9 = (f32[256,128]{1,0:T(8,128)S(1)}, f32[256,128]{1,0:T(8,128)S(1)}, u32[]{:S(2)}, u32[]{:S(2)}) collective-permute-start(f32[256,128]{1,0:T(8,128)S(1)} %pad_maximum_fusion), channel_id=1, source_target_pairs={{0,1},{1,0},{2,3},{3,2},{4,5},{5,4},{6,7},{7,6},{8,9},{9,8},{10,11... | collective-permute-start | bytes 393224 | tf_op jit(solution)/shard_map/ppermute | solution.py:357
  13.5 0.1 collective-permute-start.2
  13.5 2.9 %collective-permute-done.5 = f32[256,128]{1,0:T(8,128)S(1)} collective-permute-done((f32[256,128]{1,0:T(8,128)S(1)}, f32[256,128]{1,0:T(8,128)S(1)}, u32[]{:S(2)}, u32[]{:S(2)}) %collective-permute-start.5) | collective-permute-done | bytes 131104 | tf_op jit(solution)/shard_map/ppermute | solution.py:393
  16.5 0.0 collective-permute-start.6
  16.5 0.0 collective-permute-done.3
  16.5 0.5 %collective-permute-start.4 = (f32[256,128]{1,0:T(8,128)S(1)}, f32[256,128]{1,0:T(8,128)S(1)}, u32[]{:S(2)}, u32[]{:S(2)}) collective-permute-start(f32[256,128]{1,0:T(8,128)S(1)} %collective-permute-done.3), channel_id=1, source_target_pairs={{0,1},{1,0},{2,3},{3,2},{4,5},{5,4},{6,7},{7,6},{8,9},{9,8},{10,11... | collective-permute-start | bytes 393224 | tf_op jit(solution)/shard_map/ppermute | solution.py:357
  17.0 0.0 collective-permute-done.9
  17.0 0.0 copy-done.1
  17.0 0.0 copy-done
  17.0 0.7 %correlate.2.refs_11_ = f32[16,8,400]{2,1,0:T(8,128)S(1)} custom-call(s32[8,128]{1,0:T(8,128)S(1)} %get-tuple-element.7.refs_0_, f32[4,4,2,8,128]{4,3,2,1,0:T(8,128)S(1)} %bitcast.9, f32[2,4,2,8,128]{4,3,2,1,0:T(8,128)S(1)} %bitcast.11, f32[2,4,2,8,128]{4,3,2,1,0:T(8,128)S(1)} %bitcast.15, f32[4,4,2,8,128]{4,3,2,1,0:T(8,128)S(1)} %bitcast.13, ...), custom_call_target="tpu_custom_call" | custom-call | tf_op jit(solution)/shard_map/correlate/pallas_call | solution.py:303
  17.7 0.2 collective-permute-done.2
  17.9 0.0 collective-permute-done.6
  17.9 0.1 collective-permute-done.4
  18.0 2.4 %correlate.3 = f32[64,8,400]{2,1,0:T(8,128)} custom-call(s32[8,128]{1,0:T(8,128)S(1)} %get-tuple-element.7.refs_0_, f32[4,4,2,8,128]{4,3,2,1,0:T(8,128)S(1)} %bitcast.10, f32[4,4,2,8,128]{4,3,2,1,0:T(8,128)S(1)} %bitcast.18, f32[4,4,2,8,128]{4,3,2,1,0:T(8,128)S(1)} %bitcast.17, f32[4,4,2,8,128]{4,3,2,1,0:T(8,128)S(1)} %bitcast.20, ...), custom_call_target="tpu_custom_call" | custom-call | flops 471859200 | bytes 614400 | tf_op jit(solution)/shard_map/correlate/pallas_call | solution.py:303
  (4 shorter events, 0.0 us)
Async XLA Ops:
  1.7 1.4 %collective-permute-start = (f32[64,128]{1,0:T(8,128)S(1)}, f32[64,128]{1,0:T(8,128)S(1)}, u32[]{:S(2)}, u32[]{:S(2)}) collective-permute-start(f32[64,128]{1,0:T(8,128)S(1)} %get-tuple-element.8), channel_id=1, source_target_pairs={{0,1},{1,0},{2,3},{3,2},{4,5},{5,4},{6,7},{7,6},{8,9},{9,8},{10,11... | collective-permute-start | bytes 98312 | tf_op jit(solution)/shard_map/ppermute | solution.py:357
  2.2 14.8 %copy-start.1 = (bf16[512,256]{1,0:T(8,128)(2,1)S(1)}, bf16[512,256]{1,0:T(8,128)(2,1)}, u32[]{:S(2)}) copy-start(bf16[512,256]{1,0:T(8,128)(2,1)} %constant.10.clone.refs_5_.refs_9_) | copy-start | bytes 786436
  2.2 14.8 %copy-start = (bf16[512,256]{1,0:T(8,128)(2,1)S(1)}, bf16[512,256]{1,0:T(8,128)(2,1)}, u32[]{:S(2)}) copy-start(bf16[512,256]{1,0:T(8,128)(2,1)} %constant.11.clone.refs_6_.refs_10_) | copy-start | bytes 786436
  3.1 5.3 %collective-permute-start.1 = (f32[128,128]{1,0:T(8,128)S(1)}, f32[128,128]{1,0:T(8,128)S(1)}, u32[]{:S(2)}, u32[]{:S(2)}) collective-permute-start(f32[128,128]{1,0:T(8,128)S(1)} %get-tuple-element.9), channel_id=1, source_target_pairs={{0,2},{1,3},{2,0},{3,1},{4,6},{5,7},{6,4},{7,5},{8,10},{9,11},{10,... | collective-permute-start | bytes 196616 | tf_op jit(solution)/shard_map/ppermute | solution.py:357
  5.9 6.7 %collective-permute-start.8 = (f32[128,128]{1,0:T(8,128)S(1)}, f32[128,128]{1,0:T(8,128)S(1)}, u32[]{:S(2)}, u32[]{:S(2)}) collective-permute-start(f32[128,128]{1,0:T(8,128)S(1)} %get-tuple-element.9), channel_id=1, source_target_pairs={{29,0},{1,4},{5,8},{9,12},{13,16},{17,20},{21,24},{25,28},{31,1},{... | collective-permute-start | bytes 196616 | tf_op jit(solution)/shard_map/ppermute | solution.py:384
  6.0 6.7 %collective-permute-start.7 = (f32[128,128]{1,0:T(8,128)S(1)}, f32[128,128]{1,0:T(8,128)S(1)}, u32[]{:S(2)}, u32[]{:S(2)}) collective-permute-start(f32[128,128]{1,0:T(8,128)S(1)} %get-tuple-element.9), channel_id=1, source_target_pairs={{25,0},{29,4},{1,8},{5,12},{9,16},{13,20},{17,24},{21,28},{27,1},{... | collective-permute-start | bytes 196616 | tf_op jit(solution)/shard_map/ppermute | solution.py:384
  8.4 8.1 %collective-permute-start.5 = (f32[256,128]{1,0:T(8,128)S(1)}, f32[256,128]{1,0:T(8,128)S(1)}, u32[]{:S(2)}, u32[]{:S(2)}) collective-permute-start(f32[256,128]{1,0:T(8,128)S(1)} %constant_dynamic-update-slice_fusion.2), channel_id=1, source_target_pairs={{19,0},{23,4},{27,8},{31,12},{3,16},{7,20},{11,24},{15,28},{21,1},... | collective-permute-start | bytes 393224 | tf_op jit(solution)/shard_map/ppermute | solution.py:393
  10.2 6.3 %collective-permute-start.3 = (f32[256,128]{1,0:T(8,128)S(1)}, f32[256,128]{1,0:T(8,128)S(1)}, u32[]{:S(2)}, u32[]{:S(2)}) collective-permute-start(f32[256,128]{1,0:T(8,128)S(1)} %constant_dynamic-update-slice_fusion.2), channel_id=1, source_target_pairs={{11,0},{15,4},{19,8},{23,12},{27,16},{31,20},{3,24},{7,28},{13,1},... | collective-permute-start | bytes 393224 | tf_op jit(solution)/shard_map/ppermute | solution.py:393
  12.7 4.3 %collective-permute-start.9 = (f32[256,128]{1,0:T(8,128)S(1)}, f32[256,128]{1,0:T(8,128)S(1)}, u32[]{:S(2)}, u32[]{:S(2)}) collective-permute-start(f32[256,128]{1,0:T(8,128)S(1)} %pad_maximum_fusion), channel_id=1, source_target_pairs={{0,1},{1,0},{2,3},{3,2},{4,5},{5,4},{6,7},{7,6},{8,9},{9,8},{10,11... | collective-permute-start | bytes 393224 | tf_op jit(solution)/shard_map/ppermute | solution.py:357
  13.5 4.4 %collective-permute-start.2 = (f32[256,128]{1,0:T(8,128)S(1)}, f32[256,128]{1,0:T(8,128)S(1)}, u32[]{:S(2)}, u32[]{:S(2)}) collective-permute-start(f32[256,128]{1,0:T(8,128)S(1)} %constant_dynamic-update-slice_fusion.2), channel_id=1, source_target_pairs={{5,0},{9,4},{13,8},{17,12},{21,16},{25,20},{29,24},{1,28},{0,1},{4... | collective-permute-start | bytes 393224 | tf_op jit(solution)/shard_map/ppermute | solution.py:388
  16.5 1.4 %collective-permute-start.6 = (f32[256,128]{1,0:T(8,128)S(1)}, f32[256,128]{1,0:T(8,128)S(1)}, u32[]{:S(2)}, u32[]{:S(2)}) collective-permute-start(f32[256,128]{1,0:T(8,128)S(1)} %collective-permute-done.5), channel_id=1, source_target_pairs={{0,1},{1,0},{2,3},{3,2},{4,5},{5,4},{6,7},{7,6},{8,9},{9,8},{10,11... | collective-permute-start | bytes 393224 | tf_op jit(solution)/shard_map/ppermute | solution.py:357
  16.5 1.5 %collective-permute-start.4 = (f32[256,128]{1,0:T(8,128)S(1)}, f32[256,128]{1,0:T(8,128)S(1)}, u32[]{:S(2)}, u32[]{:S(2)}) collective-permute-start(f32[256,128]{1,0:T(8,128)S(1)} %collective-permute-done.3), channel_id=1, source_target_pairs={{0,1},{1,0},{2,3},{3,2},{4,5},{5,4},{6,7},{7,6},{8,9},{9,8},{10,11... | collective-permute-start | bytes 393224 | tf_op jit(solution)/shard_map/ppermute | solution.py:357
